TPU v7x, 512 devices: a whole 4x8x8 slice. The times are simulated.
512 devices in a mesh: elem: 64 (over z_hi, y, core), rhs: 8 (over z_lo, x).
Axes of the slice: x: 4, y: 8, z: 8 (z_hi: 4, z_lo: 2; z = z_hi * 2 + z_lo), core: 2. Of those that a mesh axis runs over, the one named last changes fastest.
Arguments:
- blocks: bfloat16 [262144, 448], P('elem'), may hold values from -0.25 to 0.25
- cols: int32 [6, 4096], P(None, 'elem'), may hold values from 0 to 4095, as said below
- inverse: bfloat16 [64, 262144], P(None, 'elem'), may hold values from -0.75 to 0.75
- right_side: float32 [128, 262144], P('rhs', 'elem'), may hold values from -6 to 6
- start: float32 [128, 262144], P('rhs', 'elem'), may hold values from -6 to 6
Outputs:
- adjoint: float32 [128, 262144], P('rhs', 'elem')
- residual: float32 [128, 262144], P('rhs', 'elem')
Inputs may be any that keep to these rules, and one draw needn't show every extreme that they name: Element e lies on device e // 64 along elem; every element named by cols lies on a device at most 2 positions away from the device of the element whose face it is.
All inputs are finite; a program needn't handle non-finite values.
Results may differ from a plain program's by a relative error of at most 0.0036.
Values sent between devices are 32-bit elements; how exact they have to be, the bound alone decides.
No kernel may reach another device: no remote copies, remote signals or barrier semaphores. Data moves between devices by JAX's collectives and lax.ppermute only.
A program may use at most 64 MiB of HBM per device.

v0:
```python
import jax
import jax.numpy as jnp
from jax import lax
from jax.sharding import PartitionSpec as P


def passed_along(value, axis, steps):
    count = lax.axis_size(axis)
    initial, last = (max(0, -steps), min(count, count - steps))
    return lax.ppermute(value, axis, [(source, source + steps) for source in range(initial, last)])


def transposed_apply(vector, blocks, cols):
    width = vector.shape[0]
    count = cols.shape[1]
    dof = blocks.shape[1] // 7
    vb = vector.astype(jnp.bfloat16).reshape(width, count, dof)
    panel = blocks.reshape(count, dof, 7 * dof)
    terms = jnp.einsum("ikm,rik->rim", panel, vb, preferred_element_type=jnp.float32)
    terms = terms.reshape(width, count * 7, dof)
    device = lax.axis_index("elem")
    own_slot = jnp.arange(count, dtype=jnp.int32)[:, None] + 2 * count
    face_slot = cols.T - (device - 2) * count
    target = jnp.concatenate([own_slot, face_slot], 1).reshape(-1)
    route = (target[:, None] == jnp.arange(5 * count, dtype=jnp.int32)[None, :]).astype(jnp.float32)
    window = jnp.einsum("rsm,sw->rwm", terms, route, precision=lax.Precision.HIGHEST)

    def slab(offset):
        return window[:, (offset + 2) * count : (offset + 3) * count]

    total = slab(0)
    total = total + passed_along(slab(1), "elem", 1)
    total = total + passed_along(slab(-1), "elem", -1)
    total = total + passed_along(slab(2), "elem", 2)
    total = total + passed_along(slab(-2), "elem", -2)
    return total.reshape(width, count * dof)


def precondition(res, inverse):
    width = res.shape[0]
    dof = inverse.shape[0]
    count = inverse.shape[1] // dof
    resb = res.astype(jnp.bfloat16).reshape(width, count, dof)
    inv = inverse.reshape(dof, count, dof)
    update = jnp.einsum("jik,rik->rij", inv, resb, preferred_element_type=jnp.float32)
    return update.reshape(width, count * dof)


def body(blocks, cols, inverse, right_side, start):
    res_one = right_side - transposed_apply(start, blocks, cols)
    first = start + precondition(res_one, inverse)
    residual = right_side - transposed_apply(first, blocks, cols)
    adjoint = first + precondition(residual, inverse)
    return (adjoint, residual)


def solution(mesh):
    return jax.shard_map(
        body,
        mesh=mesh,
        in_specs=(
            P("elem", None),
            P(None, "elem"),
            P(None, "elem"),
            P("rhs", "elem"),
            P("rhs", "elem"),
        ),
        out_specs=(P("rhs", "elem"), P("rhs", "elem")),
        check_vma=False,
    )
```

profile of v0, /device:TPU:190, one launch (start us, length us, event | category | flops | bytes accessed | tf_op | source)
XLA Modules:
  0.0 133.1 jit_solution(14538700777504330250)
XLA Ops:
  0.7 6.5 %copy.16 = bf16[4096,448]{1,0:T(8,128)(2,1)} copy(bf16[4096,448]{0,1:T(8,128)(2,1)} %param.5) | data formatting | bytes 7340032 | tf_op args[0]
  7.4 2.9 %convolution_bitcast_fusion.1 = f32[16,64,448]{2,0,1:T(8,128)S(1)} fusion(bf16[64,64,448]{2,1,0:T(8,128)(2,1)} %bitcast.27, bf16[16,64,64]{2,1,0:T(8,128)(2,1)S(1)} %reshape.51), kind=kOutput, calls=%fused_computation.1 | convolution fusion | flops 58720256 | bytes 5636096 | tf_op jit(solution)/shard_map/ikm,rik->rim/dot_general | solution.py:19
  10.2 1.2 copy.18
  11.5 2.3 %reshape.53 = f32[16,448,64]{2,1,0:T(8,128)} reshape(f32[16,64,448]{2,1,0:T(8,128)S(1)} %copy.18) | data formatting | bytes 3670016 | tf_op jit(solution)/shard_map/reshape | solution.py:20
  13.7 3.7 %copy.19 = f32[16,448,64]{1,2,0:T(8,128)} copy(f32[16,448,64]{2,1,0:T(8,128)} %reshape.53) | data formatting | bytes 3670016 | tf_op jit(solution)/shard_map/reshape | solution.py:20
  17.7 3.4 %fusion.3 = f32[320,1024]{0,1:S(1)} fusion(f32[448,1024]{0,1:T(8,128)} %bitcast.33, s32[448]{0:T(512)S(1)} %eq.8), kind=kOutput, calls=%fused_computation.8 | convolution fusion | flops 1761751040 | bytes 3147520
  21.1 1.6 %fusion.19 = (f32[16,64,64]{1,2,0:T(8,128)}, f32[16,64,64]{1,2,0:T(8,128)}, f32[16,64,64]{1,2,0:T(8,128)}, f32[16,64,64]{1,2,0:T(8,128)}) fusion(f32[16,320,64]{1,2,0:T(8,128)S(1)} %bitcast.29), kind=kLoop, calls=%fused_computation.30 | loop fusion | bytes 2097152 | tf_op jit(solution)/shard_map/slice | solution.py:29
  22.7 1.9 %collective-permute-start = (f32[16,64,64]{1,2,0:T(8,128)}, f32[16,64,64]{1,2,0:T(8,128)}, u32[]{:S(2)}, u32[]{:S(2)}) collective-permute-start(f32[16,64,64]{1,2,0:T(8,128)} %get-tuple-element.10), channel_id=1, source_target_pairs={{0,8},{8,16},{16,24},{24,32},{32,40},{40,48},{48,56},{56,64},{64,7... | collective-permute-start | bytes 786440 | tf_op jit(solution)/shard_map/ppermute | solution.py:10
  24.6 3.6 %collective-permute-start.1 = (f32[16,64,64]{1,2,0:T(8,128)}, f32[16,64,64]{1,2,0:T(8,128)}, u32[]{:S(2)}, u32[]{:S(2)}) collective-permute-start(f32[16,64,64]{1,2,0:T(8,128)} %get-tuple-element.13), channel_id=1, source_target_pairs={{8,0},{16,8},{24,16},{32,24},{40,32},{48,40},{56,48},{64,56},{72,6... | collective-permute-start | bytes 786440 | tf_op jit(solution)/shard_map/ppermute | solution.py:10
  28.2 10.7 %collective-permute-start.2 = (f32[16,64,64]{1,2,0:T(8,128)}, f32[16,64,64]{1,2,0:T(8,128)}, u32[]{:S(2)}, u32[]{:S(2)}) collective-permute-start(f32[16,64,64]{1,2,0:T(8,128)} %get-tuple-element.12), channel_id=1, source_target_pairs={{0,16},{8,24},{16,32},{24,40},{32,48},{40,56},{48,64},{56,72},{64,... | collective-permute-start | bytes 786440 | tf_op jit(solution)/shard_map/ppermute | solution.py:10
  39.0 2.1 %collective-permute-start.3 = (f32[16,64,64]{1,2,0:T(8,128)}, f32[16,64,64]{1,2,0:T(8,128)}, u32[]{:S(2)}, u32[]{:S(2)}) collective-permute-start(f32[16,64,64]{1,2,0:T(8,128)} %get-tuple-element.11), channel_id=1, source_target_pairs={{16,0},{24,8},{32,16},{40,24},{48,32},{56,40},{64,48},{72,56},{80,... | collective-permute-start | bytes 786440 | tf_op jit(solution)/shard_map/ppermute | solution.py:10
  42.3 19.2 %collective-permute-done.2 = f32[16,64,64]{1,2,0:T(8,128)} collective-permute-done((f32[16,64,64]{1,2,0:T(8,128)}, f32[16,64,64]{1,2,0:T(8,128)}, u32[]{:S(2)}, u32[]{:S(2)}) %collective-permute-start.2) | collective-permute-done | bytes 262176 | tf_op jit(solution)/shard_map/ppermute | solution.py:10
  61.5 9.3 %collective-permute-done.3 = f32[16,64,64]{1,2,0:T(8,128)} collective-permute-done((f32[16,64,64]{1,2,0:T(8,128)}, f32[16,64,64]{1,2,0:T(8,128)}, u32[]{:S(2)}, u32[]{:S(2)}) %collective-permute-start.3) | collective-permute-done | bytes 262176 | tf_op jit(solution)/shard_map/ppermute | solution.py:10
  70.7 1.7 %fusion.9 = f32[16,64,64]{1,2,0:T(8,128)S(1)} fusion(f32[16,64,64]{1,2,0:T(8,128)} %collective-permute-done.3, f32[16,64,64]{1,2,0:T(8,128)} %collective-permute-done.2, f32[16,64,64]{1,2,0:T(8,128)} %collective-permute-done.1, f32[16,64,64]{1,2,0:T(8,128)} %collective-permute-done, f32[16,320,64]{1,2,0:T(8,128)S(1)} %bitcast.30), kind=kLoop, calls=%fused_computation.16 | loop fusion | flops 262144 | bytes 1572864 | tf_op jit(solution)/shard_map/add | solution.py:35
  74.7 2.9 %convolution_bitcast_fusion = f32[16,64,448]{2,0,1:T(8,128)S(1)} fusion(bf16[64,64,448]{2,1,0:T(8,128)(2,1)} %bitcast.28, bf16[16,64,64]{2,1,0:T(8,128)(2,1)S(1)} %reshape.58), kind=kOutput, calls=%fused_computation | convolution fusion | flops 58720256 | bytes 5636096 | tf_op jit(solution)/shard_map/ikm,rik->rim/dot_general | solution.py:19
  78.8 2.3 %reshape.59 = f32[16,448,64]{2,1,0:T(8,128)} reshape(f32[16,64,448]{2,1,0:T(8,128)S(1)} %copy.25) | data formatting | bytes 3670016 | tf_op jit(solution)/shard_map/reshape | solution.py:20
  81.1 2.7 %copy.26 = f32[16,448,64]{1,2,0:T(8,128)S(1)} copy(f32[16,448,64]{2,1,0:T(8,128)} %reshape.59) | data formatting | bytes 3670016 | tf_op jit(solution)/shard_map/reshape | solution.py:20
  83.8 1.8 %fusion.2 = f32[320,1024]{0,1:S(1)} fusion(f32[448,1024]{0,1:T(8,128)S(1)} %bitcast.34, s32[448]{0:T(512)S(1)} %eq.8), kind=kOutput, calls=%fused_computation.7 | convolution fusion | flops 1761751040 | bytes 3147520
  86.0 1.9 %collective-permute-start.4 = (f32[16,64,64]{1,2,0:T(8,128)S(1)}, f32[16,64,64]{1,2,0:T(8,128)S(1)}, u32[]{:S(2)}, u32[]{:S(2)}) collective-permute-start(f32[16,64,64]{1,2,0:T(8,128)S(1)} %get-tuple-element.6), channel_id=1, source_target_pairs={{0,8},{8,16},{16,24},{24,32},{32,40},{40,48},{48,56},{56,64},{64,7... | collective-permute-start | bytes 786440 | tf_op jit(solution)/shard_map/ppermute | solution.py:10
  87.9 3.6 %collective-permute-start.5 = (f32[16,64,64]{1,2,0:T(8,128)S(1)}, f32[16,64,64]{1,2,0:T(8,128)S(1)}, u32[]{:S(2)}, u32[]{:S(2)}) collective-permute-start(f32[16,64,64]{1,2,0:T(8,128)S(1)} %get-tuple-element.9), channel_id=1, source_target_pairs={{8,0},{16,8},{24,16},{32,24},{40,32},{48,40},{56,48},{64,56},{72,6... | collective-permute-start | bytes 786440 | tf_op jit(solution)/shard_map/ppermute | solution.py:10
  91.6 5.8 %collective-permute-start.6 = (f32[16,64,64]{1,2,0:T(8,128)S(1)}, f32[16,64,64]{1,2,0:T(8,128)S(1)}, u32[]{:S(2)}, u32[]{:S(2)}) collective-permute-start(f32[16,64,64]{1,2,0:T(8,128)S(1)} %get-tuple-element.8), channel_id=1, source_target_pairs={{0,16},{8,24},{16,32},{24,40},{32,48},{40,56},{48,64},{56,72},{64,... | collective-permute-start | bytes 786440 | tf_op jit(solution)/shard_map/ppermute | solution.py:10
  97.4 2.1 %collective-permute-start.7 = (f32[16,64,64]{1,2,0:T(8,128)S(1)}, f32[16,64,64]{1,2,0:T(8,128)S(1)}, u32[]{:S(2)}, u32[]{:S(2)}) collective-permute-start(f32[16,64,64]{1,2,0:T(8,128)S(1)} %get-tuple-element.7), channel_id=1, source_target_pairs={{16,0},{24,8},{32,16},{40,24},{48,32},{56,40},{64,48},{72,56},{80,... | collective-permute-start | bytes 786440 | tf_op jit(solution)/shard_map/ppermute | solution.py:10
  100.2 19.2 %collective-permute-done.6 = f32[16,64,64]{1,2,0:T(8,128)S(1)} collective-permute-done((f32[16,64,64]{1,2,0:T(8,128)S(1)}, f32[16,64,64]{1,2,0:T(8,128)S(1)}, u32[]{:S(2)}, u32[]{:S(2)}) %collective-permute-start.6) | collective-permute-done | bytes 262176 | tf_op jit(solution)/shard_map/ppermute | solution.py:10
  119.5 10.0 %collective-permute-done.7 = f32[16,64,64]{1,2,0:T(8,128)S(1)} collective-permute-done((f32[16,64,64]{1,2,0:T(8,128)S(1)}, f32[16,64,64]{1,2,0:T(8,128)S(1)}, u32[]{:S(2)}, u32[]{:S(2)}) %collective-permute-start.7) | collective-permute-done | bytes 262176 | tf_op jit(solution)/shard_map/ppermute | solution.py:10
  (44 shorter events, 9.9 us)
Async XLA Ops:
  0.6 6.5 %copy-start = (f32[16,4096]{1,0:T(8,128)S(1)}, f32[16,4096]{1,0:T(8,128)}, u32[]{:S(2)}) copy-start(f32[16,4096]{1,0:T(8,128)} %param.9) | copy-start | bytes 786436
  13.7 3.7 %copy-start.5 = (s32[6,64]{1,0:T(8,128)S(1)}, s32[6,64]{1,0:T(8,128)}, u32[]{:S(2)}) copy-start(s32[6,64]{1,0:T(8,128)} %param.6) | copy-start | bytes 4612
  21.1 20.0 %copy-start.4 = (bf16[64,4096]{1,0:T(8,128)(2,1)S(1)}, bf16[64,4096]{1,0:T(8,128)(2,1)}, u32[]{:S(2)}) copy-start(bf16[64,4096]{1,0:T(8,128)(2,1)} %param.7) | copy-start | bytes 1572868
  22.7 19.6 %collective-permute-start = (f32[16,64,64]{1,2,0:T(8,128)}, f32[16,64,64]{1,2,0:T(8,128)}, u32[]{:S(2)}, u32[]{:S(2)}) collective-permute-start(f32[16,64,64]{1,2,0:T(8,128)} %get-tuple-element.10), channel_id=1, source_target_pairs={{0,8},{8,16},{16,24},{24,32},{32,40},{40,48},{48,56},{56,64},{64,7... | collective-permute-start | bytes 786440 | tf_op jit(solution)/shard_map/ppermute | solution.py:10
  24.6 17.7 %collective-permute-start.1 = (f32[16,64,64]{1,2,0:T(8,128)}, f32[16,64,64]{1,2,0:T(8,128)}, u32[]{:S(2)}, u32[]{:S(2)}) collective-permute-start(f32[16,64,64]{1,2,0:T(8,128)} %get-tuple-element.13), channel_id=1, source_target_pairs={{8,0},{16,8},{24,16},{32,24},{40,32},{48,40},{56,48},{64,56},{72,6... | collective-permute-start | bytes 786440 | tf_op jit(solution)/shard_map/ppermute | solution.py:10
  28.2 33.2 %collective-permute-start.2 = (f32[16,64,64]{1,2,0:T(8,128)}, f32[16,64,64]{1,2,0:T(8,128)}, u32[]{:S(2)}, u32[]{:S(2)}) collective-permute-start(f32[16,64,64]{1,2,0:T(8,128)} %get-tuple-element.12), channel_id=1, source_target_pairs={{0,16},{8,24},{16,32},{24,40},{32,48},{40,56},{48,64},{56,72},{64,... | collective-permute-start | bytes 786440 | tf_op jit(solution)/shard_map/ppermute | solution.py:10
  39.0 31.7 %collective-permute-start.3 = (f32[16,64,64]{1,2,0:T(8,128)}, f32[16,64,64]{1,2,0:T(8,128)}, u32[]{:S(2)}, u32[]{:S(2)}) collective-permute-start(f32[16,64,64]{1,2,0:T(8,128)} %get-tuple-element.11), channel_id=1, source_target_pairs={{16,0},{24,8},{32,16},{40,24},{48,32},{56,40},{64,48},{72,56},{80,... | collective-permute-start | bytes 786440 | tf_op jit(solution)/shard_map/ppermute | solution.py:10
  42.2 30.6 %copy-start.2 = (f32[16,4096]{1,0:T(8,128)S(1)}, f32[16,4096]{1,0:T(8,128)}, u32[]{:S(2)}) copy-start(f32[16,4096]{1,0:T(8,128)} %param.8) | copy-start | bytes 786436
  72.8 1.6 %copy-start.1 = (f32[16,4096]{1,0:T(8,128)S(1)}, f32[16,4096]{1,0:T(8,128)}, u32[]{:S(2)}) copy-start(f32[16,4096]{1,0:T(8,128)} %param.9) | copy-start | bytes 786436
  86.0 13.5 %collective-permute-start.4 = (f32[16,64,64]{1,2,0:T(8,128)S(1)}, f32[16,64,64]{1,2,0:T(8,128)S(1)}, u32[]{:S(2)}, u32[]{:S(2)}) collective-permute-start(f32[16,64,64]{1,2,0:T(8,128)S(1)} %get-tuple-element.6), channel_id=1, source_target_pairs={{0,8},{8,16},{16,24},{24,32},{32,40},{40,48},{48,56},{56,64},{64,7... | collective-permute-start | bytes 786440 | tf_op jit(solution)/shard_map/ppermute | solution.py:10
  87.9 12.3 %collective-permute-start.5 = (f32[16,64,64]{1,2,0:T(8,128)S(1)}, f32[16,64,64]{1,2,0:T(8,128)S(1)}, u32[]{:S(2)}, u32[]{:S(2)}) collective-permute-start(f32[16,64,64]{1,2,0:T(8,128)S(1)} %get-tuple-element.9), channel_id=1, source_target_pairs={{8,0},{16,8},{24,16},{32,24},{40,32},{48,40},{56,48},{64,56},{72,6... | collective-permute-start | bytes 786440 | tf_op jit(solution)/shard_map/ppermute | solution.py:10
  91.6 27.9 %collective-permute-start.6 = (f32[16,64,64]{1,2,0:T(8,128)S(1)}, f32[16,64,64]{1,2,0:T(8,128)S(1)}, u32[]{:S(2)}, u32[]{:S(2)}) collective-permute-start(f32[16,64,64]{1,2,0:T(8,128)S(1)} %get-tuple-element.8), channel_id=1, source_target_pairs={{0,16},{8,24},{16,32},{24,40},{32,48},{40,56},{48,64},{56,72},{64,... | collective-permute-start | bytes 786440 | tf_op jit(solution)/shard_map/ppermute | solution.py:10
  97.4 32.7 %copy-start.3 = (f32[16,4096]{1,0:T(8,128)S(1)}, f32[16,4096]{1,0:T(8,128)}, u32[]{:S(2)}) copy-start(f32[16,4096]{1,0:T(8,128)} %param.8) | copy-start | bytes 786436
  97.4 32.0 %collective-permute-start.7 = (f32[16,64,64]{1,2,0:T(8,128)S(1)}, f32[16,64,64]{1,2,0:T(8,128)S(1)}, u32[]{:S(2)}, u32[]{:S(2)}) collective-permute-start(f32[16,64,64]{1,2,0:T(8,128)S(1)} %get-tuple-element.7), channel_id=1, source_target_pairs={{16,0},{24,8},{32,16},{40,24},{48,32},{56,40},{64,48},{72,56},{80,... | collective-permute-start | bytes 786440 | tf_op jit(solution)/shard_map/ppermute | solution.py:10
where the time goes:
time: 134 us; the launch traced here: 133 us
  waiting for transfers between devices  58.4 us (44%)
  starting transfers between devices  31.8 us (24%)
  local copies, waits for them, and re-layouts  25.6 us (19%)
  matrix products  12.9 us (10%)
  other arithmetic  3.46 us (3%)
    ppermute x8, waiting for transfers between devices, passed_along(): lax.ppermute(value, axis, [(source, source + steps) for source in range(i...  58.4 us
    ppermute x8, starting transfers between devices, passed_along(): lax.ppermute(value, axis, [(source, source + steps) for source in range(i...  31.8 us
    reshape x4, local copies, waits for them, and re-layouts, transposed_apply(): terms = terms.reshape(width, count * 7, dof)  10.9 us
    unnamed x13, local copies, waits for them, and re-layouts  6.49 us
    dot_general x2, matrix products, transposed_apply(): jnp.einsum('ikm,rik->rim', panel, vb, preferred_element_type=jnp.float32)  5.72 us
    unnamed x2, matrix products  5.23 us
  transfers between devices with their start and end apart: 8, of which 5 were waited for; matrix products, arithmetic and copies ran while one was open for 1% of the time, Pallas kernels for 0%

commit v1 on v0

v1 whole, which is shorter than its diff:
```python
import functools

import jax
import jax.numpy as jnp
from jax import lax
from jax.experimental import pallas as pl
from jax.experimental.pallas import tpu as pltpu
from jax.sharding import PartitionSpec as P

DOF = 64
SLOTS = 7
QUAD = 4 * DOF
WINDOWS = 2
CHUNKS = 4


def masked_lanes(value, part):
    lane = lax.broadcasted_iota(jnp.int32, value.shape, 1)
    return jnp.where(lane // DOF == part, value, jnp.zeros_like(value))


def products(vb, panel):
    spread = jnp.concatenate([masked_lanes(vb, e) for e in range(4)], 0)
    return lax.dot_general(spread, panel, (((1,), (1,)), ((), ())), preferred_element_type=jnp.float32)


def scatter(vb_ref, panel_of, cols_ref, device, windows, own_ref, stage_ref):
    width = vb_ref.shape[0]
    count = cols_ref.shape[1]
    half = count // 2
    sign = 1 - 2 * lax.rem(device, 2)
    lane = lax.broadcasted_iota(jnp.int32, (width, 2 * DOF), 1) // DOF
    for window in windows:
        window[...] = jnp.zeros_like(window)
    for quad in range(count // 4):
        out = products(vb_ref[:, quad * QUAD : (quad + 1) * QUAD], panel_of(quad))
        stage = stage_ref.at[quad % 2]
        stage[:, : SLOTS * DOF] = out
        for e in range(4):
            element = 4 * quad + e
            rows = slice(e * width, (e + 1) * width)
            for s in range(1, SLOTS):
                tile = stage[rows, (s // 2) * 2 * DOF : (s // 2 + 1) * 2 * DOF]
                target = cols_ref[s - 1, element]
                role = sign * (target // count - device) + 2
                place = role * half + lax.rem(target, count) // 2
                side = lax.rem(target, 2)
                turned = pltpu.roll(tile, (side ^ (s % 2)) * DOF, 1)
                window = windows[s % len(windows)]
                window[place] += jnp.where(lane == side, turned, 0.0)
        for pair in range(2):
            low = stage[2 * pair * width : (2 * pair + 1) * width, : 2 * DOF]
            high = stage[(2 * pair + 1) * width : (2 * pair + 2) * width, : 2 * DOF]
            own_ref[2 * quad + pair] = jnp.where(lane == 0, low, pltpu.roll(high, DOF, 1))


def hand_out(windows, own_ref, far_ref, near_ref, here_ref, mate_ref):
    half = own_ref.shape[0]

    def total(role):
        value = windows[0][role * half : (role + 1) * half]
        for window in windows[1:]:
            value = value + window[role * half : (role + 1) * half]
        return value

    far_ref[...] = total(0)
    near_ref[...] = total(1)
    here_ref[...] = total(2) + own_ref[...]
    mate_ref[:half] = total(3)
    mate_ref[half:] = total(4)


def fetch(panel_hbm, panel_ref, sem):
    span = panel_ref.shape[1] // CHUNKS
    copies = []
    for chunk in range(CHUNKS):
        lanes = pl.ds(chunk * span, span)
        copies.append(pltpu.make_async_copy(panel_hbm.at[:, lanes], panel_ref.at[:, lanes], sem.at[chunk]))
    for copy in copies:
        copy.start()
    return copies


def panels(copies, panel_ref, count):
    per = count // 4 // CHUNKS

    def panel_of(quad):
        if quad % per == 0:
            copies[quad // per].wait()
        return panel_ref[:, quad * QUAD : (quad + 1) * QUAD]

    return panel_of


def first_kernel(cols_ref, place_ref, panel_hbm, start_ref, far_ref, near_ref, here_ref, mate_ref, panel_ref, vb_ref, own_ref, stage_ref, sem, *windows):
    copies = fetch(panel_hbm, panel_ref, sem)
    vb_ref[...] = start_ref[...].astype(jnp.bfloat16)
    panel_of = panels(copies, panel_ref, cols_ref.shape[1])
    scatter(vb_ref, panel_of, cols_ref, place_ref[0], windows, own_ref, stage_ref)
    hand_out(windows, own_ref, far_ref, near_ref, here_ref, mate_ref)


def residual_and_update(quad, right_ref, from_ref, inv_ref, parts):
    lanes = slice(quad * QUAD, (quad + 1) * QUAD)
    sums = []
    for pair in (2 * quad, 2 * quad + 1):
        total = parts[0][pair]
        for part in parts[1:]:
            total = total + part[pair]
        sums.append(total)
    res = right_ref[:, lanes] - jnp.concatenate(sums, 1)
    inv = inv_ref[:, lanes]
    weights = jnp.concatenate([masked_lanes(inv, e) for e in range(4)], 0)
    update = lax.dot_general(res.astype(jnp.bfloat16), weights, (((1,), (1,)), ((), ())), preferred_element_type=jnp.float32)
    return res, from_ref[:, lanes] + update


def second_kernel(cols_ref, place_ref, panel_hbm, right_ref, start_ref, inv_ref, here_in, mate_in, far_in, near_in,
                  first_ref, far_ref, near_ref, here_ref, mate_ref, panel_ref, vb_ref, own_ref, stage_ref, sem, *windows):
    copies = fetch(panel_hbm, panel_ref, sem)
    count = cols_ref.shape[1]
    for quad in range(count // 4):
        _, first = residual_and_update(quad, right_ref, start_ref, inv_ref, (here_in, mate_in, far_in, near_in))
        lanes = slice(quad * QUAD, (quad + 1) * QUAD)
        first_ref[:, lanes] = first
        vb_ref[:, lanes] = first.astype(jnp.bfloat16)
    panel_of = panels(copies, panel_ref, count)
    scatter(vb_ref, panel_of, cols_ref, place_ref[0], windows, own_ref, stage_ref)
    hand_out(windows, own_ref, far_ref, near_ref, here_ref, mate_ref)


def last_kernel(right_ref, first_ref, inv_ref, here_in, mate_in, far_in, near_in, adjoint_ref, residual_ref):
    for quad in range(right_ref.shape[1] // QUAD):
        lanes = slice(quad * QUAD, (quad + 1) * QUAD)
        res, adjoint = residual_and_update(quad, right_ref, first_ref, inv_ref, (here_in, mate_in, far_in, near_in))
        residual_ref[:, lanes] = res
        adjoint_ref[:, lanes] = adjoint


VMEM = pl.BlockSpec(memory_space=pltpu.VMEM)
SMEM = pl.BlockSpec(memory_space=pltpu.SMEM)
ANY = pl.BlockSpec(memory_space=pl.ANY)
PARAMS = pltpu.CompilerParams(vmem_limit_bytes=40 * 1024 * 1024)


def slabs(width, count):
    slab = jax.ShapeDtypeStruct((count // 2, width, 2 * DOF), jnp.float32)
    double = jax.ShapeDtypeStruct((count, width, 2 * DOF), jnp.float32)
    return [slab, slab, slab, double]


def scratch(width, count):
    return [
        pltpu.VMEM((SLOTS * DOF, count * DOF), jnp.bfloat16),
        pltpu.VMEM((width, count * DOF), jnp.bfloat16),
        pltpu.VMEM((count // 2, width, 2 * DOF), jnp.float32),
        pltpu.VMEM((2, 4 * width, 8 * DOF), jnp.float32),
        pltpu.SemaphoreType.DMA((CHUNKS,)),
    ] + [pltpu.VMEM((5 * count // 2, width, 2 * DOF), jnp.float32)] * WINDOWS


def exchange(far, near, mate):
    size = lax.axis_size("elem")
    half = near.shape[0]
    outward = [(i, i + 2) for i in range(1, size - 2, 2)] + [(i, i - 2) for i in range(2, size, 2)]
    across = [(i, i + 1) for i in range(1, size - 1, 2)] + [(i + 1, i) for i in range(1, size - 1, 2)]
    far = lax.ppermute(far, "elem", outward)
    mate = lax.ppermute(mate, "elem", [(i, i ^ 1) for i in range(size)])
    near = lax.ppermute(near + mate[half:], "elem", across)
    return far, near, mate[:half]


def body(blocks, cols, inverse, right_side, start):
    width = start.shape[0]
    count = cols.shape[1]
    panel = blocks.T
    place = lax.axis_index("elem").astype(jnp.int32).reshape(1)
    out = jax.ShapeDtypeStruct(start.shape, jnp.float32)
    far, near, here, mate = pl.pallas_call(
        first_kernel,
        out_shape=slabs(width, count),
        in_specs=[SMEM, SMEM, ANY, VMEM],
        out_specs=[VMEM] * 4,
        scratch_shapes=scratch(width, count),
        compiler_params=PARAMS,
    )(cols, place, panel, start)
    far, near, mate = exchange(far, near, mate)
    first, far, near, here, mate = pl.pallas_call(
        second_kernel,
        out_shape=[out] + slabs(width, count),
        in_specs=[SMEM, SMEM, ANY] + [VMEM] * 7,
        out_specs=[VMEM] * 5,
        scratch_shapes=scratch(width, count),
        compiler_params=PARAMS,
    )(cols, place, panel, right_side, start, inverse, here, mate, far, near)
    far, near, mate = exchange(far, near, mate)
    adjoint, residual = pl.pallas_call(
        last_kernel,
        out_shape=[out, out],
        in_specs=[VMEM] * 7,
        out_specs=[VMEM] * 2,
        compiler_params=PARAMS,
    )(right_side, first, inverse, here, mate, far, near)
    return (adjoint, residual)


def solution(mesh):
    return jax.shard_map(
        body,
        mesh=mesh,
        in_specs=(
            P("elem", None),
            P(None, "elem"),
            P(None, "elem"),
            P("rhs", "elem"),
            P("rhs", "elem"),
        ),
        out_specs=(P("rhs", "elem"), P("rhs", "elem")),
        check_vma=False,
    )
```

time: 134 us -> 65.1 us (0.49)
  the two profiles are of different devices: /device:TPU:190 before, /device:TPU:191 now
where the time goes in v1:
time: 65.1 us; the launch traced here: 64.7 us
  starting transfers between devices  24.5 us (38%)
  waiting for transfers between devices  20.1 us (31%)
  Pallas kernels  15.6 us (24%)
  local copies, waits for them, and re-layouts  3.67 us (6%)
  between operations  0.75 us (1%)
    ppermute x2, waiting for transfers between devices, exchange(): near = lax.ppermute(near + mate[half:], 'elem', across)  18.8 us
    ppermute x2, starting transfers between devices, exchange(): far = lax.ppermute(far, 'elem', outward)  13.4 us
    pallas_call x1, Pallas kernels, body(): pl.pallas_call(second_kernel, out_shape=[out] + slabs(width, count), in_s...  7.38 us
    pallas_call x1, Pallas kernels, body(): pl.pallas_call(first_kernel, out_shape=slabs(width, count), in_specs=[SME...  6.82 us
    ppermute x2, starting transfers between devices, exchange(): near = lax.ppermute(near + mate[half:], 'elem', across)  6.67 us
    ppermute x2, starting transfers between devices, exchange(): mate = lax.ppermute(mate, 'elem', [(i, i ^ 1) for i in range(size)])  4.51 us
    unnamed x10, local copies, waits for them, and re-layouts  3.67 us
    pallas_call x1, Pallas kernels, body(): pl.pallas_call(last_kernel, out_shape=[out, out], in_specs=[VMEM] * 7, ou...  1.38 us
  transfers between devices with their start and end apart: 6, of which 4 were waited for; matrix products, arithmetic and copies ran while one was open for 0% of the time, Pallas kernels for 0%

profile of v1, /device:TPU:191, one launch (start us, length us, event | category | flops | bytes accessed | tf_op | source)
XLA Modules:
  0.0 64.7 jit_solution(2926811605425644219)
XLA Ops:
  0.6 0.0 copy-start
  0.6 2.0 %copy-done = bf16[4096,448]{0,1:T(8,128)(2,1)S(1)} copy-done((bf16[4096,448]{0,1:T(8,128)(2,1)S(1)}, bf16[4096,448]{0,1:T(8,128)(2,1)}, u32[]{:S(2)}) %copy-start) | copy-done | bytes 3670040
  2.7 0.0 copy-start.2
  2.7 0.9 %copy-done.2 = f32[16,4096]{1,0:T(8,128)S(1)} copy-done((f32[16,4096]{1,0:T(8,128)S(1)}, f32[16,4096]{1,0:T(8,128)}, u32[]{:S(2)}) %copy-start.2) | copy-done | bytes 262168
  3.6 0.7 %copy-done.4 = s32[6,64]{1,0:T(8,128)S(1)} copy-done((s32[6,64]{1,0:T(8,128)S(1)}, s32[6,64]{1,0:T(8,128)}, u32[]{:S(2)}) %copy-start.4) | copy-done | bytes 1560
  4.3 6.8 %shard_map.68 = (f32[32,16,128]{2,1,0:T(8,128)S(1)}, f32[32,16,128]{2,1,0:T(8,128)S(1)}, f32[32,16,128]{2,1,0:T(8,128)S(1)}, f32[64,16,128]{2,1,0:T(8,128)S(1)}) custom-call(s32[6,64]{1,0:T(8,128)S(1)} %copy-done.4, s32[1]{0:T(128)} %bitcast.place_ref, bf16[448,4096]{1,0:T(8,128)(2,1)S(1)} %bitcast.2, f32[16,4096]{1,0:T(8,128)S(1)} %copy-done.2), custom_call_target="tpu_custom_call" | custom-call | tf_op jit(solution)/shard_map/pallas_call | solution.py:179
  11.1 2.6 %collective-permute-start = (f32[64,16,128]{2,1,0:T(8,128)S(1)}, f32[64,16,128]{2,1,0:T(8,128)S(1)}, u32[]{:S(2)}, u32[]{:S(2)}) collective-permute-start(f32[64,16,128]{2,1,0:T(8,128)S(1)} %get-tuple-element.12), channel_id=1, source_target_pairs={{0,8},{8,0},{16,24},{24,16},{32,40},{40,32},{48,56},{56,48},{64,72... | collective-permute-start | bytes 1572872 | tf_op jit(solution)/shard_map/ppermute | solution.py:168
  13.7 6.2 %collective-permute-start.1 = (f32[32,16,128]{2,1,0:T(8,128)S(1)}, f32[32,16,128]{2,1,0:T(8,128)S(1)}, u32[]{:S(2)}, u32[]{:S(2)}) collective-permute-start(f32[32,16,128]{2,1,0:T(8,128)S(1)} %get-tuple-element.13), channel_id=1, source_target_pairs={{8,24},{24,40},{40,56},{56,72},{72,88},{88,104},{104,120},{120,136... | collective-permute-start | bytes 786440 | tf_op jit(solution)/shard_map/ppermute | solution.py:167
  20.0 0.0 collective-permute-done
  20.0 0.1 slice_add_fusion.1
  20.0 3.6 %collective-permute-start.2 = (f32[32,16,128]{2,1,0:T(8,128)S(1)}, f32[32,16,128]{2,1,0:T(8,128)S(1)}, u32[]{:S(2)}, u32[]{:S(2)}) collective-permute-start(f32[32,16,128]{2,1,0:T(8,128)S(1)} %get-tuple-element.22), channel_id=1, source_target_pairs={{8,16},{24,32},{40,48},{56,64},{72,80},{88,96},{104,112},{120,128}... | collective-permute-start | bytes 786440 | tf_op jit(solution)/shard_map/ppermute | solution.py:169
  23.7 0.4 collective-permute-done.1.far_in
  24.1 9.2 %collective-permute-done.2.near_in = f32[32,16,128]{2,1,0:T(8,128)S(1)} collective-permute-done((f32[32,16,128]{2,1,0:T(8,128)S(1)}, f32[32,16,128]{2,1,0:T(8,128)S(1)}, u32[]{:S(2)}, u32[]{:S(2)}) %collective-permute-start.2) | collective-permute-done | bytes 262176 | tf_op jit(solution)/shard_map/ppermute | solution.py:169
  33.3 0.0 copy-done.1
  33.3 0.0 copy-done.3
  33.3 7.4 %shard_map.69 = (f32[16,4096]{1,0:T(8,128)S(1)}, f32[32,16,128]{2,1,0:T(8,128)S(1)}, f32[32,16,128]{2,1,0:T(8,128)S(1)}, f32[32,16,128]{2,1,0:T(8,128)S(1)}, f32[64,16,128]{2,1,0:T(8,128)S(1)}) custom-call(s32[6,64]{1,0:T(8,128)S(1)} %copy-done.4, s32[1]{0:T(128)} %bitcast.place_ref, bf16[448,4096]{1,0:T(8,128)(2,1)S(1)} %bitcast.3, ...), custom_call_target="tpu_custom_call" | custom-call | tf_op jit(solution)/shard_map/pallas_call | solution.py:188
  40.7 1.9 %collective-permute-start.3 = (f32[64,16,128]{2,1,0:T(8,128)S(1)}, f32[64,16,128]{2,1,0:T(8,128)S(1)}, u32[]{:S(2)}, u32[]{:S(2)}) collective-permute-start(f32[64,16,128]{2,1,0:T(8,128)S(1)} %get-tuple-element.17), channel_id=1, source_target_pairs={{0,8},{8,0},{16,24},{24,16},{32,40},{40,32},{48,56},{56,48},{64,72... | collective-permute-start | bytes 1572872 | tf_op jit(solution)/shard_map/ppermute | solution.py:168
  42.6 7.1 %collective-permute-start.4 = (f32[32,16,128]{2,1,0:T(8,128)S(1)}, f32[32,16,128]{2,1,0:T(8,128)S(1)}, u32[]{:S(2)}, u32[]{:S(2)}) collective-permute-start(f32[32,16,128]{2,1,0:T(8,128)S(1)} %get-tuple-element.18), channel_id=1, source_target_pairs={{8,24},{24,40},{40,56},{56,72},{72,88},{88,104},{104,120},{120,136... | collective-permute-start | bytes 786440 | tf_op jit(solution)/shard_map/ppermute | solution.py:167
  49.7 0.0 collective-permute-done.3
  49.7 0.1 slice_add_fusion
  49.8 3.0 %collective-permute-start.5 = (f32[32,16,128]{2,1,0:T(8,128)S(1)}, f32[32,16,128]{2,1,0:T(8,128)S(1)}, u32[]{:S(2)}, u32[]{:S(2)}) collective-permute-start(f32[32,16,128]{2,1,0:T(8,128)S(1)} %get-tuple-element.20), channel_id=1, source_target_pairs={{8,16},{24,32},{40,48},{56,64},{72,80},{88,96},{104,112},{120,128}... | collective-permute-start | bytes 786440 | tf_op jit(solution)/shard_map/ppermute | solution.py:169
  52.8 0.9 %collective-permute-done.4.far_in = f32[32,16,128]{2,1,0:T(8,128)S(1)} collective-permute-done((f32[32,16,128]{2,1,0:T(8,128)S(1)}, f32[32,16,128]{2,1,0:T(8,128)S(1)}, u32[]{:S(2)}, u32[]{:S(2)}) %collective-permute-start.4) | collective-permute-done | bytes 262176 | tf_op jit(solution)/shard_map/ppermute | solution.py:167
  53.7 9.6 %collective-permute-done.5.near_in = f32[32,16,128]{2,1,0:T(8,128)S(1)} collective-permute-done((f32[32,16,128]{2,1,0:T(8,128)S(1)}, f32[32,16,128]{2,1,0:T(8,128)S(1)}, u32[]{:S(2)}, u32[]{:S(2)}) %collective-permute-start.5) | collective-permute-done | bytes 262176 | tf_op jit(solution)/shard_map/ppermute | solution.py:169
  63.3 1.4 %shard_map.70 = (f32[16,4096]{1,0:T(8,128)}, f32[16,4096]{1,0:T(8,128)}) custom-call(f32[16,4096]{1,0:T(8,128)S(1)} %copy-done.3, f32[16,4096]{1,0:T(8,128)S(1)} %get-tuple-element.15.first_ref, bf16[64,4096]{1,0:T(8,128)(2,1)S(1)} %copy-done.1, f32[32,16,128]{2,1,0:T(8,128)S(1)} %get-tuple-element.16.here_in, f32[32,16,128]{2,1,0:T(8,128)S(1)} %get-tuple-element.21.mate_in, ...), custom_call_target="tpu_custom_call" | custom-call | tf_op jit(solution)/shard_map/pallas_call | solution.py:197
  (3 shorter events, 0.0 us)
Async XLA Ops:
  0.6 2.0 %copy-start = (bf16[4096,448]{0,1:T(8,128)(2,1)S(1)}, bf16[4096,448]{0,1:T(8,128)(2,1)}, u32[]{:S(2)}) copy-start(bf16[4096,448]{0,1:T(8,128)(2,1)} %param.5) | copy-start | bytes 11010052
  2.7 0.9 %copy-start.2 = (f32[16,4096]{1,0:T(8,128)S(1)}, f32[16,4096]{1,0:T(8,128)}, u32[]{:S(2)}) copy-start(f32[16,4096]{1,0:T(8,128)} %start_ref.3) | copy-start | bytes 786436
  3.6 0.7 %copy-start.4 = (s32[6,64]{1,0:T(8,128)S(1)}, s32[6,64]{1,0:T(8,128)}, u32[]{:S(2)}) copy-start(s32[6,64]{1,0:T(8,128)} %cols_ref.3) | copy-start | bytes 4612
  4.3 29.0 %copy-start.1 = (bf16[64,4096]{1,0:T(8,128)(2,1)S(1)}, bf16[64,4096]{1,0:T(8,128)(2,1)}, u32[]{:S(2)}) copy-start(bf16[64,4096]{1,0:T(8,128)(2,1)} %inv_ref.3) | copy-start | bytes 1572868
  4.3 29.0 %copy-start.3 = (f32[16,4096]{1,0:T(8,128)S(1)}, f32[16,4096]{1,0:T(8,128)}, u32[]{:S(2)}) copy-start(f32[16,4096]{1,0:T(8,128)} %right_ref.3) | copy-start | bytes 786436
  11.1 8.8 %collective-permute-start = (f32[64,16,128]{2,1,0:T(8,128)S(1)}, f32[64,16,128]{2,1,0:T(8,128)S(1)}, u32[]{:S(2)}, u32[]{:S(2)}) collective-permute-start(f32[64,16,128]{2,1,0:T(8,128)S(1)} %get-tuple-element.12), channel_id=1, source_target_pairs={{0,8},{8,0},{16,24},{24,16},{32,40},{40,32},{48,56},{56,48},{64,72... | collective-permute-start | bytes 1572872 | tf_op jit(solution)/shard_map/ppermute | solution.py:168
  13.7 10.4 %collective-permute-start.1 = (f32[32,16,128]{2,1,0:T(8,128)S(1)}, f32[32,16,128]{2,1,0:T(8,128)S(1)}, u32[]{:S(2)}, u32[]{:S(2)}) collective-permute-start(f32[32,16,128]{2,1,0:T(8,128)S(1)} %get-tuple-element.13), channel_id=1, source_target_pairs={{8,24},{24,40},{40,56},{56,72},{72,88},{88,104},{104,120},{120,136... | collective-permute-start | bytes 786440 | tf_op jit(solution)/shard_map/ppermute | solution.py:167
  20.0 13.2 %collective-permute-start.2 = (f32[32,16,128]{2,1,0:T(8,128)S(1)}, f32[32,16,128]{2,1,0:T(8,128)S(1)}, u32[]{:S(2)}, u32[]{:S(2)}) collective-permute-start(f32[32,16,128]{2,1,0:T(8,128)S(1)} %get-tuple-element.22), channel_id=1, source_target_pairs={{8,16},{24,32},{40,48},{56,64},{72,80},{88,96},{104,112},{120,128}... | collective-permute-start | bytes 786440 | tf_op jit(solution)/shard_map/ppermute | solution.py:169
  40.7 9.1 %collective-permute-start.3 = (f32[64,16,128]{2,1,0:T(8,128)S(1)}, f32[64,16,128]{2,1,0:T(8,128)S(1)}, u32[]{:S(2)}, u32[]{:S(2)}) collective-permute-start(f32[64,16,128]{2,1,0:T(8,128)S(1)} %get-tuple-element.17), channel_id=1, source_target_pairs={{0,8},{8,0},{16,24},{24,16},{32,40},{40,32},{48,56},{56,48},{64,72... | collective-permute-start | bytes 1572872 | tf_op jit(solution)/shard_map/ppermute | solution.py:168
  42.6 11.1 %collective-permute-start.4 = (f32[32,16,128]{2,1,0:T(8,128)S(1)}, f32[32,16,128]{2,1,0:T(8,128)S(1)}, u32[]{:S(2)}, u32[]{:S(2)}) collective-permute-start(f32[32,16,128]{2,1,0:T(8,128)S(1)} %get-tuple-element.18), channel_id=1, source_target_pairs={{8,24},{24,40},{40,56},{56,72},{72,88},{88,104},{104,120},{120,136... | collective-permute-start | bytes 786440 | tf_op jit(solution)/shard_map/ppermute | solution.py:167
  49.8 13.5 %collective-permute-start.5 = (f32[32,16,128]{2,1,0:T(8,128)S(1)}, f32[32,16,128]{2,1,0:T(8,128)S(1)}, u32[]{:S(2)}, u32[]{:S(2)}) collective-permute-start(f32[32,16,128]{2,1,0:T(8,128)S(1)} %get-tuple-element.20), channel_id=1, source_target_pairs={{8,16},{24,32},{40,48},{56,64},{72,80},{88,96},{104,112},{120,128}... | collective-permute-start | bytes 786440 | tf_op jit(solution)/shard_map/ppermute | solution.py:169

commit v2 on v1

v2 whole, which is shorter than its diff:
```python
import jax
import jax.numpy as jnp
from jax import lax
from jax.experimental import pallas as pl
from jax.experimental.pallas import tpu as pltpu
from jax.sharding import PartitionSpec as P

DOF = 64
SLOTS = 7
QUAD = 4 * DOF
CHUNKS = 8


def masked_lanes(value, part):
    lane = lax.broadcasted_iota(jnp.int32, value.shape, 1)
    return jnp.where(lane // DOF == part, value, jnp.zeros_like(value))


def products(vb, panel):
    spread = jnp.concatenate([masked_lanes(vb, e) for e in range(4)], 0)
    return lax.dot_general(spread, panel, (((1,), (1,)), ((), ())), preferred_element_type=jnp.float32)


def scatter(vb_ref, panel_of, cols_ref, device, window, own_ref, stage_ref):
    width = vb_ref.shape[0]
    count = cols_ref.shape[1]
    low = lax.broadcasted_iota(jnp.int32, (width, 2 * DOF), 1) < DOF
    base = (device - 2) * count
    for quad in range(count // 4):
        stage = stage_ref.at[quad]
        stage[:, : SLOTS * DOF] = products(vb_ref[:, quad * QUAD : (quad + 1) * QUAD], panel_of(quad))
        for e in range(4):
            rows = slice(e * width, (e + 1) * width)
            for s in range(1, SLOTS):
                tile = stage[rows, (s // 2) * 2 * DOF : (s // 2 + 1) * 2 * DOF]
                place = cols_ref[s - 1, 4 * quad + e] - base
                window[place] += jnp.where(low, tile, 0.0) if s % 2 == 0 else jnp.where(low, 0.0, tile)
        for pair in range(2):
            even = stage[2 * pair * width : (2 * pair + 1) * width, : 2 * DOF]
            odd = stage[(2 * pair + 1) * width : (2 * pair + 2) * width, : 2 * DOF]
            own_ref[2 * quad + pair] = jnp.where(low, even, pltpu.roll(odd, DOF, 1))


def hand_out(device, window, own_ref, far_ref, near_ref, here_ref, mate_ref):
    half, width, lanes = own_ref.shape
    low = lax.broadcasted_iota(jnp.int32, (width, lanes), 1) < DOF
    core = lax.rem(device, 2)

    def slab(role, out, at=0, more=None):
        first = (core * (4 - role) + (1 - core) * role) * 2 * half
        for pair in range(half):
            even = window[first + 2 * pair]
            odd = window[first + 2 * pair + 1]
            total = jnp.where(low, even, odd) + pltpu.roll(jnp.where(low, odd, even), DOF, 1)
            out[at + pair] = total if more is None else total + more[pair]

    slab(0, far_ref)
    slab(3, mate_ref)
    slab(4, mate_ref, half)
    slab(1, near_ref)
    slab(2, here_ref, 0, own_ref)


def fetch(panel_hbm, panel_ref, sem):
    span = panel_ref.shape[1] // CHUNKS
    copies = []
    for chunk in range(CHUNKS):
        lanes = pl.ds(chunk * span, span)
        copies.append(pltpu.make_async_copy(panel_hbm.at[:, lanes], panel_ref.at[:, lanes], sem.at[chunk]))
    for copy in copies:
        copy.start()
    return copies


def panels(copies, panel_ref, count):
    per = count // 4 // CHUNKS

    def panel_of(quad):
        if quad % per == 0:
            copies[quad // per].wait()
        return panel_ref[:, quad * QUAD : (quad + 1) * QUAD]

    return panel_of


def first_kernel(place_ref, cols_hbm, panel_hbm, start_hbm, far_ref, near_ref, here_ref, mate_ref,
                 cols_ref, start_ref, panel_ref, vb_ref, own_ref, stage_ref, window, sem):
    device = place_ref[0]
    small = pltpu.make_async_copy(cols_hbm, cols_ref, sem.at[CHUNKS])
    begin = pltpu.make_async_copy(start_hbm, start_ref, sem.at[CHUNKS + 1])
    begin.start()
    small.start()
    copies = fetch(panel_hbm, panel_ref, sem)
    window[...] = jnp.zeros_like(window)
    begin.wait()
    vb_ref[...] = start_ref[...].astype(jnp.bfloat16)
    small.wait()
    scatter(vb_ref, panels(copies, panel_ref, cols_ref.shape[1]), cols_ref, device, window, own_ref, stage_ref)
    hand_out(device, window, own_ref, far_ref, near_ref, here_ref, mate_ref)


def residual_and_update(quad, right_ref, from_ref, inv_ref, parts):
    lanes = slice(quad * QUAD, (quad + 1) * QUAD)
    sums = []
    for pair in (2 * quad, 2 * quad + 1):
        total = parts[0][pair]
        for part in parts[1:]:
            total = total + part[pair]
        sums.append(total)
    res = right_ref[:, lanes] - jnp.concatenate(sums, 1)
    inv = inv_ref[:, lanes]
    weights = jnp.concatenate([masked_lanes(inv, e) for e in range(4)], 0)
    update = lax.dot_general(res.astype(jnp.bfloat16), weights, (((1,), (1,)), ((), ())), preferred_element_type=jnp.float32)
    return res, from_ref[:, lanes] + update


def second_kernel(place_ref, cols_hbm, panel_hbm, right_ref, start_ref, inv_ref, here_in, mate_in, far_in, near_in,
                  first_ref, far_ref, near_ref, here_ref, mate_ref,
                  cols_ref, panel_ref, vb_ref, own_ref, stage_ref, window, sem):
    device = place_ref[0]
    count = cols_ref.shape[1]
    small = pltpu.make_async_copy(cols_hbm, cols_ref, sem.at[CHUNKS])
    small.start()
    copies = fetch(panel_hbm, panel_ref, sem)
    window[...] = jnp.zeros_like(window)
    for quad in range(count // 4):
        _, first = residual_and_update(quad, right_ref, start_ref, inv_ref, (here_in, mate_in, far_in, near_in))
        lanes = slice(quad * QUAD, (quad + 1) * QUAD)
        first_ref[:, lanes] = first
        vb_ref[:, lanes] = first.astype(jnp.bfloat16)
    small.wait()
    scatter(vb_ref, panels(copies, panel_ref, count), cols_ref, device, window, own_ref, stage_ref)
    hand_out(device, window, own_ref, far_ref, near_ref, here_ref, mate_ref)


def last_kernel(right_ref, first_ref, inv_ref, here_in, mate_in, far_in, near_in, adjoint_ref, residual_ref):
    for quad in range(right_ref.shape[1] // QUAD):
        lanes = slice(quad * QUAD, (quad + 1) * QUAD)
        res, adjoint = residual_and_update(quad, right_ref, first_ref, inv_ref, (here_in, mate_in, far_in, near_in))
        residual_ref[:, lanes] = res
        adjoint_ref[:, lanes] = adjoint


VMEM = pl.BlockSpec(memory_space=pltpu.VMEM)
SMEM = pl.BlockSpec(memory_space=pltpu.SMEM)
HBM = pl.BlockSpec(memory_space=pltpu.HBM)
PARAMS = pltpu.CompilerParams(vmem_limit_bytes=40 * 1024 * 1024)


def slabs(width, count):
    slab = jax.ShapeDtypeStruct((count // 2, width, 2 * DOF), jnp.float32)
    double = jax.ShapeDtypeStruct((count, width, 2 * DOF), jnp.float32)
    return [slab, slab, slab, double]


def scratch(width, count):
    return [
        pltpu.VMEM((SLOTS * DOF, count * DOF), jnp.bfloat16),
        pltpu.VMEM((width, count * DOF), jnp.bfloat16),
        pltpu.VMEM((count // 2, width, 2 * DOF), jnp.float32),
        pltpu.VMEM((count // 4, 4 * width, 8 * DOF), jnp.float32),
        pltpu.VMEM((5 * count, width, 2 * DOF), jnp.float32),
        pltpu.SemaphoreType.DMA((CHUNKS + 2,)),
    ]


def exchange(far, near, mate):
    size = lax.axis_size("elem")
    half = near.shape[0]
    outward = [(i, i + 2) for i in range(1, size - 2, 2)] + [(i, i - 2) for i in range(2, size, 2)]
    across = [(i, i + 1) for i in range(1, size - 1, 2)] + [(i + 1, i) for i in range(1, size - 1, 2)]
    far = lax.ppermute(far, "elem", outward)
    mate = lax.ppermute(mate, "elem", [(i, i ^ 1) for i in range(size)])
    near = lax.ppermute(near + mate[half:], "elem", across)
    return far, near, mate[:half]


def body(blocks, cols, inverse, right_side, start):
    width = start.shape[0]
    count = cols.shape[1]
    panel = blocks.T
    place = lax.axis_index("elem").astype(jnp.int32).reshape(1)
    out = jax.ShapeDtypeStruct(start.shape, jnp.float32)
    far, near, here, mate = pl.pallas_call(
        first_kernel,
        out_shape=slabs(width, count),
        in_specs=[SMEM, HBM, HBM, HBM],
        out_specs=[VMEM] * 4,
        scratch_shapes=[pltpu.SMEM(cols.shape, jnp.int32), pltpu.VMEM(start.shape, jnp.float32)] + scratch(width, count),
        compiler_params=PARAMS,
    )(place, cols, panel, start)
    far, near, mate = exchange(far, near, mate)
    first, far, near, here, mate = pl.pallas_call(
        second_kernel,
        out_shape=[out] + slabs(width, count),
        in_specs=[SMEM, HBM, HBM] + [VMEM] * 7,
        out_specs=[VMEM] * 5,
        scratch_shapes=[pltpu.SMEM(cols.shape, jnp.int32)] + scratch(width, count),
        compiler_params=PARAMS,
    )(place, cols, panel, right_side, start, inverse, here, mate, far, near)
    far, near, mate = exchange(far, near, mate)
    adjoint, residual = pl.pallas_call(
        last_kernel,
        out_shape=[out, out],
        in_specs=[VMEM] * 7,
        out_specs=[VMEM] * 2,
        compiler_params=PARAMS,
    )(right_side, first, inverse, here, mate, far, near)
    return (adjoint, residual)


def solution(mesh):
    return jax.shard_map(
        body,
        mesh=mesh,
        in_specs=(
            P("elem", None),
            P(None, "elem"),
            P(None, "elem"),
            P("rhs", "elem"),
            P("rhs", "elem"),
        ),
        out_specs=(P("rhs", "elem"), P("rhs", "elem")),
        check_vma=False,
    )
```

time: 65.1 us -> 59.5 us (0.914)
  Pallas kernels: 15.6 us -> 10 us
    pallas_call x1, Pallas kernels: 7.38 us -> 4.56 us  [body(): pl.pallas_call(second_kernel, out_shape=[out] + slabs(width, count), in_s...]
    pallas_call x1, Pallas kernels: 6.82 us -> 4.07 us  [body(): pl.pallas_call(first_kernel, out_shape=slabs(width, count), in_specs=[SME...]
where the time goes in v2:
time: 59.5 us; the launch traced here: 59.1 us
  starting transfers between devices  24.3 us (41%)
  waiting for transfers between devices  20.3 us (34%)
  Pallas kernels  10 us (17%)
  local copies, waits for them, and re-layouts  3.67 us (6%)
  between operations  0.74 us (1%)
    ppermute x2, waiting for transfers between devices, exchange(): near = lax.ppermute(near + mate[half:], 'elem', across)  18.8 us
    ppermute x2, starting transfers between devices, exchange(): far = lax.ppermute(far, 'elem', outward)  13.4 us
    ppermute x2, starting transfers between devices, exchange(): near = lax.ppermute(near + mate[half:], 'elem', across)  6.49 us
    pallas_call x1, Pallas kernels, body(): pl.pallas_call(second_kernel, out_shape=[out] + slabs(width, count), in_s...  4.56 us
    ppermute x2, starting transfers between devices, exchange(): mate = lax.ppermute(mate, 'elem', [(i, i ^ 1) for i in range(size)])  4.5 us
    pallas_call x1, Pallas kernels, body(): pl.pallas_call(first_kernel, out_shape=slabs(width, count), in_specs=[SME...  4.07 us
    unnamed x10, local copies, waits for them, and re-layouts  3.67 us
    ppermute x2, waiting for transfers between devices, exchange(): far = lax.ppermute(far, 'elem', outward)  1.49 us
  transfers between devices with their start and end apart: 6, of which 4 were waited for; matrix products, arithmetic and copies ran while one was open for 0% of the time, Pallas kernels for 0%

profile of v2, /device:TPU:191, one launch (start us, length us, event | category | flops | bytes accessed | tf_op | source)
XLA Modules:
  0.0 59.1 jit_solution(3657596740171973945)
XLA Ops:
  0.6 0.0 copy-start
  0.6 2.0 %copy-done = bf16[4096,448]{0,1:T(8,128)(2,1)S(1)} copy-done((bf16[4096,448]{0,1:T(8,128)(2,1)S(1)}, bf16[4096,448]{0,1:T(8,128)(2,1)}, u32[]{:S(2)}) %copy-start) | copy-done | bytes 3670040
  2.7 0.0 copy-start.2
  2.7 0.9 %copy-done.2 = f32[16,4096]{1,0:T(8,128)S(1)} copy-done((f32[16,4096]{1,0:T(8,128)S(1)}, f32[16,4096]{1,0:T(8,128)}, u32[]{:S(2)}) %copy-start.2) | copy-done | bytes 262168
  3.6 0.7 %copy-done.4 = s32[6,64]{1,0:T(8,128)S(1)} copy-done((s32[6,64]{1,0:T(8,128)S(1)}, s32[6,64]{1,0:T(8,128)}, u32[]{:S(2)}) %copy-start.4) | copy-done | bytes 1560
  4.3 4.1 %shard_map.68 = (f32[32,16,128]{2,1,0:T(8,128)S(1)}, f32[32,16,128]{2,1,0:T(8,128)S(1)}, f32[32,16,128]{2,1,0:T(8,128)S(1)}, f32[64,16,128]{2,1,0:T(8,128)S(1)}) custom-call(s32[1]{0:T(128)} %bitcast.place_ref, s32[6,64]{1,0:T(8,128)S(1)} %copy-done.4, bf16[448,4096]{1,0:T(8,128)(2,1)S(1)} %bitcast.2, f32[16,4096]{1,0:T(8,128)S(1)} %copy-done.2), custom_call_target="tpu_custom_call" | custom-call | tf_op jit(solution)/shard_map/pallas_call | solution.py:184
  8.4 2.6 %collective-permute-start = (f32[64,16,128]{2,1,0:T(8,128)S(1)}, f32[64,16,128]{2,1,0:T(8,128)S(1)}, u32[]{:S(2)}, u32[]{:S(2)}) collective-permute-start(f32[64,16,128]{2,1,0:T(8,128)S(1)} %get-tuple-element.12), channel_id=1, source_target_pairs={{0,8},{8,0},{16,24},{24,16},{32,40},{40,32},{48,56},{56,48},{64,72... | collective-permute-start | bytes 1572872 | tf_op jit(solution)/shard_map/ppermute | solution.py:173
  11.0 6.2 %collective-permute-start.1 = (f32[32,16,128]{2,1,0:T(8,128)S(1)}, f32[32,16,128]{2,1,0:T(8,128)S(1)}, u32[]{:S(2)}, u32[]{:S(2)}) collective-permute-start(f32[32,16,128]{2,1,0:T(8,128)S(1)} %get-tuple-element.13), channel_id=1, source_target_pairs={{8,24},{24,40},{40,56},{56,72},{72,88},{88,104},{104,120},{120,136... | collective-permute-start | bytes 786440 | tf_op jit(solution)/shard_map/ppermute | solution.py:172
  17.2 0.0 collective-permute-done
  17.2 0.1 slice_add_fusion.1
  17.3 3.5 %collective-permute-start.2 = (f32[32,16,128]{2,1,0:T(8,128)S(1)}, f32[32,16,128]{2,1,0:T(8,128)S(1)}, u32[]{:S(2)}, u32[]{:S(2)}) collective-permute-start(f32[32,16,128]{2,1,0:T(8,128)S(1)} %get-tuple-element.22), channel_id=1, source_target_pairs={{8,16},{24,32},{40,48},{56,64},{72,80},{88,96},{104,112},{120,128}... | collective-permute-start | bytes 786440 | tf_op jit(solution)/shard_map/ppermute | solution.py:174
  20.7 0.6 %collective-permute-done.1.far_in = f32[32,16,128]{2,1,0:T(8,128)S(1)} collective-permute-done((f32[32,16,128]{2,1,0:T(8,128)S(1)}, f32[32,16,128]{2,1,0:T(8,128)S(1)}, u32[]{:S(2)}, u32[]{:S(2)}) %collective-permute-start.1) | collective-permute-done | bytes 262176 | tf_op jit(solution)/shard_map/ppermute | solution.py:172
  21.3 9.2 %collective-permute-done.2.near_in = f32[32,16,128]{2,1,0:T(8,128)S(1)} collective-permute-done((f32[32,16,128]{2,1,0:T(8,128)S(1)}, f32[32,16,128]{2,1,0:T(8,128)S(1)}, u32[]{:S(2)}, u32[]{:S(2)}) %collective-permute-start.2) | collective-permute-done | bytes 262176 | tf_op jit(solution)/shard_map/ppermute | solution.py:174
  30.5 0.0 copy-done.1
  30.5 0.0 copy-done.3
  30.5 4.6 %shard_map.69 = (f32[16,4096]{1,0:T(8,128)S(1)}, f32[32,16,128]{2,1,0:T(8,128)S(1)}, f32[32,16,128]{2,1,0:T(8,128)S(1)}, f32[32,16,128]{2,1,0:T(8,128)S(1)}, f32[64,16,128]{2,1,0:T(8,128)S(1)}) custom-call(s32[1]{0:T(128)} %bitcast.place_ref, s32[6,64]{1,0:T(8,128)S(1)} %copy-done.4, bf16[448,4096]{1,0:T(8,128)(2,1)S(1)} %bitcast.3, ...), custom_call_target="tpu_custom_call" | custom-call | tf_op jit(solution)/shard_map/pallas_call | solution.py:193
  35.1 1.9 %collective-permute-start.3 = (f32[64,16,128]{2,1,0:T(8,128)S(1)}, f32[64,16,128]{2,1,0:T(8,128)S(1)}, u32[]{:S(2)}, u32[]{:S(2)}) collective-permute-start(f32[64,16,128]{2,1,0:T(8,128)S(1)} %get-tuple-element.17), channel_id=1, source_target_pairs={{0,8},{8,0},{16,24},{24,16},{32,40},{40,32},{48,56},{56,48},{64,72... | collective-permute-start | bytes 1572872 | tf_op jit(solution)/shard_map/ppermute | solution.py:173
  37.0 7.1 %collective-permute-start.4 = (f32[32,16,128]{2,1,0:T(8,128)S(1)}, f32[32,16,128]{2,1,0:T(8,128)S(1)}, u32[]{:S(2)}, u32[]{:S(2)}) collective-permute-start(f32[32,16,128]{2,1,0:T(8,128)S(1)} %get-tuple-element.18), channel_id=1, source_target_pairs={{8,24},{24,40},{40,56},{56,72},{72,88},{88,104},{104,120},{120,136... | collective-permute-start | bytes 786440 | tf_op jit(solution)/shard_map/ppermute | solution.py:172
  44.2 0.0 collective-permute-done.3
  44.2 0.1 slice_add_fusion
  44.2 3.0 %collective-permute-start.5 = (f32[32,16,128]{2,1,0:T(8,128)S(1)}, f32[32,16,128]{2,1,0:T(8,128)S(1)}, u32[]{:S(2)}, u32[]{:S(2)}) collective-permute-start(f32[32,16,128]{2,1,0:T(8,128)S(1)} %get-tuple-element.20), channel_id=1, source_target_pairs={{8,16},{24,32},{40,48},{56,64},{72,80},{88,96},{104,112},{120,128}... | collective-permute-start | bytes 786440 | tf_op jit(solution)/shard_map/ppermute | solution.py:174
  47.3 0.9 %collective-permute-done.4.far_in = f32[32,16,128]{2,1,0:T(8,128)S(1)} collective-permute-done((f32[32,16,128]{2,1,0:T(8,128)S(1)}, f32[32,16,128]{2,1,0:T(8,128)S(1)}, u32[]{:S(2)}, u32[]{:S(2)}) %collective-permute-start.4) | collective-permute-done | bytes 262176 | tf_op jit(solution)/shard_map/ppermute | solution.py:172
  48.2 9.6 %collective-permute-done.5.near_in = f32[32,16,128]{2,1,0:T(8,128)S(1)} collective-permute-done((f32[32,16,128]{2,1,0:T(8,128)S(1)}, f32[32,16,128]{2,1,0:T(8,128)S(1)}, u32[]{:S(2)}, u32[]{:S(2)}) %collective-permute-start.5) | collective-permute-done | bytes 262176 | tf_op jit(solution)/shard_map/ppermute | solution.py:174
  57.8 1.4 %shard_map.70 = (f32[16,4096]{1,0:T(8,128)}, f32[16,4096]{1,0:T(8,128)}) custom-call(f32[16,4096]{1,0:T(8,128)S(1)} %copy-done.3, f32[16,4096]{1,0:T(8,128)S(1)} %get-tuple-element.15.first_ref, bf16[64,4096]{1,0:T(8,128)(2,1)S(1)} %copy-done.1, f32[32,16,128]{2,1,0:T(8,128)S(1)} %get-tuple-element.16.here_in, f32[32,16,128]{2,1,0:T(8,128)S(1)} %get-tuple-element.21.mate_in, ...), custom_call_target="tpu_custom_call" | custom-call | tf_op jit(solution)/shard_map/pallas_call | solution.py:202
  (3 shorter events, 0.0 us)
Async XLA Ops:
  0.6 2.0 %copy-start = (bf16[4096,448]{0,1:T(8,128)(2,1)S(1)}, bf16[4096,448]{0,1:T(8,128)(2,1)}, u32[]{:S(2)}) copy-start(bf16[4096,448]{0,1:T(8,128)(2,1)} %param.5) | copy-start | bytes 11010052
  2.7 0.9 %copy-start.2 = (f32[16,4096]{1,0:T(8,128)S(1)}, f32[16,4096]{1,0:T(8,128)}, u32[]{:S(2)}) copy-start(f32[16,4096]{1,0:T(8,128)} %start_ref.1) | copy-start | bytes 786436
  3.6 0.7 %copy-start.4 = (s32[6,64]{1,0:T(8,128)S(1)}, s32[6,64]{1,0:T(8,128)}, u32[]{:S(2)}) copy-start(s32[6,64]{1,0:T(8,128)} %cols_hbm.3) | copy-start | bytes 4612
  4.3 26.2 %copy-start.1 = (bf16[64,4096]{1,0:T(8,128)(2,1)S(1)}, bf16[64,4096]{1,0:T(8,128)(2,1)}, u32[]{:S(2)}) copy-start(bf16[64,4096]{1,0:T(8,128)(2,1)} %inv_ref.3) | copy-start | bytes 1572868
  4.3 26.2 %copy-start.3 = (f32[16,4096]{1,0:T(8,128)S(1)}, f32[16,4096]{1,0:T(8,128)}, u32[]{:S(2)}) copy-start(f32[16,4096]{1,0:T(8,128)} %right_ref.3) | copy-start | bytes 786436
  8.4 8.8 %collective-permute-start = (f32[64,16,128]{2,1,0:T(8,128)S(1)}, f32[64,16,128]{2,1,0:T(8,128)S(1)}, u32[]{:S(2)}, u32[]{:S(2)}) collective-permute-start(f32[64,16,128]{2,1,0:T(8,128)S(1)} %get-tuple-element.12), channel_id=1, source_target_pairs={{0,8},{8,0},{16,24},{24,16},{32,40},{40,32},{48,56},{56,48},{64,72... | collective-permute-start | bytes 1572872 | tf_op jit(solution)/shard_map/ppermute | solution.py:173
  11.0 10.4 %collective-permute-start.1 = (f32[32,16,128]{2,1,0:T(8,128)S(1)}, f32[32,16,128]{2,1,0:T(8,128)S(1)}, u32[]{:S(2)}, u32[]{:S(2)}) collective-permute-start(f32[32,16,128]{2,1,0:T(8,128)S(1)} %get-tuple-element.13), channel_id=1, source_target_pairs={{8,24},{24,40},{40,56},{56,72},{72,88},{88,104},{104,120},{120,136... | collective-permute-start | bytes 786440 | tf_op jit(solution)/shard_map/ppermute | solution.py:172
  17.3 13.2 %collective-permute-start.2 = (f32[32,16,128]{2,1,0:T(8,128)S(1)}, f32[32,16,128]{2,1,0:T(8,128)S(1)}, u32[]{:S(2)}, u32[]{:S(2)}) collective-permute-start(f32[32,16,128]{2,1,0:T(8,128)S(1)} %get-tuple-element.22), channel_id=1, source_target_pairs={{8,16},{24,32},{40,48},{56,64},{72,80},{88,96},{104,112},{120,128}... | collective-permute-start | bytes 786440 | tf_op jit(solution)/shard_map/ppermute | solution.py:174
  35.1 9.1 %collective-permute-start.3 = (f32[64,16,128]{2,1,0:T(8,128)S(1)}, f32[64,16,128]{2,1,0:T(8,128)S(1)}, u32[]{:S(2)}, u32[]{:S(2)}) collective-permute-start(f32[64,16,128]{2,1,0:T(8,128)S(1)} %get-tuple-element.17), channel_id=1, source_target_pairs={{0,8},{8,0},{16,24},{24,16},{32,40},{40,32},{48,56},{56,48},{64,72... | collective-permute-start | bytes 1572872 | tf_op jit(solution)/shard_map/ppermute | solution.py:173
  37.0 11.1 %collective-permute-start.4 = (f32[32,16,128]{2,1,0:T(8,128)S(1)}, f32[32,16,128]{2,1,0:T(8,128)S(1)}, u32[]{:S(2)}, u32[]{:S(2)}) collective-permute-start(f32[32,16,128]{2,1,0:T(8,128)S(1)} %get-tuple-element.18), channel_id=1, source_target_pairs={{8,24},{24,40},{40,56},{56,72},{72,88},{88,104},{104,120},{120,136... | collective-permute-start | bytes 786440 | tf_op jit(solution)/shard_map/ppermute | solution.py:172
  44.2 13.5 %collective-permute-start.5 = (f32[32,16,128]{2,1,0:T(8,128)S(1)}, f32[32,16,128]{2,1,0:T(8,128)S(1)}, u32[]{:S(2)}, u32[]{:S(2)}) collective-permute-start(f32[32,16,128]{2,1,0:T(8,128)S(1)} %get-tuple-element.20), channel_id=1, source_target_pairs={{8,16},{24,32},{40,48},{56,64},{72,80},{88,96},{104,112},{120,128}... | collective-permute-start | bytes 786440 | tf_op jit(solution)/shard_map/ppermute | solution.py:174

commit v3 on v2

--- a/solution.py
+++ b/solution.py
@@ -41,24 +41,27 @@
             own_ref[2 * quad + pair] = jnp.where(low, even, pltpu.roll(odd, DOF, 1))
 
 
-def hand_out(device, window, own_ref, far_ref, near_ref, here_ref, mate_ref):
-    half, width, lanes = own_ref.shape
-    low = lax.broadcasted_iota(jnp.int32, (width, lanes), 1) < DOF
+def hand_out(device, window, role, out, at=0, more=None):
+    half = window.shape[0] // 10
+    low = lax.broadcasted_iota(jnp.int32, window.shape[1:], 1) < DOF
     core = lax.rem(device, 2)
-
-    def slab(role, out, at=0, more=None):
-        first = (core * (4 - role) + (1 - core) * role) * 2 * half
-        for pair in range(half):
-            even = window[first + 2 * pair]
-            odd = window[first + 2 * pair + 1]
-            total = jnp.where(low, even, odd) + pltpu.roll(jnp.where(low, odd, even), DOF, 1)
-            out[at + pair] = total if more is None else total + more[pair]
-
-    slab(0, far_ref)
-    slab(3, mate_ref)
-    slab(4, mate_ref, half)
-    slab(1, near_ref)
-    slab(2, here_ref, 0, own_ref)
+    first = (core * (4 - role) + (1 - core) * role) * 2 * half
+    for pair in range(half):
+        even = window[first + 2 * pair]
+        odd = window[first + 2 * pair + 1]
+        total = jnp.where(low, even, odd) + pltpu.roll(jnp.where(low, odd, even), DOF, 1)
+        out[at + pair] = total if more is None else total + more[pair]
+
+
+def mate_kernel(place_ref, window, mate_ref):
+    half = mate_ref.shape[0] // 2
+    hand_out(place_ref[0], window, 3, mate_ref)
+    hand_out(place_ref[0], window, 4, mate_ref, half)
+
+
+def rest_kernel(place_ref, window, own_ref, near_ref, here_ref):
+    hand_out(place_ref[0], window, 1, near_ref)
+    hand_out(place_ref[0], window, 2, here_ref, 0, own_ref)
 
 
 def fetch(panel_hbm, panel_ref, sem):
@@ -76,15 +79,15 @@
     per = count // 4 // CHUNKS
 
     def panel_of(quad):
-        if quad % per == 0:
+        if copies and quad % per == 0:
             copies[quad // per].wait()
         return panel_ref[:, quad * QUAD : (quad + 1) * QUAD]
 
     return panel_of
 
 
-def first_kernel(place_ref, cols_hbm, panel_hbm, start_hbm, far_ref, near_ref, here_ref, mate_ref,
-                 cols_ref, start_ref, panel_ref, vb_ref, own_ref, stage_ref, window, sem):
+def first_kernel(place_ref, cols_hbm, panel_hbm, start_hbm, far_ref, window, own_ref, panel_ref,
+                 cols_ref, start_ref, vb_ref, stage_ref, sem):
     device = place_ref[0]
     small = pltpu.make_async_copy(cols_hbm, cols_ref, sem.at[CHUNKS])
     begin = pltpu.make_async_copy(start_hbm, start_ref, sem.at[CHUNKS + 1])
@@ -96,7 +99,7 @@
     vb_ref[...] = start_ref[...].astype(jnp.bfloat16)
     small.wait()
     scatter(vb_ref, panels(copies, panel_ref, cols_ref.shape[1]), cols_ref, device, window, own_ref, stage_ref)
-    hand_out(device, window, own_ref, far_ref, near_ref, here_ref, mate_ref)
+    hand_out(device, window, 0, far_ref)
 
 
 def residual_and_update(quad, right_ref, from_ref, inv_ref, parts):
@@ -114,14 +117,12 @@
     return res, from_ref[:, lanes] + update
 
 
-def second_kernel(place_ref, cols_hbm, panel_hbm, right_ref, start_ref, inv_ref, here_in, mate_in, far_in, near_in,
-                  first_ref, far_ref, near_ref, here_ref, mate_ref,
-                  cols_ref, panel_ref, vb_ref, own_ref, stage_ref, window, sem):
+def second_kernel(place_ref, cols_hbm, panel_ref, right_ref, start_ref, inv_ref, here_in, mate_in, far_in, near_in,
+                  first_ref, far_ref, window, own_ref, cols_ref, vb_ref, stage_ref, sem):
     device = place_ref[0]
     count = cols_ref.shape[1]
     small = pltpu.make_async_copy(cols_hbm, cols_ref, sem.at[CHUNKS])
     small.start()
-    copies = fetch(panel_hbm, panel_ref, sem)
     window[...] = jnp.zeros_like(window)
     for quad in range(count // 4):
         _, first = residual_and_update(quad, right_ref, start_ref, inv_ref, (here_in, mate_in, far_in, near_in))
@@ -129,8 +130,8 @@
         first_ref[:, lanes] = first
         vb_ref[:, lanes] = first.astype(jnp.bfloat16)
     small.wait()
-    scatter(vb_ref, panels(copies, panel_ref, count), cols_ref, device, window, own_ref, stage_ref)
-    hand_out(device, window, own_ref, far_ref, near_ref, here_ref, mate_ref)
+    scatter(vb_ref, panels((), panel_ref, count), cols_ref, device, window, own_ref, stage_ref)
+    hand_out(device, window, 0, far_ref)
 
 
 def last_kernel(right_ref, first_ref, inv_ref, here_in, mate_in, far_in, near_in, adjoint_ref, residual_ref):
@@ -147,65 +148,84 @@
 PARAMS = pltpu.CompilerParams(vmem_limit_bytes=40 * 1024 * 1024)
 
 
-def slabs(width, count):
+def applied(width, count):
     slab = jax.ShapeDtypeStruct((count // 2, width, 2 * DOF), jnp.float32)
-    double = jax.ShapeDtypeStruct((count, width, 2 * DOF), jnp.float32)
-    return [slab, slab, slab, double]
+    window = jax.ShapeDtypeStruct((5 * count, width, 2 * DOF), jnp.float32)
+    return [slab, window, slab]
 
 
 def scratch(width, count):
     return [
-        pltpu.VMEM((SLOTS * DOF, count * DOF), jnp.bfloat16),
         pltpu.VMEM((width, count * DOF), jnp.bfloat16),
-        pltpu.VMEM((count // 2, width, 2 * DOF), jnp.float32),
         pltpu.VMEM((count // 4, 4 * width, 8 * DOF), jnp.float32),
-        pltpu.VMEM((5 * count, width, 2 * DOF), jnp.float32),
         pltpu.SemaphoreType.DMA((CHUNKS + 2,)),
     ]
 
 
-def exchange(far, near, mate):
+def in_hbm(value):
+    return pltpu.with_memory_space_constraint(value, pltpu.HBM)
+
+
+def exchange(place, far, window, own):
     size = lax.axis_size("elem")
-    half = near.shape[0]
+    half, width, lanes = own.shape
+    slab = jax.ShapeDtypeStruct(own.shape, jnp.float32)
+    double = jax.ShapeDtypeStruct((2 * half, width, lanes), jnp.float32)
     outward = [(i, i + 2) for i in range(1, size - 2, 2)] + [(i, i - 2) for i in range(2, size, 2)]
     across = [(i, i + 1) for i in range(1, size - 1, 2)] + [(i + 1, i) for i in range(1, size - 1, 2)]
     far = lax.ppermute(far, "elem", outward)
+    mate = pl.pallas_call(
+        mate_kernel,
+        out_shape=double,
+        in_specs=[SMEM, VMEM],
+        out_specs=VMEM,
+        compiler_params=PARAMS,
+        cost_estimate=pl.CostEstimate(flops=10**8, bytes_accessed=4 * 10**6, transcendentals=0),
+    )(place, window)
     mate = lax.ppermute(mate, "elem", [(i, i ^ 1) for i in range(size)])
+    near, here = pl.pallas_call(
+        rest_kernel,
+        out_shape=[slab, slab],
+        in_specs=[SMEM, VMEM, VMEM],
+        out_specs=[VMEM, VMEM],
+        compiler_params=PARAMS,
+        cost_estimate=pl.CostEstimate(flops=10**10, bytes_accessed=4 * 10**6, transcendentals=0),
+    )(place, window, own)
     near = lax.ppermute(near + mate[half:], "elem", across)
-    return far, near, mate[:half]
+    return here, mate[:half], far, near
 
 
 def body(blocks, cols, inverse, right_side, start):
     width = start.shape[0]
     count = cols.shape[1]
-    panel = blocks.T
     place = lax.axis_index("elem").astype(jnp.int32).reshape(1)
     out = jax.ShapeDtypeStruct(start.shape, jnp.float32)
-    far, near, here, mate = pl.pallas_call(
+    cols = in_hbm(cols)
+    far, window, own, panel = pl.pallas_call(
         first_kernel,
-        out_shape=slabs(width, count),
+        out_shape=applied(width, count) + [pltpu.VMEM(blocks.shape[::-1], jnp.bfloat16)],
         in_specs=[SMEM, HBM, HBM, HBM],
         out_specs=[VMEM] * 4,
         scratch_shapes=[pltpu.SMEM(cols.shape, jnp.int32), pltpu.VMEM(start.shape, jnp.float32)] + scratch(width, count),
         compiler_params=PARAMS,
-    )(place, cols, panel, start)
-    far, near, mate = exchange(far, near, mate)
-    first, far, near, here, mate = pl.pallas_call(
+    )(place, cols, in_hbm(blocks.T), in_hbm(start))
+    parts = exchange(place, far, window, own)
+    first, far, window, own = pl.pallas_call(
         second_kernel,
-        out_shape=[out] + slabs(width, count),
-        in_specs=[SMEM, HBM, HBM] + [VMEM] * 7,
-        out_specs=[VMEM] * 5,
+        out_shape=[out] + applied(width, count),
+        in_specs=[SMEM, HBM] + [VMEM] * 8,
+        out_specs=[VMEM] * 4,
         scratch_shapes=[pltpu.SMEM(cols.shape, jnp.int32)] + scratch(width, count),
         compiler_params=PARAMS,
-    )(place, cols, panel, right_side, start, inverse, here, mate, far, near)
-    far, near, mate = exchange(far, near, mate)
+    )(place, cols, panel, right_side, start, inverse, *parts)
+    parts = exchange(place, far, window, own)
     adjoint, residual = pl.pallas_call(
         last_kernel,
         out_shape=[out, out],
         in_specs=[VMEM] * 7,
         out_specs=[VMEM] * 2,
         compiler_params=PARAMS,
-    )(right_side, first, inverse, here, mate, far, near)
+    )(right_side, first, inverse, *parts)
     return (adjoint, residual)
 
 

time: 59.5 us -> 54.1 us (0.909)
  the two profiles are of different devices: /device:TPU:191 before, /device:TPU:251 now
where the time goes in v3:
time: 54.1 us; the launch traced here: 53.8 us
  waiting for transfers between devices  21.7 us (40%)
  starting transfers between devices  21.2 us (39%)
  Pallas kernels  10 us (18%)
  between operations  0.78 us (1%)
    ppermute x2, waiting for transfers between devices, exchange(): near = lax.ppermute(near + mate[half:], 'elem', across)  18.4 us
    ppermute x2, starting transfers between devices, exchange(): near = lax.ppermute(near + mate[half:], 'elem', across)  10.1 us
    ppermute x2, starting transfers between devices, exchange(): far = lax.ppermute(far, 'elem', outward)  7.24 us
    pallas_call x1, Pallas kernels, body(): pl.pallas_call(first_kernel, out_shape=applied(width, count) + [pltpu.VME...  4.5 us
    ppermute x2, starting transfers between devices, exchange(): mate = lax.ppermute(mate, 'elem', [(i, i ^ 1) for i in range(size)])  3.84 us
    pallas_call x1, Pallas kernels, body(): pl.pallas_call(second_kernel, out_shape=[out] + applied(width, count), in...  3.28 us
    ppermute x2, waiting for transfers between devices, exchange(): mate = lax.ppermute(mate, 'elem', [(i, i ^ 1) for i in range(size)])  3.27 us
    pallas_call x1, Pallas kernels, body(): pl.pallas_call(last_kernel, out_shape=[out, out], in_specs=[VMEM] * 7, ou...  1.38 us
  transfers between devices with their start and end apart: 6, of which 4 were waited for; matrix products, arithmetic and copies ran while one was open for 0% of the time, Pallas kernels for 2%

profile of v3, /device:TPU:251, one launch (start us, length us, event | category | flops | bytes accessed | tf_op | source)
XLA Modules:
  0.0 53.8 jit_solution(1449390142926974649)
XLA Ops:
  0.6 4.5 %shard_map.68 = (f32[32,16,128]{2,1,0:T(8,128)S(1)}, f32[320,16,128]{2,1,0:T(8,128)S(1)}, f32[32,16,128]{2,1,0:T(8,128)S(1)}, bf16[448,4096]{1,0:T(8,128)(2,1)S(1)}) custom-call(s32[1]{0:T(128)} %bitcast.place_ref, s32[6,64]{1,0:T(8,128)} %cols_hbm.3, bf16[448,4096]{1,0:T(8,128)(2,1)} %bitcast.2, f32[16,4096]{1,0:T(8,128)} %start_ref.1), custom_call_target="tpu_custom_call" | custom-call | tf_op jit(solution)/shard_map/pallas_call | solution.py:204
  5.1 5.3 %collective-permute-start.1 = (f32[32,16,128]{2,1,0:T(8,128)S(1)}, f32[32,16,128]{2,1,0:T(8,128)S(1)}, u32[]{:S(2)}, u32[]{:S(2)}) collective-permute-start(f32[32,16,128]{2,1,0:T(8,128)S(1)} %get-tuple-element.18), channel_id=1, source_target_pairs={{8,24},{24,40},{40,56},{56,72},{72,88},{88,104},{104,120},{120,136... | collective-permute-start | bytes 786440 | tf_op jit(solution)/shard_map/ppermute | solution.py:176
  10.5 0.2 shard_map.70
  10.7 1.9 %collective-permute-start = (f32[64,16,128]{2,1,0:T(8,128)S(1)}, f32[64,16,128]{2,1,0:T(8,128)S(1)}, u32[]{:S(2)}, u32[]{:S(2)}) collective-permute-start(f32[64,16,128]{2,1,0:T(8,128)S(1)} %shard_map.70), channel_id=1, source_target_pairs={{0,8},{8,0},{16,24},{24,16},{32,40},{40,32},{48,56},{56,48},{64,72... | collective-permute-start | bytes 1572872 | tf_op jit(solution)/shard_map/ppermute | solution.py:185
  12.6 0.0 copy-start
  12.6 0.0 copy-start.1
  12.7 0.0 copy-start.2
  12.7 0.2 shard_map.69
  12.9 1.6 %collective-permute-done = f32[64,16,128]{2,1,0:T(8,128)S(1)} collective-permute-done((f32[64,16,128]{2,1,0:T(8,128)S(1)}, f32[64,16,128]{2,1,0:T(8,128)S(1)}, u32[]{:S(2)}, u32[]{:S(2)}) %collective-permute-start) | collective-permute-done | bytes 524320 | tf_op jit(solution)/shard_map/ppermute | solution.py:185
  14.5 0.1 slice_add_fusion.1
  14.6 5.0 %collective-permute-start.2 = (f32[32,16,128]{2,1,0:T(8,128)S(1)}, f32[32,16,128]{2,1,0:T(8,128)S(1)}, u32[]{:S(2)}, u32[]{:S(2)}) collective-permute-start(f32[32,16,128]{2,1,0:T(8,128)S(1)} %get-tuple-element.28), channel_id=1, source_target_pairs={{8,16},{24,32},{40,48},{56,64},{72,80},{88,96},{104,112},{120,128}... | collective-permute-start | bytes 786440 | tf_op jit(solution)/shard_map/ppermute | solution.py:194
  19.6 0.0 collective-permute-done.1.far_in
  19.6 9.3 %collective-permute-done.2.near_in = f32[32,16,128]{2,1,0:T(8,128)S(1)} collective-permute-done((f32[32,16,128]{2,1,0:T(8,128)S(1)}, f32[32,16,128]{2,1,0:T(8,128)S(1)}, u32[]{:S(2)}, u32[]{:S(2)}) %collective-permute-start.2) | collective-permute-done | bytes 262176 | tf_op jit(solution)/shard_map/ppermute | solution.py:194
  28.9 3.3 %shard_map.71 = (f32[16,4096]{1,0:T(8,128)S(1)}, f32[32,16,128]{2,1,0:T(8,128)S(1)}, f32[320,16,128]{2,1,0:T(8,128)S(1)}, f32[32,16,128]{2,1,0:T(8,128)S(1)}) custom-call(s32[1]{0:T(128)} %bitcast.place_ref, s32[6,64]{1,0:T(8,128)} %cols_hbm.3, bf16[448,4096]{1,0:T(8,128)(2,1)S(1)} %get-tuple-element.14.panel_ref, f32[16,4096]{1,0:T(8,128)S(1)} %copy-done.2, ...), custom_call_target="tpu_custom_call" | custom-call | tf_op jit(solution)/shard_map/pallas_call | solution.py:213
  32.2 1.9 %collective-permute-start.4 = (f32[32,16,128]{2,1,0:T(8,128)S(1)}, f32[32,16,128]{2,1,0:T(8,128)S(1)}, u32[]{:S(2)}, u32[]{:S(2)}) collective-permute-start(f32[32,16,128]{2,1,0:T(8,128)S(1)} %get-tuple-element.24), channel_id=1, source_target_pairs={{8,24},{24,40},{40,56},{56,72},{72,88},{88,104},{104,120},{120,136... | collective-permute-start | bytes 786440 | tf_op jit(solution)/shard_map/ppermute | solution.py:176
  34.1 0.2 shard_map.73
  34.4 1.9 %collective-permute-start.3 = (f32[64,16,128]{2,1,0:T(8,128)S(1)}, f32[64,16,128]{2,1,0:T(8,128)S(1)}, u32[]{:S(2)}, u32[]{:S(2)}) collective-permute-start(f32[64,16,128]{2,1,0:T(8,128)S(1)} %shard_map.73), channel_id=1, source_target_pairs={{0,8},{8,0},{16,24},{24,16},{32,40},{40,32},{48,56},{56,48},{64,72... | collective-permute-start | bytes 1572872 | tf_op jit(solution)/shard_map/ppermute | solution.py:185
  36.3 0.2 shard_map.72
  36.5 1.6 %collective-permute-done.3 = f32[64,16,128]{2,1,0:T(8,128)S(1)} collective-permute-done((f32[64,16,128]{2,1,0:T(8,128)S(1)}, f32[64,16,128]{2,1,0:T(8,128)S(1)}, u32[]{:S(2)}, u32[]{:S(2)}) %collective-permute-start.3) | collective-permute-done | bytes 524320 | tf_op jit(solution)/shard_map/ppermute | solution.py:185
  38.2 0.1 slice_add_fusion
  38.2 5.1 %collective-permute-start.5 = (f32[32,16,128]{2,1,0:T(8,128)S(1)}, f32[32,16,128]{2,1,0:T(8,128)S(1)}, u32[]{:S(2)}, u32[]{:S(2)}) collective-permute-start(f32[32,16,128]{2,1,0:T(8,128)S(1)} %get-tuple-element.26), channel_id=1, source_target_pairs={{8,16},{24,32},{40,48},{56,64},{72,80},{88,96},{104,112},{120,128}... | collective-permute-start | bytes 786440 | tf_op jit(solution)/shard_map/ppermute | solution.py:194
  43.3 0.0 collective-permute-done.4.far_in
  43.3 9.1 %collective-permute-done.5.near_in = f32[32,16,128]{2,1,0:T(8,128)S(1)} collective-permute-done((f32[32,16,128]{2,1,0:T(8,128)S(1)}, f32[32,16,128]{2,1,0:T(8,128)S(1)}, u32[]{:S(2)}, u32[]{:S(2)}) %collective-permute-start.5) | collective-permute-done | bytes 262176 | tf_op jit(solution)/shard_map/ppermute | solution.py:194
  52.4 1.4 %shard_map.74 = (f32[16,4096]{1,0:T(8,128)}, f32[16,4096]{1,0:T(8,128)}) custom-call(f32[16,4096]{1,0:T(8,128)S(1)} %copy-done.2, f32[16,4096]{1,0:T(8,128)S(1)} %get-tuple-element.20.first_ref, bf16[64,4096]{1,0:T(8,128)(2,1)S(1)} %copy-done, f32[32,16,128]{2,1,0:T(8,128)S(1)} %get-tuple-element.23.here_in, f32[32,16,128]{2,1,0:T(8,128)S(1)} %get-tuple-element.27.mate_in, ...), custom_call_target="tpu_custom_call" | custom-call | tf_op jit(solution)/shard_map/pallas_call | solution.py:222
  (3 shorter events, 0.0 us)
Async XLA Ops:
  5.1 14.4 %collective-permute-start.1 = (f32[32,16,128]{2,1,0:T(8,128)S(1)}, f32[32,16,128]{2,1,0:T(8,128)S(1)}, u32[]{:S(2)}, u32[]{:S(2)}) collective-permute-start(f32[32,16,128]{2,1,0:T(8,128)S(1)} %get-tuple-element.18), channel_id=1, source_target_pairs={{8,24},{24,40},{40,56},{56,72},{72,88},{88,104},{104,120},{120,136... | collective-permute-start | bytes 786440 | tf_op jit(solution)/shard_map/ppermute | solution.py:176
  10.7 3.8 %collective-permute-start = (f32[64,16,128]{2,1,0:T(8,128)S(1)}, f32[64,16,128]{2,1,0:T(8,128)S(1)}, u32[]{:S(2)}, u32[]{:S(2)}) collective-permute-start(f32[64,16,128]{2,1,0:T(8,128)S(1)} %shard_map.70), channel_id=1, source_target_pairs={{0,8},{8,0},{16,24},{24,16},{32,40},{40,32},{48,56},{56,48},{64,72... | collective-permute-start | bytes 1572872 | tf_op jit(solution)/shard_map/ppermute | solution.py:185
  12.6 16.3 %copy-start = (bf16[64,4096]{1,0:T(8,128)(2,1)S(1)}, bf16[64,4096]{1,0:T(8,128)(2,1)}, u32[]{:S(2)}) copy-start(bf16[64,4096]{1,0:T(8,128)(2,1)} %inv_ref.3) | copy-start | bytes 1572868
  12.6 16.3 %copy-start.1 = (f32[16,4096]{1,0:T(8,128)S(1)}, f32[16,4096]{1,0:T(8,128)}, u32[]{:S(2)}) copy-start(f32[16,4096]{1,0:T(8,128)} %start_ref.1) | copy-start | bytes 786436
  12.7 16.3 %copy-start.2 = (f32[16,4096]{1,0:T(8,128)S(1)}, f32[16,4096]{1,0:T(8,128)}, u32[]{:S(2)}) copy-start(f32[16,4096]{1,0:T(8,128)} %right_ref.3) | copy-start | bytes 786436
  14.6 14.4 %collective-permute-start.2 = (f32[32,16,128]{2,1,0:T(8,128)S(1)}, f32[32,16,128]{2,1,0:T(8,128)S(1)}, u32[]{:S(2)}, u32[]{:S(2)}) collective-permute-start(f32[32,16,128]{2,1,0:T(8,128)S(1)} %get-tuple-element.28), channel_id=1, source_target_pairs={{8,16},{24,32},{40,48},{56,64},{72,80},{88,96},{104,112},{120,128}... | collective-permute-start | bytes 786440 | tf_op jit(solution)/shard_map/ppermute | solution.py:194
  32.2 11.1 %collective-permute-start.4 = (f32[32,16,128]{2,1,0:T(8,128)S(1)}, f32[32,16,128]{2,1,0:T(8,128)S(1)}, u32[]{:S(2)}, u32[]{:S(2)}) collective-permute-start(f32[32,16,128]{2,1,0:T(8,128)S(1)} %get-tuple-element.24), channel_id=1, source_target_pairs={{8,24},{24,40},{40,56},{56,72},{72,88},{88,104},{104,120},{120,136... | collective-permute-start | bytes 786440 | tf_op jit(solution)/shard_map/ppermute | solution.py:176
  34.4 3.8 %collective-permute-start.3 = (f32[64,16,128]{2,1,0:T(8,128)S(1)}, f32[64,16,128]{2,1,0:T(8,128)S(1)}, u32[]{:S(2)}, u32[]{:S(2)}) collective-permute-start(f32[64,16,128]{2,1,0:T(8,128)S(1)} %shard_map.73), channel_id=1, source_target_pairs={{0,8},{8,0},{16,24},{24,16},{32,40},{40,32},{48,56},{56,48},{64,72... | collective-permute-start | bytes 1572872 | tf_op jit(solution)/shard_map/ppermute | solution.py:185
  38.2 14.2 %collective-permute-start.5 = (f32[32,16,128]{2,1,0:T(8,128)S(1)}, f32[32,16,128]{2,1,0:T(8,128)S(1)}, u32[]{:S(2)}, u32[]{:S(2)}) collective-permute-start(f32[32,16,128]{2,1,0:T(8,128)S(1)} %get-tuple-element.26), channel_id=1, source_target_pairs={{8,16},{24,32},{40,48},{56,64},{72,80},{88,96},{104,112},{120,128}... | collective-permute-start | bytes 786440 | tf_op jit(solution)/shard_map/ppermute | solution.py:194

commit v4 on v3

--- a/solution.py
+++ b/solution.py
@@ -8,7 +8,9 @@
 DOF = 64
 SLOTS = 7
 QUAD = 4 * DOF
-CHUNKS = 8
+CHUNKS = 4
+WINDOWS = 2
+PIECES = 2
 
 
 def masked_lanes(value, part):
@@ -21,7 +23,7 @@
     return lax.dot_general(spread, panel, (((1,), (1,)), ((), ())), preferred_element_type=jnp.float32)
 
 
-def scatter(vb_ref, panel_of, cols_ref, device, window, own_ref, stage_ref):
+def scatter(vb_ref, panel_of, cols_ref, device, windows, own_ref, stage_ref):
     width = vb_ref.shape[0]
     count = cols_ref.shape[1]
     low = lax.broadcasted_iota(jnp.int32, (width, 2 * DOF), 1) < DOF
@@ -34,34 +36,48 @@
             for s in range(1, SLOTS):
                 tile = stage[rows, (s // 2) * 2 * DOF : (s // 2 + 1) * 2 * DOF]
                 place = cols_ref[s - 1, 4 * quad + e] - base
-                window[place] += jnp.where(low, tile, 0.0) if s % 2 == 0 else jnp.where(low, 0.0, tile)
+                windows[s % WINDOWS][place] += jnp.where(low, tile, 0.0) if s % 2 == 0 else jnp.where(low, 0.0, tile)
         for pair in range(2):
             even = stage[2 * pair * width : (2 * pair + 1) * width, : 2 * DOF]
             odd = stage[(2 * pair + 1) * width : (2 * pair + 2) * width, : 2 * DOF]
             own_ref[2 * quad + pair] = jnp.where(low, even, pltpu.roll(odd, DOF, 1))
 
 
-def hand_out(device, window, role, out, at=0, more=None):
-    half = window.shape[0] // 10
-    low = lax.broadcasted_iota(jnp.int32, window.shape[1:], 1) < DOF
+def sum_of(windows, place):
+    total = windows[0][place]
+    for window in windows[1:]:
+        total = total + window[place]
+    return total
+
+
+def clear(windows):
+    for window in windows:
+        window[...] = jnp.zeros_like(window)
+
+
+def hand_out(device, windows, role, out, at=0, more=None):
+    half = windows[0].shape[0] // 10
+    low = lax.broadcasted_iota(jnp.int32, windows[0].shape[1:], 1) < DOF
     core = lax.rem(device, 2)
     first = (core * (4 - role) + (1 - core) * role) * 2 * half
     for pair in range(half):
-        even = window[first + 2 * pair]
-        odd = window[first + 2 * pair + 1]
+        even = sum_of(windows, first + 2 * pair)
+        odd = sum_of(windows, first + 2 * pair + 1)
         total = jnp.where(low, even, odd) + pltpu.roll(jnp.where(low, odd, even), DOF, 1)
         out[at + pair] = total if more is None else total + more[pair]
 
 
-def mate_kernel(place_ref, window, mate_ref):
+def mate_kernel(place_ref, *refs):
+    windows, (mate_ref,) = refs[:WINDOWS], refs[WINDOWS:]
     half = mate_ref.shape[0] // 2
-    hand_out(place_ref[0], window, 3, mate_ref)
-    hand_out(place_ref[0], window, 4, mate_ref, half)
-
-
-def rest_kernel(place_ref, window, own_ref, near_ref, here_ref):
-    hand_out(place_ref[0], window, 1, near_ref)
-    hand_out(place_ref[0], window, 2, here_ref, 0, own_ref)
+    hand_out(place_ref[0], windows, 3, mate_ref)
+    hand_out(place_ref[0], windows, 4, mate_ref, half)
+
+
+def rest_kernel(place_ref, *refs):
+    windows, (own_ref, near_ref, here_ref) = refs[:WINDOWS], refs[WINDOWS:]
+    hand_out(place_ref[0], windows, 1, near_ref)
+    hand_out(place_ref[0], windows, 2, here_ref, 0, own_ref)
 
 
 def fetch(panel_hbm, panel_ref, sem):
@@ -86,20 +102,20 @@
     return panel_of
 
 
-def first_kernel(place_ref, cols_hbm, panel_hbm, start_hbm, far_ref, window, own_ref, panel_ref,
-                 cols_ref, start_ref, vb_ref, stage_ref, sem):
+def first_kernel(place_ref, cols_hbm, panel_hbm, start_hbm, *refs):
+    windows, (own_ref, far_ref, panel_ref, cols_ref, start_ref, vb_ref, stage_ref, sem) = refs[:WINDOWS], refs[WINDOWS:]
     device = place_ref[0]
     small = pltpu.make_async_copy(cols_hbm, cols_ref, sem.at[CHUNKS])
     begin = pltpu.make_async_copy(start_hbm, start_ref, sem.at[CHUNKS + 1])
     begin.start()
     small.start()
     copies = fetch(panel_hbm, panel_ref, sem)
-    window[...] = jnp.zeros_like(window)
+    clear(windows)
     begin.wait()
     vb_ref[...] = start_ref[...].astype(jnp.bfloat16)
     small.wait()
-    scatter(vb_ref, panels(copies, panel_ref, cols_ref.shape[1]), cols_ref, device, window, own_ref, stage_ref)
-    hand_out(device, window, 0, far_ref)
+    scatter(vb_ref, panels(copies, panel_ref, cols_ref.shape[1]), cols_ref, device, windows, own_ref, stage_ref)
+    hand_out(device, windows, 0, far_ref)
 
 
 def residual_and_update(quad, right_ref, from_ref, inv_ref, parts):
@@ -117,29 +133,39 @@
     return res, from_ref[:, lanes] + update
 
 
-def second_kernel(place_ref, cols_hbm, panel_ref, right_ref, start_ref, inv_ref, here_in, mate_in, far_in, near_in,
-                  first_ref, far_ref, window, own_ref, cols_ref, vb_ref, stage_ref, sem):
+def second_kernel(place_ref, cols_hbm, panel_ref, right_ref, start_ref, inv_ref, here_in, mate_in, far_in, near_in, *refs):
+    windows, (own_ref, far_ref, first_ref, cols_ref, vb_ref, stage_ref, sem) = refs[:WINDOWS], refs[WINDOWS:]
     device = place_ref[0]
     count = cols_ref.shape[1]
     small = pltpu.make_async_copy(cols_hbm, cols_ref, sem.at[CHUNKS])
     small.start()
-    window[...] = jnp.zeros_like(window)
+    clear(windows)
     for quad in range(count // 4):
         _, first = residual_and_update(quad, right_ref, start_ref, inv_ref, (here_in, mate_in, far_in, near_in))
         lanes = slice(quad * QUAD, (quad + 1) * QUAD)
         first_ref[:, lanes] = first
         vb_ref[:, lanes] = first.astype(jnp.bfloat16)
     small.wait()
-    scatter(vb_ref, panels((), panel_ref, count), cols_ref, device, window, own_ref, stage_ref)
-    hand_out(device, window, 0, far_ref)
-
-
-def last_kernel(right_ref, first_ref, inv_ref, here_in, mate_in, far_in, near_in, adjoint_ref, residual_ref):
-    for quad in range(right_ref.shape[1] // QUAD):
+    scatter(vb_ref, panels((), panel_ref, count), cols_ref, device, windows, own_ref, stage_ref)
+    hand_out(device, windows, 0, far_ref)
+
+
+def last_kernel(right_ref, first_ref, inv_ref, here_in, mate_in, far_in, near_in, adjoint_hbm, residual_hbm, adjoint_ref, residual_ref, sem):
+    quads = right_ref.shape[1] // QUAD
+    copies = []
+    for quad in range(quads):
         lanes = slice(quad * QUAD, (quad + 1) * QUAD)
         res, adjoint = residual_and_update(quad, right_ref, first_ref, inv_ref, (here_in, mate_in, far_in, near_in))
         residual_ref[:, lanes] = res
         adjoint_ref[:, lanes] = adjoint
+        if (quad + 1) % (quads // PIECES) == 0:
+            piece = quad // (quads // PIECES)
+            done = pl.ds(piece * (quads // PIECES) * QUAD, quads // PIECES * QUAD)
+            for i, (kept, out) in enumerate(((residual_ref, residual_hbm), (adjoint_ref, adjoint_hbm))):
+                copies.append(pltpu.make_async_copy(kept.at[:, done], out.at[:, done], sem.at[i, piece]))
+                copies[-1].start()
+    for copy in copies:
+        copy.wait()
 
 
 VMEM = pl.BlockSpec(memory_space=pltpu.VMEM)
@@ -151,7 +177,7 @@
 def applied(width, count):
     slab = jax.ShapeDtypeStruct((count // 2, width, 2 * DOF), jnp.float32)
     window = jax.ShapeDtypeStruct((5 * count, width, 2 * DOF), jnp.float32)
-    return [slab, window, slab]
+    return [window] * WINDOWS + [slab, slab]
 
 
 def scratch(width, count):
@@ -166,7 +192,7 @@
     return pltpu.with_memory_space_constraint(value, pltpu.HBM)
 
 
-def exchange(place, far, window, own):
+def exchange(place, windows, own, far):
     size = lax.axis_size("elem")
     half, width, lanes = own.shape
     slab = jax.ShapeDtypeStruct(own.shape, jnp.float32)
@@ -177,20 +203,20 @@
     mate = pl.pallas_call(
         mate_kernel,
         out_shape=double,
-        in_specs=[SMEM, VMEM],
+        in_specs=[SMEM] + [VMEM] * WINDOWS,
         out_specs=VMEM,
         compiler_params=PARAMS,
         cost_estimate=pl.CostEstimate(flops=10**8, bytes_accessed=4 * 10**6, transcendentals=0),
-    )(place, window)
+    )(place, *windows)
     mate = lax.ppermute(mate, "elem", [(i, i ^ 1) for i in range(size)])
     near, here = pl.pallas_call(
         rest_kernel,
         out_shape=[slab, slab],
-        in_specs=[SMEM, VMEM, VMEM],
+        in_specs=[SMEM] + [VMEM] * (WINDOWS + 1),
         out_specs=[VMEM, VMEM],
         compiler_params=PARAMS,
         cost_estimate=pl.CostEstimate(flops=10**10, bytes_accessed=4 * 10**6, transcendentals=0),
-    )(place, window, own)
+    )(place, *windows, own)
     near = lax.ppermute(near + mate[half:], "elem", across)
     return here, mate[:half], far, near
 
@@ -201,29 +227,30 @@
     place = lax.axis_index("elem").astype(jnp.int32).reshape(1)
     out = jax.ShapeDtypeStruct(start.shape, jnp.float32)
     cols = in_hbm(cols)
-    far, window, own, panel = pl.pallas_call(
+    *windows, own, far, panel = pl.pallas_call(
         first_kernel,
         out_shape=applied(width, count) + [pltpu.VMEM(blocks.shape[::-1], jnp.bfloat16)],
         in_specs=[SMEM, HBM, HBM, HBM],
-        out_specs=[VMEM] * 4,
+        out_specs=[VMEM] * (WINDOWS + 3),
         scratch_shapes=[pltpu.SMEM(cols.shape, jnp.int32), pltpu.VMEM(start.shape, jnp.float32)] + scratch(width, count),
         compiler_params=PARAMS,
     )(place, cols, in_hbm(blocks.T), in_hbm(start))
-    parts = exchange(place, far, window, own)
-    first, far, window, own = pl.pallas_call(
+    parts = exchange(place, windows, own, far)
+    *windows, own, far, first = pl.pallas_call(
         second_kernel,
-        out_shape=[out] + applied(width, count),
+        out_shape=applied(width, count) + [out],
         in_specs=[SMEM, HBM] + [VMEM] * 8,
-        out_specs=[VMEM] * 4,
+        out_specs=[VMEM] * (WINDOWS + 3),
         scratch_shapes=[pltpu.SMEM(cols.shape, jnp.int32)] + scratch(width, count),
         compiler_params=PARAMS,
     )(place, cols, panel, right_side, start, inverse, *parts)
-    parts = exchange(place, far, window, own)
+    parts = exchange(place, windows, own, far)
     adjoint, residual = pl.pallas_call(
         last_kernel,
         out_shape=[out, out],
         in_specs=[VMEM] * 7,
-        out_specs=[VMEM] * 2,
+        out_specs=[HBM] * 2,
+        scratch_shapes=[pltpu.VMEM(start.shape, jnp.float32)] * 2 + [pltpu.SemaphoreType.DMA((2, PIECES))],
         compiler_params=PARAMS,
     )(right_side, first, inverse, *parts)
     return (adjoint, residual)

time: 54.1 us -> 52.3 us (0.967)
  the two profiles are of different devices: /device:TPU:251 before, /device:TPU:255 now
where the time goes in v4:
time: 52.3 us; the launch traced here: 52 us
  waiting for transfers between devices  21.7 us (41%)
  starting transfers between devices  21.2 us (41%)
  Pallas kernels  8.25 us (16%)
  between operations  0.77 us (1%)
    ppermute x2, waiting for transfers between devices, exchange(): near = lax.ppermute(near + mate[half:], 'elem', across)  18.4 us
    ppermute x2, starting transfers between devices, exchange(): near = lax.ppermute(near + mate[half:], 'elem', across)  10.1 us
    ppermute x2, starting transfers between devices, exchange(): far = lax.ppermute(far, 'elem', outward)  7.24 us
    ppermute x2, starting transfers between devices, exchange(): mate = lax.ppermute(mate, 'elem', [(i, i ^ 1) for i in range(size)])  3.84 us
    pallas_call x1, Pallas kernels, body(): pl.pallas_call(first_kernel, out_shape=applied(width, count) + [pltpu.VME...  3.6 us
    ppermute x2, waiting for transfers between devices, exchange(): mate = lax.ppermute(mate, 'elem', [(i, i ^ 1) for i in range(size)])  3.27 us
    pallas_call x1, Pallas kernels, body(): pl.pallas_call(second_kernel, out_shape=applied(width, count) + [out], in...  2.41 us
    pallas_call x1, Pallas kernels, body(): pl.pallas_call(last_kernel, out_shape=[out, out], in_specs=[VMEM] * 7, ou...  1.37 us
  transfers between devices with their start and end apart: 6, of which 4 were waited for; matrix products, arithmetic and copies ran while one was open for 0% of the time, Pallas kernels for 2%

profile of v4, /device:TPU:255, one launch (start us, length us, event | category | flops | bytes accessed | tf_op | source)
XLA Modules:
  0.0 52.0 jit_solution(15319999011760232287)
XLA Ops:
  0.6 3.6 %shard_map.68 = (f32[320,16,128]{2,1,0:T(8,128)S(1)}, f32[320,16,128]{2,1,0:T(8,128)S(1)}, f32[32,16,128]{2,1,0:T(8,128)S(1)}, f32[32,16,128]{2,1,0:T(8,128)S(1)}, bf16[448,4096]{1,0:T(8,128)(2,1)S(1)}) custom-call(s32[1]{0:T(128)} %bitcast.place_ref, s32[6,64]{1,0:T(8,128)} %cols_hbm.3, bf16[448,4096]{1,0:T(8,128)(2,1)} %bitcast.2, f32[16,4096]{1,0:T(8,128)} %start_ref.1), custom_call_target="tpu_custom_call" | custom-call | tf_op jit(solution)/shard_map/pallas_call | solution.py:230
  4.2 5.3 %collective-permute-start.1 = (f32[32,16,128]{2,1,0:T(8,128)S(1)}, f32[32,16,128]{2,1,0:T(8,128)S(1)}, u32[]{:S(2)}, u32[]{:S(2)}) collective-permute-start(f32[32,16,128]{2,1,0:T(8,128)S(1)} %get-tuple-element.21), channel_id=1, source_target_pairs={{8,24},{24,40},{40,56},{56,72},{72,88},{88,104},{104,120},{120,136... | collective-permute-start | bytes 786440 | tf_op jit(solution)/shard_map/ppermute | solution.py:202
  9.6 0.2 shard_map.70
  9.8 1.9 %collective-permute-start = (f32[64,16,128]{2,1,0:T(8,128)S(1)}, f32[64,16,128]{2,1,0:T(8,128)S(1)}, u32[]{:S(2)}, u32[]{:S(2)}) collective-permute-start(f32[64,16,128]{2,1,0:T(8,128)S(1)} %shard_map.70), channel_id=1, source_target_pairs={{0,8},{8,0},{16,24},{24,16},{32,40},{40,32},{48,56},{56,48},{64,72... | collective-permute-start | bytes 1572872 | tf_op jit(solution)/shard_map/ppermute | solution.py:211
  11.7 0.0 copy-start
  11.7 0.0 copy-start.1
  11.7 0.0 copy-start.2
  11.8 0.2 shard_map.69
  12.0 1.6 %collective-permute-done = f32[64,16,128]{2,1,0:T(8,128)S(1)} collective-permute-done((f32[64,16,128]{2,1,0:T(8,128)S(1)}, f32[64,16,128]{2,1,0:T(8,128)S(1)}, u32[]{:S(2)}, u32[]{:S(2)}) %collective-permute-start) | collective-permute-done | bytes 524320 | tf_op jit(solution)/shard_map/ppermute | solution.py:211
  13.6 0.1 slice_add_fusion.1
  13.7 5.0 %collective-permute-start.2 = (f32[32,16,128]{2,1,0:T(8,128)S(1)}, f32[32,16,128]{2,1,0:T(8,128)S(1)}, u32[]{:S(2)}, u32[]{:S(2)}) collective-permute-start(f32[32,16,128]{2,1,0:T(8,128)S(1)} %get-tuple-element.32), channel_id=1, source_target_pairs={{8,16},{24,32},{40,48},{56,64},{72,80},{88,96},{104,112},{120,128}... | collective-permute-start | bytes 786440 | tf_op jit(solution)/shard_map/ppermute | solution.py:220
  18.7 0.0 collective-permute-done.1.far_in
  18.7 9.3 %collective-permute-done.2.near_in = f32[32,16,128]{2,1,0:T(8,128)S(1)} collective-permute-done((f32[32,16,128]{2,1,0:T(8,128)S(1)}, f32[32,16,128]{2,1,0:T(8,128)S(1)}, u32[]{:S(2)}, u32[]{:S(2)}) %collective-permute-start.2) | collective-permute-done | bytes 262176 | tf_op jit(solution)/shard_map/ppermute | solution.py:220
  28.0 2.4 %shard_map.71 = (f32[320,16,128]{2,1,0:T(8,128)S(1)}, f32[320,16,128]{2,1,0:T(8,128)S(1)}, f32[32,16,128]{2,1,0:T(8,128)S(1)}, f32[32,16,128]{2,1,0:T(8,128)S(1)}, f32[16,4096]{1,0:T(8,128)S(1)}) custom-call(s32[1]{0:T(128)} %bitcast.place_ref, s32[6,64]{1,0:T(8,128)} %cols_hbm.3, bf16[448,4096]{1,0:T(8,128)(2,1)S(1)} %get-tuple-element.16.panel_ref, ...), custom_call_target="tpu_custom_call" | custom-call | tf_op jit(solution)/shard_map/pallas_call | solution.py:239
  30.4 1.9 %collective-permute-start.4 = (f32[32,16,128]{2,1,0:T(8,128)S(1)}, f32[32,16,128]{2,1,0:T(8,128)S(1)}, u32[]{:S(2)}, u32[]{:S(2)}) collective-permute-start(f32[32,16,128]{2,1,0:T(8,128)S(1)} %get-tuple-element.28), channel_id=1, source_target_pairs={{8,24},{24,40},{40,56},{56,72},{72,88},{88,104},{104,120},{120,136... | collective-permute-start | bytes 786440 | tf_op jit(solution)/shard_map/ppermute | solution.py:202
  32.4 0.2 shard_map.73
  32.6 1.9 %collective-permute-start.3 = (f32[64,16,128]{2,1,0:T(8,128)S(1)}, f32[64,16,128]{2,1,0:T(8,128)S(1)}, u32[]{:S(2)}, u32[]{:S(2)}) collective-permute-start(f32[64,16,128]{2,1,0:T(8,128)S(1)} %shard_map.73), channel_id=1, source_target_pairs={{0,8},{8,0},{16,24},{24,16},{32,40},{40,32},{48,56},{56,48},{64,72... | collective-permute-start | bytes 1572872 | tf_op jit(solution)/shard_map/ppermute | solution.py:211
  34.5 0.2 shard_map.72
  34.7 1.7 %collective-permute-done.3 = f32[64,16,128]{2,1,0:T(8,128)S(1)} collective-permute-done((f32[64,16,128]{2,1,0:T(8,128)S(1)}, f32[64,16,128]{2,1,0:T(8,128)S(1)}, u32[]{:S(2)}, u32[]{:S(2)}) %collective-permute-start.3) | collective-permute-done | bytes 524320 | tf_op jit(solution)/shard_map/ppermute | solution.py:211
  36.4 0.1 slice_add_fusion
  36.4 5.1 %collective-permute-start.5 = (f32[32,16,128]{2,1,0:T(8,128)S(1)}, f32[32,16,128]{2,1,0:T(8,128)S(1)}, u32[]{:S(2)}, u32[]{:S(2)}) collective-permute-start(f32[32,16,128]{2,1,0:T(8,128)S(1)} %get-tuple-element.30), channel_id=1, source_target_pairs={{8,16},{24,32},{40,48},{56,64},{72,80},{88,96},{104,112},{120,128}... | collective-permute-start | bytes 786440 | tf_op jit(solution)/shard_map/ppermute | solution.py:220
  41.5 0.0 collective-permute-done.4.far_in
  41.5 9.1 %collective-permute-done.5.near_in = f32[32,16,128]{2,1,0:T(8,128)S(1)} collective-permute-done((f32[32,16,128]{2,1,0:T(8,128)S(1)}, f32[32,16,128]{2,1,0:T(8,128)S(1)}, u32[]{:S(2)}, u32[]{:S(2)}) %collective-permute-start.5) | collective-permute-done | bytes 262176 | tf_op jit(solution)/shard_map/ppermute | solution.py:220
  50.6 1.4 %shard_map.74 = (f32[16,4096]{1,0:T(8,128)}, f32[16,4096]{1,0:T(8,128)}) custom-call(f32[16,4096]{1,0:T(8,128)S(1)} %copy-done.2, f32[16,4096]{1,0:T(8,128)S(1)} %get-tuple-element.23.first_ref, bf16[64,4096]{1,0:T(8,128)(2,1)S(1)} %copy-done, f32[32,16,128]{2,1,0:T(8,128)S(1)} %get-tuple-element.27.here_in, f32[32,16,128]{2,1,0:T(8,128)S(1)} %get-tuple-element.31.mate_in, ...), custom_call_target="tpu_custom_call" | custom-call | tf_op jit(solution)/shard_map/pallas_call | solution.py:248
  (3 shorter events, 0.0 us)
Async XLA Ops:
  4.2 14.4 %collective-permute-start.1 = (f32[32,16,128]{2,1,0:T(8,128)S(1)}, f32[32,16,128]{2,1,0:T(8,128)S(1)}, u32[]{:S(2)}, u32[]{:S(2)}) collective-permute-start(f32[32,16,128]{2,1,0:T(8,128)S(1)} %get-tuple-element.21), channel_id=1, source_target_pairs={{8,24},{24,40},{40,56},{56,72},{72,88},{88,104},{104,120},{120,136... | collective-permute-start | bytes 786440 | tf_op jit(solution)/shard_map/ppermute | solution.py:202
  9.8 3.8 %collective-permute-start = (f32[64,16,128]{2,1,0:T(8,128)S(1)}, f32[64,16,128]{2,1,0:T(8,128)S(1)}, u32[]{:S(2)}, u32[]{:S(2)}) collective-permute-start(f32[64,16,128]{2,1,0:T(8,128)S(1)} %shard_map.70), channel_id=1, source_target_pairs={{0,8},{8,0},{16,24},{24,16},{32,40},{40,32},{48,56},{56,48},{64,72... | collective-permute-start | bytes 1572872 | tf_op jit(solution)/shard_map/ppermute | solution.py:211
  11.7 16.3 %copy-start = (bf16[64,4096]{1,0:T(8,128)(2,1)S(1)}, bf16[64,4096]{1,0:T(8,128)(2,1)}, u32[]{:S(2)}) copy-start(bf16[64,4096]{1,0:T(8,128)(2,1)} %inv_ref.3) | copy-start | bytes 1572868
  11.7 16.3 %copy-start.1 = (f32[16,4096]{1,0:T(8,128)S(1)}, f32[16,4096]{1,0:T(8,128)}, u32[]{:S(2)}) copy-start(f32[16,4096]{1,0:T(8,128)} %start_ref.1) | copy-start | bytes 786436
  11.7 16.3 %copy-start.2 = (f32[16,4096]{1,0:T(8,128)S(1)}, f32[16,4096]{1,0:T(8,128)}, u32[]{:S(2)}) copy-start(f32[16,4096]{1,0:T(8,128)} %right_ref.3) | copy-start | bytes 786436
  13.7 14.4 %collective-permute-start.2 = (f32[32,16,128]{2,1,0:T(8,128)S(1)}, f32[32,16,128]{2,1,0:T(8,128)S(1)}, u32[]{:S(2)}, u32[]{:S(2)}) collective-permute-start(f32[32,16,128]{2,1,0:T(8,128)S(1)} %get-tuple-element.32), channel_id=1, source_target_pairs={{8,16},{24,32},{40,48},{56,64},{72,80},{88,96},{104,112},{120,128}... | collective-permute-start | bytes 786440 | tf_op jit(solution)/shard_map/ppermute | solution.py:220
  30.4 11.1 %collective-permute-start.4 = (f32[32,16,128]{2,1,0:T(8,128)S(1)}, f32[32,16,128]{2,1,0:T(8,128)S(1)}, u32[]{:S(2)}, u32[]{:S(2)}) collective-permute-start(f32[32,16,128]{2,1,0:T(8,128)S(1)} %get-tuple-element.28), channel_id=1, source_target_pairs={{8,24},{24,40},{40,56},{56,72},{72,88},{88,104},{104,120},{120,136... | collective-permute-start | bytes 786440 | tf_op jit(solution)/shard_map/ppermute | solution.py:202
  32.6 3.8 %collective-permute-start.3 = (f32[64,16,128]{2,1,0:T(8,128)S(1)}, f32[64,16,128]{2,1,0:T(8,128)S(1)}, u32[]{:S(2)}, u32[]{:S(2)}) collective-permute-start(f32[64,16,128]{2,1,0:T(8,128)S(1)} %shard_map.73), channel_id=1, source_target_pairs={{0,8},{8,0},{16,24},{24,16},{32,40},{40,32},{48,56},{56,48},{64,72... | collective-permute-start | bytes 1572872 | tf_op jit(solution)/shard_map/ppermute | solution.py:211
  36.4 14.2 %collective-permute-start.5 = (f32[32,16,128]{2,1,0:T(8,128)S(1)}, f32[32,16,128]{2,1,0:T(8,128)S(1)}, u32[]{:S(2)}, u32[]{:S(2)}) collective-permute-start(f32[32,16,128]{2,1,0:T(8,128)S(1)} %get-tuple-element.30), channel_id=1, source_target_pairs={{8,16},{24,32},{40,48},{56,64},{72,80},{88,96},{104,112},{120,128}... | collective-permute-start | bytes 786440 | tf_op jit(solution)/shard_map/ppermute | solution.py:220

commit v5 on v4

--- a/solution.py
+++ b/solution.py
@@ -8,7 +8,7 @@
 DOF = 64
 SLOTS = 7
 QUAD = 4 * DOF
-CHUNKS = 4
+CHUNKS = 2
 WINDOWS = 2
 PIECES = 2
 
@@ -28,19 +28,32 @@
     count = cols_ref.shape[1]
     low = lax.broadcasted_iota(jnp.int32, (width, 2 * DOF), 1) < DOF
     base = (device - 2) * count
-    for quad in range(count // 4):
+
+    def multiply(quad):
+        stage_ref[quad, :, : SLOTS * DOF] = products(vb_ref[:, quad * QUAD : (quad + 1) * QUAD], panel_of(quad))
+
+    def add(quad):
         stage = stage_ref.at[quad]
-        stage[:, : SLOTS * DOF] = products(vb_ref[:, quad * QUAD : (quad + 1) * QUAD], panel_of(quad))
+        kept = None
         for e in range(4):
             rows = slice(e * width, (e + 1) * width)
-            for s in range(1, SLOTS):
-                tile = stage[rows, (s // 2) * 2 * DOF : (s // 2 + 1) * 2 * DOF]
-                place = cols_ref[s - 1, 4 * quad + e] - base
-                windows[s % WINDOWS][place] += jnp.where(low, tile, 0.0) if s % 2 == 0 else jnp.where(low, 0.0, tile)
-        for pair in range(2):
-            even = stage[2 * pair * width : (2 * pair + 1) * width, : 2 * DOF]
-            odd = stage[(2 * pair + 1) * width : (2 * pair + 2) * width, : 2 * DOF]
-            own_ref[2 * quad + pair] = jnp.where(low, even, pltpu.roll(odd, DOF, 1))
+            for pair in range(4):
+                tile = stage[rows, pair * 2 * DOF : (pair + 1) * 2 * DOF]
+                if pair == 0:
+                    if e % 2 == 0:
+                        kept = tile
+                    else:
+                        own_ref[2 * quad + e // 2] = jnp.where(low, kept, pltpu.roll(tile, DOF, 1))
+                else:
+                    place = cols_ref[2 * pair - 1, 4 * quad + e] - base
+                    windows[0][place] += jnp.where(low, tile, 0.0)
+                if pair < 3:
+                    place = cols_ref[2 * pair, 4 * quad + e] - base
+                    windows[1][place] += jnp.where(low, 0.0, tile)
+
+    for quad in range(count // 4):
+        multiply(quad)
+        add(quad)
 
 
 def sum_of(windows, place):
@@ -127,9 +140,13 @@
             total = total + part[pair]
         sums.append(total)
     res = right_ref[:, lanes] - jnp.concatenate(sums, 1)
-    inv = inv_ref[:, lanes]
-    weights = jnp.concatenate([masked_lanes(inv, e) for e in range(4)], 0)
-    update = lax.dot_general(res.astype(jnp.bfloat16), weights, (((1,), (1,)), ((), ())), preferred_element_type=jnp.float32)
+    resb = res.astype(jnp.bfloat16)
+    spread = jnp.concatenate([masked_lanes(resb, e) for e in range(4)], 0)
+    out = lax.dot_general(spread, inv_ref[:, lanes], (((1,), (1,)), ((), ())), preferred_element_type=jnp.float32)
+    width = res.shape[0]
+    nothing = jnp.zeros((width, DOF), jnp.float32)
+    each = [jnp.concatenate([out[e * width : (e + 1) * width], nothing], 1) for e in range(4)]
+    update = jnp.concatenate([each[0] + pltpu.roll(each[1], DOF, 1), each[2] + pltpu.roll(each[3], DOF, 1)], 1)
     return res, from_ref[:, lanes] + update
 
 
@@ -192,7 +209,7 @@
     return pltpu.with_memory_space_constraint(value, pltpu.HBM)
 
 
-def exchange(place, windows, own, far):
+def exchange(place, windows, own, far, hint):
     size = lax.axis_size("elem")
     half, width, lanes = own.shape
     slab = jax.ShapeDtypeStruct(own.shape, jnp.float32)
@@ -215,7 +232,7 @@
         in_specs=[SMEM] + [VMEM] * (WINDOWS + 1),
         out_specs=[VMEM, VMEM],
         compiler_params=PARAMS,
-        cost_estimate=pl.CostEstimate(flops=10**10, bytes_accessed=4 * 10**6, transcendentals=0),
+        cost_estimate=pl.CostEstimate(flops=hint, bytes_accessed=4 * 10**6, transcendentals=0),
     )(place, *windows, own)
     near = lax.ppermute(near + mate[half:], "elem", across)
     return here, mate[:half], far, near
@@ -235,7 +252,7 @@
         scratch_shapes=[pltpu.SMEM(cols.shape, jnp.int32), pltpu.VMEM(start.shape, jnp.float32)] + scratch(width, count),
         compiler_params=PARAMS,
     )(place, cols, in_hbm(blocks.T), in_hbm(start))
-    parts = exchange(place, windows, own, far)
+    parts = exchange(place, windows, own, far, 10**8)
     *windows, own, far, first = pl.pallas_call(
         second_kernel,
         out_shape=applied(width, count) + [out],
@@ -244,7 +261,7 @@
         scratch_shapes=[pltpu.SMEM(cols.shape, jnp.int32)] + scratch(width, count),
         compiler_params=PARAMS,
     )(place, cols, panel, right_side, start, inverse, *parts)
-    parts = exchange(place, windows, own, far)
+    parts = exchange(place, windows, own, far, 10**10)
     adjoint, residual = pl.pallas_call(
         last_kernel,
         out_shape=[out, out],

time: 52.3 us -> 50.6 us (0.967)
  the two profiles are of different devices: /device:TPU:255 before, /device:TPU:260 now
where the time goes in v5:
time: 50.6 us; the launch traced here: 50.4 us
  waiting for transfers between devices  23 us (45%)
  starting transfers between devices  18.7 us (37%)
  Pallas kernels  7.73 us (15%)
  between operations  0.78 us (2%)
    ppermute x2, waiting for transfers between devices, exchange(): near = lax.ppermute(near + mate[half:], 'elem', across)  21.4 us
    ppermute x2, starting transfers between devices, exchange(): near = lax.ppermute(near + mate[half:], 'elem', across)  9.38 us
    ppermute x2, starting transfers between devices, exchange(): far = lax.ppermute(far, 'elem', outward)  5.47 us
    ppermute x2, starting transfers between devices, exchange(): mate = lax.ppermute(mate, 'elem', [(i, i ^ 1) for i in range(size)])  3.84 us
    pallas_call x1, Pallas kernels, body(): pl.pallas_call(first_kernel, out_shape=applied(width, count) + [pltpu.VME...  3.55 us
    pallas_call x1, Pallas kernels, body(): pl.pallas_call(second_kernel, out_shape=applied(width, count) + [out], in...  2.2 us
    ppermute x2, waiting for transfers between devices, exchange(): mate = lax.ppermute(mate, 'elem', [(i, i ^ 1) for i in range(size)])  1.66 us
    pallas_call x1, Pallas kernels, body(): pl.pallas_call(last_kernel, out_shape=[out, out], in_specs=[VMEM] * 7, ou...  1.1 us
  transfers between devices with their start and end apart: 6, of which 3 were waited for; matrix products, arithmetic and copies ran while one was open for 0% of the time, Pallas kernels for 1%

profile of v5, /device:TPU:260, one launch (start us, length us, event | category | flops | bytes accessed | tf_op | source)
XLA Modules:
  0.0 50.4 jit_solution(3290067618339573415)
XLA Ops:
  0.6 3.5 %shard_map.68 = (f32[320,16,128]{2,1,0:T(8,128)S(1)}, f32[320,16,128]{2,1,0:T(8,128)S(1)}, f32[32,16,128]{2,1,0:T(8,128)S(1)}, f32[32,16,128]{2,1,0:T(8,128)S(1)}, bf16[448,4096]{1,0:T(8,128)(2,1)S(1)}) custom-call(s32[1]{0:T(128)} %bitcast.place_ref, s32[6,64]{1,0:T(8,128)} %cols_hbm.3, bf16[448,4096]{1,0:T(8,128)(2,1)} %bitcast.2, f32[16,4096]{1,0:T(8,128)} %start_ref.1), custom_call_target="tpu_custom_call" | custom-call | tf_op jit(solution)/shard_map/pallas_call | solution.py:247
  4.2 0.2 shard_map.70
  4.4 1.9 %collective-permute-start = (f32[64,16,128]{2,1,0:T(8,128)S(1)}, f32[64,16,128]{2,1,0:T(8,128)S(1)}, u32[]{:S(2)}, u32[]{:S(2)}) collective-permute-start(f32[64,16,128]{2,1,0:T(8,128)S(1)} %shard_map.70), channel_id=1, source_target_pairs={{0,8},{8,0},{16,24},{24,16},{32,40},{40,32},{48,56},{56,48},{64,72... | collective-permute-start | bytes 1572872 | tf_op jit(solution)/shard_map/ppermute | solution.py:228
  6.3 3.6 %collective-permute-start.1 = (f32[32,16,128]{2,1,0:T(8,128)S(1)}, f32[32,16,128]{2,1,0:T(8,128)S(1)}, u32[]{:S(2)}, u32[]{:S(2)}) collective-permute-start(f32[32,16,128]{2,1,0:T(8,128)S(1)} %get-tuple-element.21), channel_id=1, source_target_pairs={{8,24},{24,40},{40,56},{56,72},{72,88},{88,104},{104,120},{120,136... | collective-permute-start | bytes 786440 | tf_op jit(solution)/shard_map/ppermute | solution.py:219
  9.9 0.0 copy-start
  9.9 0.0 copy-start.1
  9.9 0.0 copy-start.2
  9.9 0.2 shard_map.69
  10.2 0.0 collective-permute-done
  10.2 0.1 slice_add_fusion.1
  10.2 6.3 %collective-permute-start.2 = (f32[32,16,128]{2,1,0:T(8,128)S(1)}, f32[32,16,128]{2,1,0:T(8,128)S(1)}, u32[]{:S(2)}, u32[]{:S(2)}) collective-permute-start(f32[32,16,128]{2,1,0:T(8,128)S(1)} %get-tuple-element.32), channel_id=1, source_target_pairs={{8,16},{24,32},{40,48},{56,64},{72,80},{88,96},{104,112},{120,128}... | collective-permute-start | bytes 786440 | tf_op jit(solution)/shard_map/ppermute | solution.py:237
  16.6 0.0 collective-permute-done.1.far_in
  16.6 10.2 %collective-permute-done.2.near_in = f32[32,16,128]{2,1,0:T(8,128)S(1)} collective-permute-done((f32[32,16,128]{2,1,0:T(8,128)S(1)}, f32[32,16,128]{2,1,0:T(8,128)S(1)}, u32[]{:S(2)}, u32[]{:S(2)}) %collective-permute-start.2) | collective-permute-done | bytes 262176 | tf_op jit(solution)/shard_map/ppermute | solution.py:237
  26.8 2.2 %shard_map.71 = (f32[320,16,128]{2,1,0:T(8,128)S(1)}, f32[320,16,128]{2,1,0:T(8,128)S(1)}, f32[32,16,128]{2,1,0:T(8,128)S(1)}, f32[32,16,128]{2,1,0:T(8,128)S(1)}, f32[16,4096]{1,0:T(8,128)S(1)}) custom-call(s32[1]{0:T(128)} %bitcast.place_ref, s32[6,64]{1,0:T(8,128)} %cols_hbm.3, bf16[448,4096]{1,0:T(8,128)(2,1)S(1)} %get-tuple-element.16.panel_ref, ...), custom_call_target="tpu_custom_call" | custom-call | tf_op jit(solution)/shard_map/pallas_call | solution.py:256
  29.0 1.9 %collective-permute-start.4 = (f32[32,16,128]{2,1,0:T(8,128)S(1)}, f32[32,16,128]{2,1,0:T(8,128)S(1)}, u32[]{:S(2)}, u32[]{:S(2)}) collective-permute-start(f32[32,16,128]{2,1,0:T(8,128)S(1)} %get-tuple-element.28), channel_id=1, source_target_pairs={{8,24},{24,40},{40,56},{56,72},{72,88},{88,104},{104,120},{120,136... | collective-permute-start | bytes 786440 | tf_op jit(solution)/shard_map/ppermute | solution.py:219
  30.9 0.2 shard_map.73
  31.2 1.9 %collective-permute-start.3 = (f32[64,16,128]{2,1,0:T(8,128)S(1)}, f32[64,16,128]{2,1,0:T(8,128)S(1)}, u32[]{:S(2)}, u32[]{:S(2)}) collective-permute-start(f32[64,16,128]{2,1,0:T(8,128)S(1)} %shard_map.73), channel_id=1, source_target_pairs={{0,8},{8,0},{16,24},{24,16},{32,40},{40,32},{48,56},{56,48},{64,72... | collective-permute-start | bytes 1572872 | tf_op jit(solution)/shard_map/ppermute | solution.py:228
  33.1 0.2 shard_map.72
  33.3 1.7 %collective-permute-done.3 = f32[64,16,128]{2,1,0:T(8,128)S(1)} collective-permute-done((f32[64,16,128]{2,1,0:T(8,128)S(1)}, f32[64,16,128]{2,1,0:T(8,128)S(1)}, u32[]{:S(2)}, u32[]{:S(2)}) %collective-permute-start.3) | collective-permute-done | bytes 524320 | tf_op jit(solution)/shard_map/ppermute | solution.py:228
  35.0 0.1 slice_add_fusion
  35.0 3.0 %collective-permute-start.5 = (f32[32,16,128]{2,1,0:T(8,128)S(1)}, f32[32,16,128]{2,1,0:T(8,128)S(1)}, u32[]{:S(2)}, u32[]{:S(2)}) collective-permute-start(f32[32,16,128]{2,1,0:T(8,128)S(1)} %get-tuple-element.30), channel_id=1, source_target_pairs={{8,16},{24,32},{40,48},{56,64},{72,80},{88,96},{104,112},{120,128}... | collective-permute-start | bytes 786440 | tf_op jit(solution)/shard_map/ppermute | solution.py:237
  38.1 0.0 collective-permute-done.4.far_in
  38.1 11.2 %collective-permute-done.5.near_in = f32[32,16,128]{2,1,0:T(8,128)S(1)} collective-permute-done((f32[32,16,128]{2,1,0:T(8,128)S(1)}, f32[32,16,128]{2,1,0:T(8,128)S(1)}, u32[]{:S(2)}, u32[]{:S(2)}) %collective-permute-start.5) | collective-permute-done | bytes 262176 | tf_op jit(solution)/shard_map/ppermute | solution.py:237
  49.3 1.1 %shard_map.74 = (f32[16,4096]{1,0:T(8,128)}, f32[16,4096]{1,0:T(8,128)}) custom-call(f32[16,4096]{1,0:T(8,128)S(1)} %copy-done.2, f32[16,4096]{1,0:T(8,128)S(1)} %get-tuple-element.23.first_ref, bf16[64,4096]{1,0:T(8,128)(2,1)S(1)} %copy-done, f32[32,16,128]{2,1,0:T(8,128)S(1)} %get-tuple-element.27.here_in, f32[32,16,128]{2,1,0:T(8,128)S(1)} %get-tuple-element.31.mate_in, ...), custom_call_target="tpu_custom_call" | custom-call | tf_op jit(solution)/shard_map/pallas_call | solution.py:265
  (3 shorter events, 0.0 us)
Async XLA Ops:
  4.4 5.7 %collective-permute-start = (f32[64,16,128]{2,1,0:T(8,128)S(1)}, f32[64,16,128]{2,1,0:T(8,128)S(1)}, u32[]{:S(2)}, u32[]{:S(2)}) collective-permute-start(f32[64,16,128]{2,1,0:T(8,128)S(1)} %shard_map.70), channel_id=1, source_target_pairs={{0,8},{8,0},{16,24},{24,16},{32,40},{40,32},{48,56},{56,48},{64,72... | collective-permute-start | bytes 1572872 | tf_op jit(solution)/shard_map/ppermute | solution.py:228
  6.3 10.2 %collective-permute-start.1 = (f32[32,16,128]{2,1,0:T(8,128)S(1)}, f32[32,16,128]{2,1,0:T(8,128)S(1)}, u32[]{:S(2)}, u32[]{:S(2)}) collective-permute-start(f32[32,16,128]{2,1,0:T(8,128)S(1)} %get-tuple-element.21), channel_id=1, source_target_pairs={{8,24},{24,40},{40,56},{56,72},{72,88},{88,104},{104,120},{120,136... | collective-permute-start | bytes 786440 | tf_op jit(solution)/shard_map/ppermute | solution.py:219
  9.9 16.9 %copy-start = (bf16[64,4096]{1,0:T(8,128)(2,1)S(1)}, bf16[64,4096]{1,0:T(8,128)(2,1)}, u32[]{:S(2)}) copy-start(bf16[64,4096]{1,0:T(8,128)(2,1)} %inv_ref.3) | copy-start | bytes 1572868
  9.9 16.9 %copy-start.1 = (f32[16,4096]{1,0:T(8,128)S(1)}, f32[16,4096]{1,0:T(8,128)}, u32[]{:S(2)}) copy-start(f32[16,4096]{1,0:T(8,128)} %start_ref.1) | copy-start | bytes 786436
  9.9 16.9 %copy-start.2 = (f32[16,4096]{1,0:T(8,128)S(1)}, f32[16,4096]{1,0:T(8,128)}, u32[]{:S(2)}) copy-start(f32[16,4096]{1,0:T(8,128)} %right_ref.3) | copy-start | bytes 786436
  10.2 16.6 %collective-permute-start.2 = (f32[32,16,128]{2,1,0:T(8,128)S(1)}, f32[32,16,128]{2,1,0:T(8,128)S(1)}, u32[]{:S(2)}, u32[]{:S(2)}) collective-permute-start(f32[32,16,128]{2,1,0:T(8,128)S(1)} %get-tuple-element.32), channel_id=1, source_target_pairs={{8,16},{24,32},{40,48},{56,64},{72,80},{88,96},{104,112},{120,128}... | collective-permute-start | bytes 786440 | tf_op jit(solution)/shard_map/ppermute | solution.py:237
  29.0 9.1 %collective-permute-start.4 = (f32[32,16,128]{2,1,0:T(8,128)S(1)}, f32[32,16,128]{2,1,0:T(8,128)S(1)}, u32[]{:S(2)}, u32[]{:S(2)}) collective-permute-start(f32[32,16,128]{2,1,0:T(8,128)S(1)} %get-tuple-element.28), channel_id=1, source_target_pairs={{8,24},{24,40},{40,56},{56,72},{72,88},{88,104},{104,120},{120,136... | collective-permute-start | bytes 786440 | tf_op jit(solution)/shard_map/ppermute | solution.py:219
  31.2 3.8 %collective-permute-start.3 = (f32[64,16,128]{2,1,0:T(8,128)S(1)}, f32[64,16,128]{2,1,0:T(8,128)S(1)}, u32[]{:S(2)}, u32[]{:S(2)}) collective-permute-start(f32[64,16,128]{2,1,0:T(8,128)S(1)} %shard_map.73), channel_id=1, source_target_pairs={{0,8},{8,0},{16,24},{24,16},{32,40},{40,32},{48,56},{56,48},{64,72... | collective-permute-start | bytes 1572872 | tf_op jit(solution)/shard_map/ppermute | solution.py:228
  35.0 14.2 %collective-permute-start.5 = (f32[32,16,128]{2,1,0:T(8,128)S(1)}, f32[32,16,128]{2,1,0:T(8,128)S(1)}, u32[]{:S(2)}, u32[]{:S(2)}) collective-permute-start(f32[32,16,128]{2,1,0:T(8,128)S(1)} %get-tuple-element.30), channel_id=1, source_target_pairs={{8,16},{24,32},{40,48},{56,64},{72,80},{88,96},{104,112},{120,128}... | collective-permute-start | bytes 786440 | tf_op jit(solution)/shard_map/ppermute | solution.py:237

commit v6 on v5

--- a/solution.py
+++ b/solution.py
@@ -8,9 +8,9 @@
 DOF = 64
 SLOTS = 7
 QUAD = 4 * DOF
-CHUNKS = 2
+CUTS = (0, 3, 8, 16)
+CHUNKS = len(CUTS) - 1
 WINDOWS = 2
-PIECES = 2
 
 
 def masked_lanes(value, part):
@@ -18,9 +18,12 @@
     return jnp.where(lane // DOF == part, value, jnp.zeros_like(value))
 
 
+def against(left, right):
+    return lax.dot_general(left, right, (((1,), (1,)), ((), ())), preferred_element_type=jnp.float32)
+
+
 def products(vb, panel):
-    spread = jnp.concatenate([masked_lanes(vb, e) for e in range(4)], 0)
-    return lax.dot_general(spread, panel, (((1,), (1,)), ((), ())), preferred_element_type=jnp.float32)
+    return against(jnp.concatenate([masked_lanes(vb, e) for e in range(4)], 0), panel)
 
 
 def scatter(vb_ref, panel_of, cols_ref, device, windows, own_ref, stage_ref):
@@ -30,7 +33,8 @@
     base = (device - 2) * count
 
     def multiply(quad):
-        stage_ref[quad, :, : SLOTS * DOF] = products(vb_ref[:, quad * QUAD : (quad + 1) * QUAD], panel_of(quad))
+        lanes = slice(quad * QUAD, (quad + 1) * QUAD)
+        stage_ref[quad, :, : SLOTS * DOF] = products(vb_ref[:, lanes], panel_of(quad)[:, lanes])
 
     def add(quad):
         stage = stage_ref.at[quad]
@@ -94,23 +98,18 @@
 
 
 def fetch(panel_hbm, panel_ref, sem):
-    span = panel_ref.shape[1] // CHUNKS
-    copies = []
+    copies = {}
     for chunk in range(CHUNKS):
-        lanes = pl.ds(chunk * span, span)
-        copies.append(pltpu.make_async_copy(panel_hbm.at[:, lanes], panel_ref.at[:, lanes], sem.at[chunk]))
-    for copy in copies:
-        copy.start()
+        lanes = pl.ds(CUTS[chunk] * QUAD, (CUTS[chunk + 1] - CUTS[chunk]) * QUAD)
+        copies[CUTS[chunk]] = pltpu.make_async_copy(panel_hbm.at[:, lanes], panel_ref.at[:, lanes], sem.at[chunk])
     return copies
 
 
-def panels(copies, panel_ref, count):
-    per = count // 4 // CHUNKS
-
+def panels(copies, panel_ref):
     def panel_of(quad):
-        if copies and quad % per == 0:
-            copies[quad // per].wait()
-        return panel_ref[:, quad * QUAD : (quad + 1) * QUAD]
+        if quad in copies:
+            copies[quad].wait()
+        return panel_ref
 
     return panel_of
 
@@ -120,14 +119,17 @@
     device = place_ref[0]
     small = pltpu.make_async_copy(cols_hbm, cols_ref, sem.at[CHUNKS])
     begin = pltpu.make_async_copy(start_hbm, start_ref, sem.at[CHUNKS + 1])
+    copies = fetch(panel_hbm, panel_ref, sem)
+    copies[0].start()
     begin.start()
     small.start()
-    copies = fetch(panel_hbm, panel_ref, sem)
+    for cut in CUTS[1:-1]:
+        copies[cut].start()
     clear(windows)
     begin.wait()
     vb_ref[...] = start_ref[...].astype(jnp.bfloat16)
     small.wait()
-    scatter(vb_ref, panels(copies, panel_ref, cols_ref.shape[1]), cols_ref, device, windows, own_ref, stage_ref)
+    scatter(vb_ref, panels(copies, panel_ref), cols_ref, device, windows, own_ref, stage_ref)
     hand_out(device, windows, 0, far_ref)
 
 
@@ -142,7 +144,7 @@
     res = right_ref[:, lanes] - jnp.concatenate(sums, 1)
     resb = res.astype(jnp.bfloat16)
     spread = jnp.concatenate([masked_lanes(resb, e) for e in range(4)], 0)
-    out = lax.dot_general(spread, inv_ref[:, lanes], (((1,), (1,)), ((), ())), preferred_element_type=jnp.float32)
+    out = against(spread, inv_ref[:, lanes])
     width = res.shape[0]
     nothing = jnp.zeros((width, DOF), jnp.float32)
     each = [jnp.concatenate([out[e * width : (e + 1) * width], nothing], 1) for e in range(4)]
@@ -163,26 +165,16 @@
         first_ref[:, lanes] = first
         vb_ref[:, lanes] = first.astype(jnp.bfloat16)
     small.wait()
-    scatter(vb_ref, panels((), panel_ref, count), cols_ref, device, windows, own_ref, stage_ref)
+    scatter(vb_ref, panels({}, panel_ref), cols_ref, device, windows, own_ref, stage_ref)
     hand_out(device, windows, 0, far_ref)
 
 
-def last_kernel(right_ref, first_ref, inv_ref, here_in, mate_in, far_in, near_in, adjoint_hbm, residual_hbm, adjoint_ref, residual_ref, sem):
-    quads = right_ref.shape[1] // QUAD
-    copies = []
-    for quad in range(quads):
+def last_kernel(right_ref, first_ref, inv_ref, here_in, mate_in, far_in, near_in, adjoint_ref, residual_ref):
+    for quad in range(right_ref.shape[1] // QUAD):
         lanes = slice(quad * QUAD, (quad + 1) * QUAD)
         res, adjoint = residual_and_update(quad, right_ref, first_ref, inv_ref, (here_in, mate_in, far_in, near_in))
         residual_ref[:, lanes] = res
         adjoint_ref[:, lanes] = adjoint
-        if (quad + 1) % (quads // PIECES) == 0:
-            piece = quad // (quads // PIECES)
-            done = pl.ds(piece * (quads // PIECES) * QUAD, quads // PIECES * QUAD)
-            for i, (kept, out) in enumerate(((residual_ref, residual_hbm), (adjoint_ref, adjoint_hbm))):
-                copies.append(pltpu.make_async_copy(kept.at[:, done], out.at[:, done], sem.at[i, piece]))
-                copies[-1].start()
-    for copy in copies:
-        copy.wait()
 
 
 VMEM = pl.BlockSpec(memory_space=pltpu.VMEM)
@@ -266,8 +258,7 @@
         last_kernel,
         out_shape=[out, out],
         in_specs=[VMEM] * 7,
-        out_specs=[HBM] * 2,
-        scratch_shapes=[pltpu.VMEM(start.shape, jnp.float32)] * 2 + [pltpu.SemaphoreType.DMA((2, PIECES))],
+        out_specs=[VMEM] * 2,
         compiler_params=PARAMS,
     )(right_side, first, inverse, *parts)
     return (adjoint, residual)

time: 50.6 us -> 50.5 us (level)
  the two profiles are of different devices: /device:TPU:260 before, /device:TPU:258 now
where the time goes in v6:
time: 50.5 us; the launch traced here: 50.2 us
  waiting for transfers between devices  23 us (46%)
  starting transfers between devices  18.7 us (37%)
  Pallas kernels  7.59 us (15%)
  between operations  0.78 us (2%)
    ppermute x2, waiting for transfers between devices, exchange(): near = lax.ppermute(near + mate[half:], 'elem', across)  21.4 us
    ppermute x2, starting transfers between devices, exchange(): near = lax.ppermute(near + mate[half:], 'elem', across)  9.37 us
    ppermute x2, starting transfers between devices, exchange(): far = lax.ppermute(far, 'elem', outward)  5.48 us
    ppermute x2, starting transfers between devices, exchange(): mate = lax.ppermute(mate, 'elem', [(i, i ^ 1) for i in range(size)])  3.84 us
    pallas_call x1, Pallas kernels, body(): pl.pallas_call(first_kernel, out_shape=applied(width, count) + [pltpu.VME...  3.42 us
    pallas_call x1, Pallas kernels, body(): pl.pallas_call(second_kernel, out_shape=applied(width, count) + [out], in...  2.21 us
    ppermute x2, waiting for transfers between devices, exchange(): mate = lax.ppermute(mate, 'elem', [(i, i ^ 1) for i in range(size)])  1.66 us
    pallas_call x1, Pallas kernels, body(): pl.pallas_call(last_kernel, out_shape=[out, out], in_specs=[VMEM] * 7, ou...  1.08 us
  transfers between devices with their start and end apart: 6, of which 3 were waited for; matrix products, arithmetic and copies ran while one was open for 0% of the time, Pallas kernels for 1%

profile of v6, /device:TPU:258, one launch (start us, length us, event | category | flops | bytes accessed | tf_op | source)
XLA Modules:
  0.0 50.2 jit_solution(13430427172506486463)
XLA Ops:
  0.6 3.4 %shard_map.68 = (f32[320,16,128]{2,1,0:T(8,128)S(1)}, f32[320,16,128]{2,1,0:T(8,128)S(1)}, f32[32,16,128]{2,1,0:T(8,128)S(1)}, f32[32,16,128]{2,1,0:T(8,128)S(1)}, bf16[448,4096]{1,0:T(8,128)(2,1)S(1)}) custom-call(s32[1]{0:T(128)} %bitcast.place_ref, s32[6,64]{1,0:T(8,128)} %cols_hbm.3, bf16[448,4096]{1,0:T(8,128)(2,1)} %bitcast.2, f32[16,4096]{1,0:T(8,128)} %start_ref.1), custom_call_target="tpu_custom_call" | custom-call | tf_op jit(solution)/shard_map/pallas_call | solution.py:239
  4.1 0.2 shard_map.70
  4.3 1.9 %collective-permute-start = (f32[64,16,128]{2,1,0:T(8,128)S(1)}, f32[64,16,128]{2,1,0:T(8,128)S(1)}, u32[]{:S(2)}, u32[]{:S(2)}) collective-permute-start(f32[64,16,128]{2,1,0:T(8,128)S(1)} %shard_map.70), channel_id=1, source_target_pairs={{0,8},{8,0},{16,24},{24,16},{32,40},{40,32},{48,56},{56,48},{64,72... | collective-permute-start | bytes 1572872 | tf_op jit(solution)/shard_map/ppermute | solution.py:220
  6.2 3.6 %collective-permute-start.1 = (f32[32,16,128]{2,1,0:T(8,128)S(1)}, f32[32,16,128]{2,1,0:T(8,128)S(1)}, u32[]{:S(2)}, u32[]{:S(2)}) collective-permute-start(f32[32,16,128]{2,1,0:T(8,128)S(1)} %get-tuple-element.21), channel_id=1, source_target_pairs={{8,24},{24,40},{40,56},{56,72},{72,88},{88,104},{104,120},{120,136... | collective-permute-start | bytes 786440 | tf_op jit(solution)/shard_map/ppermute | solution.py:211
  9.8 0.0 copy-start
  9.8 0.0 copy-start.1
  9.8 0.0 copy-start.2
  9.8 0.2 shard_map.69
  10.0 0.0 collective-permute-done
  10.0 0.1 slice_add_fusion.1
  10.1 6.3 %collective-permute-start.2 = (f32[32,16,128]{2,1,0:T(8,128)S(1)}, f32[32,16,128]{2,1,0:T(8,128)S(1)}, u32[]{:S(2)}, u32[]{:S(2)}) collective-permute-start(f32[32,16,128]{2,1,0:T(8,128)S(1)} %get-tuple-element.32), channel_id=1, source_target_pairs={{8,16},{24,32},{40,48},{56,64},{72,80},{88,96},{104,112},{120,128}... | collective-permute-start | bytes 786440 | tf_op jit(solution)/shard_map/ppermute | solution.py:229
  16.4 0.0 collective-permute-done.1.far_in
  16.4 10.2 %collective-permute-done.2.near_in = f32[32,16,128]{2,1,0:T(8,128)S(1)} collective-permute-done((f32[32,16,128]{2,1,0:T(8,128)S(1)}, f32[32,16,128]{2,1,0:T(8,128)S(1)}, u32[]{:S(2)}, u32[]{:S(2)}) %collective-permute-start.2) | collective-permute-done | bytes 262176 | tf_op jit(solution)/shard_map/ppermute | solution.py:229
  26.7 2.2 %shard_map.71 = (f32[320,16,128]{2,1,0:T(8,128)S(1)}, f32[320,16,128]{2,1,0:T(8,128)S(1)}, f32[32,16,128]{2,1,0:T(8,128)S(1)}, f32[32,16,128]{2,1,0:T(8,128)S(1)}, f32[16,4096]{1,0:T(8,128)S(1)}) custom-call(s32[1]{0:T(128)} %bitcast.place_ref, s32[6,64]{1,0:T(8,128)} %cols_hbm.3, bf16[448,4096]{1,0:T(8,128)(2,1)S(1)} %get-tuple-element.16.panel_ref, ...), custom_call_target="tpu_custom_call" | custom-call | tf_op jit(solution)/shard_map/pallas_call | solution.py:248
  28.9 1.9 %collective-permute-start.4 = (f32[32,16,128]{2,1,0:T(8,128)S(1)}, f32[32,16,128]{2,1,0:T(8,128)S(1)}, u32[]{:S(2)}, u32[]{:S(2)}) collective-permute-start(f32[32,16,128]{2,1,0:T(8,128)S(1)} %get-tuple-element.28), channel_id=1, source_target_pairs={{8,24},{24,40},{40,56},{56,72},{72,88},{88,104},{104,120},{120,136... | collective-permute-start | bytes 786440 | tf_op jit(solution)/shard_map/ppermute | solution.py:211
  30.8 0.2 shard_map.73
  31.0 1.9 %collective-permute-start.3 = (f32[64,16,128]{2,1,0:T(8,128)S(1)}, f32[64,16,128]{2,1,0:T(8,128)S(1)}, u32[]{:S(2)}, u32[]{:S(2)}) collective-permute-start(f32[64,16,128]{2,1,0:T(8,128)S(1)} %shard_map.73), channel_id=1, source_target_pairs={{0,8},{8,0},{16,24},{24,16},{32,40},{40,32},{48,56},{56,48},{64,72... | collective-permute-start | bytes 1572872 | tf_op jit(solution)/shard_map/ppermute | solution.py:220
  33.0 0.2 shard_map.72
  33.2 1.7 %collective-permute-done.3 = f32[64,16,128]{2,1,0:T(8,128)S(1)} collective-permute-done((f32[64,16,128]{2,1,0:T(8,128)S(1)}, f32[64,16,128]{2,1,0:T(8,128)S(1)}, u32[]{:S(2)}, u32[]{:S(2)}) %collective-permute-start.3) | collective-permute-done | bytes 524320 | tf_op jit(solution)/shard_map/ppermute | solution.py:220
  34.8 0.1 slice_add_fusion
  34.9 3.0 %collective-permute-start.5 = (f32[32,16,128]{2,1,0:T(8,128)S(1)}, f32[32,16,128]{2,1,0:T(8,128)S(1)}, u32[]{:S(2)}, u32[]{:S(2)}) collective-permute-start(f32[32,16,128]{2,1,0:T(8,128)S(1)} %get-tuple-element.30), channel_id=1, source_target_pairs={{8,16},{24,32},{40,48},{56,64},{72,80},{88,96},{104,112},{120,128}... | collective-permute-start | bytes 786440 | tf_op jit(solution)/shard_map/ppermute | solution.py:229
  38.0 0.0 collective-permute-done.4.far_in
  38.0 11.2 %collective-permute-done.5.near_in = f32[32,16,128]{2,1,0:T(8,128)S(1)} collective-permute-done((f32[32,16,128]{2,1,0:T(8,128)S(1)}, f32[32,16,128]{2,1,0:T(8,128)S(1)}, u32[]{:S(2)}, u32[]{:S(2)}) %collective-permute-start.5) | collective-permute-done | bytes 262176 | tf_op jit(solution)/shard_map/ppermute | solution.py:229
  49.1 1.1 %shard_map.74 = (f32[16,4096]{1,0:T(8,128)}, f32[16,4096]{1,0:T(8,128)}) custom-call(f32[16,4096]{1,0:T(8,128)S(1)} %copy-done.2, f32[16,4096]{1,0:T(8,128)S(1)} %get-tuple-element.23.first_ref, bf16[64,4096]{1,0:T(8,128)(2,1)S(1)} %copy-done, f32[32,16,128]{2,1,0:T(8,128)S(1)} %get-tuple-element.27.here_in, f32[32,16,128]{2,1,0:T(8,128)S(1)} %get-tuple-element.31.mate_in, ...), custom_call_target="tpu_custom_call" | custom-call | tf_op jit(solution)/shard_map/pallas_call | solution.py:257
  (3 shorter events, 0.0 us)
Async XLA Ops:
  4.3 5.8 %collective-permute-start = (f32[64,16,128]{2,1,0:T(8,128)S(1)}, f32[64,16,128]{2,1,0:T(8,128)S(1)}, u32[]{:S(2)}, u32[]{:S(2)}) collective-permute-start(f32[64,16,128]{2,1,0:T(8,128)S(1)} %shard_map.70), channel_id=1, source_target_pairs={{0,8},{8,0},{16,24},{24,16},{32,40},{40,32},{48,56},{56,48},{64,72... | collective-permute-start | bytes 1572872 | tf_op jit(solution)/shard_map/ppermute | solution.py:220
  6.2 10.2 %collective-permute-start.1 = (f32[32,16,128]{2,1,0:T(8,128)S(1)}, f32[32,16,128]{2,1,0:T(8,128)S(1)}, u32[]{:S(2)}, u32[]{:S(2)}) collective-permute-start(f32[32,16,128]{2,1,0:T(8,128)S(1)} %get-tuple-element.21), channel_id=1, source_target_pairs={{8,24},{24,40},{40,56},{56,72},{72,88},{88,104},{104,120},{120,136... | collective-permute-start | bytes 786440 | tf_op jit(solution)/shard_map/ppermute | solution.py:211
  9.8 16.9 %copy-start = (bf16[64,4096]{1,0:T(8,128)(2,1)S(1)}, bf16[64,4096]{1,0:T(8,128)(2,1)}, u32[]{:S(2)}) copy-start(bf16[64,4096]{1,0:T(8,128)(2,1)} %inv_ref.3) | copy-start | bytes 1572868
  9.8 16.9 %copy-start.1 = (f32[16,4096]{1,0:T(8,128)S(1)}, f32[16,4096]{1,0:T(8,128)}, u32[]{:S(2)}) copy-start(f32[16,4096]{1,0:T(8,128)} %start_ref.1) | copy-start | bytes 786436
  9.8 16.9 %copy-start.2 = (f32[16,4096]{1,0:T(8,128)S(1)}, f32[16,4096]{1,0:T(8,128)}, u32[]{:S(2)}) copy-start(f32[16,4096]{1,0:T(8,128)} %right_ref.3) | copy-start | bytes 786436
  10.1 16.5 %collective-permute-start.2 = (f32[32,16,128]{2,1,0:T(8,128)S(1)}, f32[32,16,128]{2,1,0:T(8,128)S(1)}, u32[]{:S(2)}, u32[]{:S(2)}) collective-permute-start(f32[32,16,128]{2,1,0:T(8,128)S(1)} %get-tuple-element.32), channel_id=1, source_target_pairs={{8,16},{24,32},{40,48},{56,64},{72,80},{88,96},{104,112},{120,128}... | collective-permute-start | bytes 786440 | tf_op jit(solution)/shard_map/ppermute | solution.py:229
  28.9 9.1 %collective-permute-start.4 = (f32[32,16,128]{2,1,0:T(8,128)S(1)}, f32[32,16,128]{2,1,0:T(8,128)S(1)}, u32[]{:S(2)}, u32[]{:S(2)}) collective-permute-start(f32[32,16,128]{2,1,0:T(8,128)S(1)} %get-tuple-element.28), channel_id=1, source_target_pairs={{8,24},{24,40},{40,56},{56,72},{72,88},{88,104},{104,120},{120,136... | collective-permute-start | bytes 786440 | tf_op jit(solution)/shard_map/ppermute | solution.py:211
  31.0 3.8 %collective-permute-start.3 = (f32[64,16,128]{2,1,0:T(8,128)S(1)}, f32[64,16,128]{2,1,0:T(8,128)S(1)}, u32[]{:S(2)}, u32[]{:S(2)}) collective-permute-start(f32[64,16,128]{2,1,0:T(8,128)S(1)} %shard_map.73), channel_id=1, source_target_pairs={{0,8},{8,0},{16,24},{24,16},{32,40},{40,32},{48,56},{56,48},{64,72... | collective-permute-start | bytes 1572872 | tf_op jit(solution)/shard_map/ppermute | solution.py:220
  34.9 14.2 %collective-permute-start.5 = (f32[32,16,128]{2,1,0:T(8,128)S(1)}, f32[32,16,128]{2,1,0:T(8,128)S(1)}, u32[]{:S(2)}, u32[]{:S(2)}) collective-permute-start(f32[32,16,128]{2,1,0:T(8,128)S(1)} %get-tuple-element.30), channel_id=1, source_target_pairs={{8,16},{24,32},{40,48},{56,64},{72,80},{88,96},{104,112},{120,128}... | collective-permute-start | bytes 786440 | tf_op jit(solution)/shard_map/ppermute | solution.py:229

commit v7 on v6

--- a/solution.py
+++ b/solution.py
@@ -50,21 +50,14 @@
                         own_ref[2 * quad + e // 2] = jnp.where(low, kept, pltpu.roll(tile, DOF, 1))
                 else:
                     place = cols_ref[2 * pair - 1, 4 * quad + e] - base
-                    windows[0][place] += jnp.where(low, tile, 0.0)
+                    windows[0][place] += tile
                 if pair < 3:
                     place = cols_ref[2 * pair, 4 * quad + e] - base
-                    windows[1][place] += jnp.where(low, 0.0, tile)
+                    windows[1][place] += tile
 
     for quad in range(count // 4):
         multiply(quad)
         add(quad)
-
-
-def sum_of(windows, place):
-    total = windows[0][place]
-    for window in windows[1:]:
-        total = total + window[place]
-    return total
 
 
 def clear(windows):
@@ -78,9 +71,10 @@
     core = lax.rem(device, 2)
     first = (core * (4 - role) + (1 - core) * role) * 2 * half
     for pair in range(half):
-        even = sum_of(windows, first + 2 * pair)
-        odd = sum_of(windows, first + 2 * pair + 1)
-        total = jnp.where(low, even, odd) + pltpu.roll(jnp.where(low, odd, even), DOF, 1)
+        here, next_one = first + 2 * pair, first + 2 * pair + 1
+        kept = jnp.where(low, windows[0][here], windows[1][next_one])
+        crossed = jnp.where(low, windows[0][next_one], windows[1][here])
+        total = kept + pltpu.roll(crossed, DOF, 1)
         out[at + pair] = total if more is None else total + more[pair]
 
 
@@ -89,6 +83,13 @@
     half = mate_ref.shape[0] // 2
     hand_out(place_ref[0], windows, 3, mate_ref)
     hand_out(place_ref[0], windows, 4, mate_ref, half)
+
+
+def clearing_kernel(place_ref, *refs):
+    (own_ref, near_ref, here_ref), windows = refs[WINDOWS : WINDOWS + 3], refs[WINDOWS + 3 :]
+    hand_out(place_ref[0], windows, 1, near_ref)
+    hand_out(place_ref[0], windows, 2, here_ref, 0, own_ref)
+    clear(windows)
 
 
 def rest_kernel(place_ref, *refs):
@@ -115,7 +116,7 @@
 
 
 def first_kernel(place_ref, cols_hbm, panel_hbm, start_hbm, *refs):
-    windows, (own_ref, far_ref, panel_ref, cols_ref, start_ref, vb_ref, stage_ref, sem) = refs[:WINDOWS], refs[WINDOWS:]
+    windows, (own_ref, far_ref, mate_ref, panel_ref, cols_ref, start_ref, vb_ref, stage_ref, sem) = refs[:WINDOWS], refs[WINDOWS:]
     device = place_ref[0]
     small = pltpu.make_async_copy(cols_hbm, cols_ref, sem.at[CHUNKS])
     begin = pltpu.make_async_copy(start_hbm, start_ref, sem.at[CHUNKS + 1])
@@ -131,6 +132,8 @@
     small.wait()
     scatter(vb_ref, panels(copies, panel_ref), cols_ref, device, windows, own_ref, stage_ref)
     hand_out(device, windows, 0, far_ref)
+    hand_out(device, windows, 3, mate_ref)
+    hand_out(device, windows, 4, mate_ref, mate_ref.shape[0] // 2)
 
 
 def residual_and_update(quad, right_ref, from_ref, inv_ref, parts):
@@ -153,12 +156,12 @@
 
 
 def second_kernel(place_ref, cols_hbm, panel_ref, right_ref, start_ref, inv_ref, here_in, mate_in, far_in, near_in, *refs):
+    refs = refs[WINDOWS:]
     windows, (own_ref, far_ref, first_ref, cols_ref, vb_ref, stage_ref, sem) = refs[:WINDOWS], refs[WINDOWS:]
     device = place_ref[0]
     count = cols_ref.shape[1]
     small = pltpu.make_async_copy(cols_hbm, cols_ref, sem.at[CHUNKS])
     small.start()
-    clear(windows)
     for quad in range(count // 4):
         _, first = residual_and_update(quad, right_ref, start_ref, inv_ref, (here_in, mate_in, far_in, near_in))
         lanes = slice(quad * QUAD, (quad + 1) * QUAD)
@@ -201,33 +204,37 @@
     return pltpu.with_memory_space_constraint(value, pltpu.HBM)
 
 
-def exchange(place, windows, own, far, hint):
+def mate_slabs(place, windows, own):
+    half, width, lanes = own.shape
+    return pl.pallas_call(
+        mate_kernel,
+        out_shape=jax.ShapeDtypeStruct((2 * half, width, lanes), jnp.float32),
+        in_specs=[SMEM] + [VMEM] * WINDOWS,
+        out_specs=VMEM,
+        compiler_params=PARAMS,
+        cost_estimate=pl.CostEstimate(flops=10**8, bytes_accessed=4 * 10**6, transcendentals=0),
+    )(place, *windows)
+
+
+def exchange(place, windows, own, far, mate, hint, again):
     size = lax.axis_size("elem")
-    half, width, lanes = own.shape
+    half = own.shape[0]
     slab = jax.ShapeDtypeStruct(own.shape, jnp.float32)
-    double = jax.ShapeDtypeStruct((2 * half, width, lanes), jnp.float32)
     outward = [(i, i + 2) for i in range(1, size - 2, 2)] + [(i, i - 2) for i in range(2, size, 2)]
     across = [(i, i + 1) for i in range(1, size - 1, 2)] + [(i + 1, i) for i in range(1, size - 1, 2)]
     far = lax.ppermute(far, "elem", outward)
-    mate = pl.pallas_call(
-        mate_kernel,
-        out_shape=double,
-        in_specs=[SMEM] + [VMEM] * WINDOWS,
-        out_specs=VMEM,
-        compiler_params=PARAMS,
-        cost_estimate=pl.CostEstimate(flops=10**8, bytes_accessed=4 * 10**6, transcendentals=0),
-    )(place, *windows)
     mate = lax.ppermute(mate, "elem", [(i, i ^ 1) for i in range(size)])
-    near, here = pl.pallas_call(
-        rest_kernel,
-        out_shape=[slab, slab],
+    near, here, *windows = pl.pallas_call(
+        clearing_kernel if again else rest_kernel,
+        out_shape=[slab, slab] + [jax.ShapeDtypeStruct(w.shape, w.dtype) for w in windows if again],
         in_specs=[SMEM] + [VMEM] * (WINDOWS + 1),
-        out_specs=[VMEM, VMEM],
+        out_specs=[VMEM] * (2 + WINDOWS * again),
+        input_output_aliases={1 + i: 2 + i for i in range(WINDOWS * again)},
         compiler_params=PARAMS,
         cost_estimate=pl.CostEstimate(flops=hint, bytes_accessed=4 * 10**6, transcendentals=0),
     )(place, *windows, own)
     near = lax.ppermute(near + mate[half:], "elem", across)
-    return here, mate[:half], far, near
+    return (here, mate[:half], far, near), windows
 
 
 def body(blocks, cols, inverse, right_side, start):
@@ -235,25 +242,27 @@
     count = cols.shape[1]
     place = lax.axis_index("elem").astype(jnp.int32).reshape(1)
     out = jax.ShapeDtypeStruct(start.shape, jnp.float32)
+    double = jax.ShapeDtypeStruct((count, width, 2 * DOF), jnp.float32)
     cols = in_hbm(cols)
-    *windows, own, far, panel = pl.pallas_call(
+    *windows, own, far, mate, panel = pl.pallas_call(
         first_kernel,
-        out_shape=applied(width, count) + [pltpu.VMEM(blocks.shape[::-1], jnp.bfloat16)],
+        out_shape=applied(width, count) + [double, pltpu.VMEM(blocks.shape[::-1], jnp.bfloat16)],
         in_specs=[SMEM, HBM, HBM, HBM],
-        out_specs=[VMEM] * (WINDOWS + 3),
+        out_specs=[VMEM] * (WINDOWS + 4),
         scratch_shapes=[pltpu.SMEM(cols.shape, jnp.int32), pltpu.VMEM(start.shape, jnp.float32)] + scratch(width, count),
         compiler_params=PARAMS,
     )(place, cols, in_hbm(blocks.T), in_hbm(start))
-    parts = exchange(place, windows, own, far, 10**8)
+    parts, windows = exchange(place, windows, own, far, mate, 10**8, True)
     *windows, own, far, first = pl.pallas_call(
         second_kernel,
         out_shape=applied(width, count) + [out],
-        in_specs=[SMEM, HBM] + [VMEM] * 8,
+        in_specs=[SMEM, HBM] + [VMEM] * (8 + WINDOWS),
+        input_output_aliases={10 + i: i for i in range(WINDOWS)},
         out_specs=[VMEM] * (WINDOWS + 3),
         scratch_shapes=[pltpu.SMEM(cols.shape, jnp.int32)] + scratch(width, count),
         compiler_params=PARAMS,
-    )(place, cols, panel, right_side, start, inverse, *parts)
-    parts = exchange(place, windows, own, far, 10**10)
+    )(place, cols, panel, right_side, start, inverse, *parts, *windows)
+    parts, _ = exchange(place, windows, own, far, mate_slabs(place, windows, own), 10**10, False)
     adjoint, residual = pl.pallas_call(
         last_kernel,
         out_shape=[out, out],

time: 50.5 us -> 50.7 us (level)
  the two profiles are of different devices: /device:TPU:258 before, /device:TPU:249 now
where the time goes in v7:
time: 50.7 us; the launch traced here: 50.4 us
  starting transfers between devices  21.4 us (42%)
  waiting for transfers between devices  20.2 us (40%)
  Pallas kernels  7.9 us (16%)
  between operations  0.78 us (2%)
    ppermute x2, waiting for transfers between devices, exchange(): near = lax.ppermute(near + mate[half:], 'elem', across)  18.6 us
    ppermute x2, starting transfers between devices, exchange(): near = lax.ppermute(near + mate[half:], 'elem', across)  9.67 us
    ppermute x2, starting transfers between devices, exchange(): far = lax.ppermute(far, 'elem', outward)  7.24 us
    ppermute x2, starting transfers between devices, exchange(): mate = lax.ppermute(mate, 'elem', [(i, i ^ 1) for i in range(size)])  4.51 us
    pallas_call x1, Pallas kernels, body(): pl.pallas_call(first_kernel, out_shape=applied(width, count) + [double, p...  3.55 us
    pallas_call x1, Pallas kernels, body(): pl.pallas_call(second_kernel, out_shape=applied(width, count) + [out], in...  2.2 us
    ppermute x2, waiting for transfers between devices, exchange(): mate = lax.ppermute(mate, 'elem', [(i, i ^ 1) for i in range(size)])  1.66 us
    pallas_call x1, Pallas kernels, body(): pl.pallas_call(last_kernel, out_shape=[out, out], in_specs=[VMEM] * 7, ou...  1.08 us
  transfers between devices with their start and end apart: 6, of which 3 were waited for; matrix products, arithmetic and copies ran while one was open for 0% of the time, Pallas kernels for 2%

profile of v7, /device:TPU:249, one launch (start us, length us, event | category | flops | bytes accessed | tf_op | source)
XLA Modules:
  0.0 50.4 jit_solution(4279439943075381785)
XLA Ops:
  0.6 3.5 %shard_map.68 = (f32[320,16,128]{2,1,0:T(8,128)S(1)}, f32[320,16,128]{2,1,0:T(8,128)S(1)}, f32[32,16,128]{2,1,0:T(8,128)S(1)}, f32[32,16,128]{2,1,0:T(8,128)S(1)...) custom-call(s32[1]{0:T(128)} %bitcast.place_ref, s32[6,64]{1,0:T(8,128)} %cols_hbm.3, ...), custom_call_target="tpu_custom_call" | custom-call | tf_op jit(solution)/shard_map/pallas_call | solution.py:247
  4.2 2.6 %collective-permute-start = (f32[64,16,128]{2,1,0:T(8,128)S(1)}, f32[64,16,128]{2,1,0:T(8,128)S(1)}, u32[]{:S(2)}, u32[]{:S(2)}) collective-permute-start(f32[64,16,128]{2,1,0:T(8,128)S(1)} %get-tuple-element.24), channel_id=1, source_target_pairs={{0,8},{8,0},{16,24},{24,16},{32,40},{40,32},{48,56},{56,48},{64,72... | collective-permute-start | bytes 1572872 | tf_op jit(solution)/shard_map/ppermute | solution.py:226
  6.8 5.3 %collective-permute-start.1 = (f32[32,16,128]{2,1,0:T(8,128)S(1)}, f32[32,16,128]{2,1,0:T(8,128)S(1)}, u32[]{:S(2)}, u32[]{:S(2)}) collective-permute-start(f32[32,16,128]{2,1,0:T(8,128)S(1)} %get-tuple-element.25), channel_id=1, source_target_pairs={{8,24},{24,40},{40,56},{56,72},{72,88},{88,104},{104,120},{120,136... | collective-permute-start | bytes 786440 | tf_op jit(solution)/shard_map/ppermute | solution.py:225
  12.1 0.0 copy-start
  12.1 0.0 copy-start.1
  12.1 0.0 copy-start.2
  12.2 0.6 %shard_map.69 = (f32[32,16,128]{2,1,0:T(8,128)S(1)}, f32[32,16,128]{2,1,0:T(8,128)S(1)}, f32[320,16,128]{2,1,0:T(8,128)S(1)}, f32[320,16,128]{2,1,0:T(8,128)S(1)}) custom-call(s32[1]{0:T(128)} %bitcast.place_ref, f32[320,16,128]{2,1,0:T(8,128)S(1)} %get-tuple-element.20.refs_0_, ...), custom_call_target="tpu_custom_call", output_to_operand_aliasing={{2}: (1, {}), {3}: (2, {})} | custom-call | flops 100000000 | bytes 4000000 | tf_op jit(solution)/shard_map/pallas_call | solution.py:227
  12.8 0.0 collective-permute-done
  12.8 0.1 slice_add_fusion.1
  12.9 4.4 %collective-permute-start.2 = (f32[32,16,128]{2,1,0:T(8,128)S(1)}, f32[32,16,128]{2,1,0:T(8,128)S(1)}, u32[]{:S(2)}, u32[]{:S(2)}) collective-permute-start(f32[32,16,128]{2,1,0:T(8,128)S(1)} %get-tuple-element.38), channel_id=1, source_target_pairs={{8,16},{24,32},{40,48},{56,64},{72,80},{88,96},{104,112},{120,128}... | collective-permute-start | bytes 786440 | tf_op jit(solution)/shard_map/ppermute | solution.py:236
  17.2 0.0 collective-permute-done.1.far_in
  17.3 9.5 %collective-permute-done.2.near_in = f32[32,16,128]{2,1,0:T(8,128)S(1)} collective-permute-done((f32[32,16,128]{2,1,0:T(8,128)S(1)}, f32[32,16,128]{2,1,0:T(8,128)S(1)}, u32[]{:S(2)}, u32[]{:S(2)}) %collective-permute-start.2) | collective-permute-done | bytes 262176 | tf_op jit(solution)/shard_map/ppermute | solution.py:236
  26.7 0.0 copy-done
  26.7 2.2 %shard_map.70 = (f32[320,16,128]{2,1,0:T(8,128)S(1)}, f32[320,16,128]{2,1,0:T(8,128)S(1)}, f32[32,16,128]{2,1,0:T(8,128)S(1)}, f32[32,16,128]{2,1,0:T(8,128)S(1)}, f32[16,4096]{1,0:T(8,128)S(1)}) custom-call(s32[1]{0:T(128)} %bitcast.place_ref, s32[6,64]{1,0:T(8,128)} %cols_hbm.3, ...), custom_call_target="tpu_custom_call", output_to_operand_aliasing={{0}: (10, {}), {1}: (11, {})} | custom-call | tf_op jit(solution)/shard_map/pallas_call | solution.py:256
  29.0 1.9 %collective-permute-start.4 = (f32[32,16,128]{2,1,0:T(8,128)S(1)}, f32[32,16,128]{2,1,0:T(8,128)S(1)}, u32[]{:S(2)}, u32[]{:S(2)}) collective-permute-start(f32[32,16,128]{2,1,0:T(8,128)S(1)} %get-tuple-element.34), channel_id=1, source_target_pairs={{8,24},{24,40},{40,56},{56,72},{72,88},{88,104},{104,120},{120,136... | collective-permute-start | bytes 786440 | tf_op jit(solution)/shard_map/ppermute | solution.py:225
  30.9 0.2 shard_map.72
  31.1 1.9 %collective-permute-start.3 = (f32[64,16,128]{2,1,0:T(8,128)S(1)}, f32[64,16,128]{2,1,0:T(8,128)S(1)}, u32[]{:S(2)}, u32[]{:S(2)}) collective-permute-start(f32[64,16,128]{2,1,0:T(8,128)S(1)} %shard_map.72), channel_id=1, source_target_pairs={{0,8},{8,0},{16,24},{24,16},{32,40},{40,32},{48,56},{56,48},{64,72... | collective-permute-start | bytes 1572872 | tf_op jit(solution)/shard_map/ppermute | solution.py:226
  33.0 0.2 shard_map.71
  33.2 1.7 %collective-permute-done.3 = f32[64,16,128]{2,1,0:T(8,128)S(1)} collective-permute-done((f32[64,16,128]{2,1,0:T(8,128)S(1)}, f32[64,16,128]{2,1,0:T(8,128)S(1)}, u32[]{:S(2)}, u32[]{:S(2)}) %collective-permute-start.3) | collective-permute-done | bytes 524320 | tf_op jit(solution)/shard_map/ppermute | solution.py:226
  34.9 0.1 slice_add_fusion
  35.0 5.3 %collective-permute-start.5 = (f32[32,16,128]{2,1,0:T(8,128)S(1)}, f32[32,16,128]{2,1,0:T(8,128)S(1)}, u32[]{:S(2)}, u32[]{:S(2)}) collective-permute-start(f32[32,16,128]{2,1,0:T(8,128)S(1)} %get-tuple-element.36), channel_id=1, source_target_pairs={{8,16},{24,32},{40,48},{56,64},{72,80},{88,96},{104,112},{120,128}... | collective-permute-start | bytes 786440 | tf_op jit(solution)/shard_map/ppermute | solution.py:236
  40.3 0.0 collective-permute-done.4.far_in
  40.3 9.1 %collective-permute-done.5.near_in = f32[32,16,128]{2,1,0:T(8,128)S(1)} collective-permute-done((f32[32,16,128]{2,1,0:T(8,128)S(1)}, f32[32,16,128]{2,1,0:T(8,128)S(1)}, u32[]{:S(2)}, u32[]{:S(2)}) %collective-permute-start.5) | collective-permute-done | bytes 262176 | tf_op jit(solution)/shard_map/ppermute | solution.py:236
  49.4 1.1 %shard_map.73 = (f32[16,4096]{1,0:T(8,128)}, f32[16,4096]{1,0:T(8,128)}) custom-call(f32[16,4096]{1,0:T(8,128)S(1)} %copy-done.2, f32[16,4096]{1,0:T(8,128)S(1)} %get-tuple-element.29.first_ref, bf16[64,4096]{1,0:T(8,128)(2,1)S(1)} %copy-done, f32[32,16,128]{2,1,0:T(8,128)S(1)} %get-tuple-element.33.here_in, f32[32,16,128]{2,1,0:T(8,128)S(1)} %get-tuple-element.37.mate_in, ...), custom_call_target="tpu_custom_call" | custom-call | tf_op jit(solution)/shard_map/pallas_call | solution.py:266
  (2 shorter events, 0.0 us)
Async XLA Ops:
  4.2 8.6 %collective-permute-start = (f32[64,16,128]{2,1,0:T(8,128)S(1)}, f32[64,16,128]{2,1,0:T(8,128)S(1)}, u32[]{:S(2)}, u32[]{:S(2)}) collective-permute-start(f32[64,16,128]{2,1,0:T(8,128)S(1)} %get-tuple-element.24), channel_id=1, source_target_pairs={{0,8},{8,0},{16,24},{24,16},{32,40},{40,32},{48,56},{56,48},{64,72... | collective-permute-start | bytes 1572872 | tf_op jit(solution)/shard_map/ppermute | solution.py:226
  6.8 10.5 %collective-permute-start.1 = (f32[32,16,128]{2,1,0:T(8,128)S(1)}, f32[32,16,128]{2,1,0:T(8,128)S(1)}, u32[]{:S(2)}, u32[]{:S(2)}) collective-permute-start(f32[32,16,128]{2,1,0:T(8,128)S(1)} %get-tuple-element.25), channel_id=1, source_target_pairs={{8,24},{24,40},{40,56},{56,72},{72,88},{88,104},{104,120},{120,136... | collective-permute-start | bytes 786440 | tf_op jit(solution)/shard_map/ppermute | solution.py:225
  12.1 14.6 %copy-start = (bf16[64,4096]{1,0:T(8,128)(2,1)S(1)}, bf16[64,4096]{1,0:T(8,128)(2,1)}, u32[]{:S(2)}) copy-start(bf16[64,4096]{1,0:T(8,128)(2,1)} %inv_ref.3) | copy-start | bytes 1572868
  12.1 14.6 %copy-start.1 = (f32[16,4096]{1,0:T(8,128)S(1)}, f32[16,4096]{1,0:T(8,128)}, u32[]{:S(2)}) copy-start(f32[16,4096]{1,0:T(8,128)} %start_ref.1) | copy-start | bytes 786436
  12.1 14.6 %copy-start.2 = (f32[16,4096]{1,0:T(8,128)S(1)}, f32[16,4096]{1,0:T(8,128)}, u32[]{:S(2)}) copy-start(f32[16,4096]{1,0:T(8,128)} %right_ref.3) | copy-start | bytes 786436
  12.9 13.9 %collective-permute-start.2 = (f32[32,16,128]{2,1,0:T(8,128)S(1)}, f32[32,16,128]{2,1,0:T(8,128)S(1)}, u32[]{:S(2)}, u32[]{:S(2)}) collective-permute-start(f32[32,16,128]{2,1,0:T(8,128)S(1)} %get-tuple-element.38), channel_id=1, source_target_pairs={{8,16},{24,32},{40,48},{56,64},{72,80},{88,96},{104,112},{120,128}... | collective-permute-start | bytes 786440 | tf_op jit(solution)/shard_map/ppermute | solution.py:236
  29.0 11.3 %collective-permute-start.4 = (f32[32,16,128]{2,1,0:T(8,128)S(1)}, f32[32,16,128]{2,1,0:T(8,128)S(1)}, u32[]{:S(2)}, u32[]{:S(2)}) collective-permute-start(f32[32,16,128]{2,1,0:T(8,128)S(1)} %get-tuple-element.34), channel_id=1, source_target_pairs={{8,24},{24,40},{40,56},{56,72},{72,88},{88,104},{104,120},{120,136... | collective-permute-start | bytes 786440 | tf_op jit(solution)/shard_map/ppermute | solution.py:225
  31.1 3.8 %collective-permute-start.3 = (f32[64,16,128]{2,1,0:T(8,128)S(1)}, f32[64,16,128]{2,1,0:T(8,128)S(1)}, u32[]{:S(2)}, u32[]{:S(2)}) collective-permute-start(f32[64,16,128]{2,1,0:T(8,128)S(1)} %shard_map.72), channel_id=1, source_target_pairs={{0,8},{8,0},{16,24},{24,16},{32,40},{40,32},{48,56},{56,48},{64,72... | collective-permute-start | bytes 1572872 | tf_op jit(solution)/shard_map/ppermute | solution.py:226
  35.0 14.4 %collective-permute-start.5 = (f32[32,16,128]{2,1,0:T(8,128)S(1)}, f32[32,16,128]{2,1,0:T(8,128)S(1)}, u32[]{:S(2)}, u32[]{:S(2)}) collective-permute-start(f32[32,16,128]{2,1,0:T(8,128)S(1)} %get-tuple-element.36), channel_id=1, source_target_pairs={{8,16},{24,32},{40,48},{56,64},{72,80},{88,96},{104,112},{120,128}... | collective-permute-start | bytes 786440 | tf_op jit(solution)/shard_map/ppermute | solution.py:236

commit v8 on v7

--- a/solution.py
+++ b/solution.py
@@ -85,11 +85,10 @@
     hand_out(place_ref[0], windows, 4, mate_ref, half)
 
 
-def clearing_kernel(place_ref, *refs):
-    (own_ref, near_ref, here_ref), windows = refs[WINDOWS : WINDOWS + 3], refs[WINDOWS + 3 :]
-    hand_out(place_ref[0], windows, 1, near_ref)
+def here_kernel(place_ref, *refs):
+    windows, (own_ref, far_in, here_ref) = refs[:WINDOWS], refs[WINDOWS:]
     hand_out(place_ref[0], windows, 2, here_ref, 0, own_ref)
-    clear(windows)
+    here_ref[...] += far_in[...]
 
 
 def rest_kernel(place_ref, *refs):
@@ -116,7 +115,7 @@
 
 
 def first_kernel(place_ref, cols_hbm, panel_hbm, start_hbm, *refs):
-    windows, (own_ref, far_ref, mate_ref, panel_ref, cols_ref, start_ref, vb_ref, stage_ref, sem) = refs[:WINDOWS], refs[WINDOWS:]
+    windows, (own_ref, far_ref, mate_ref, near_ref, panel_ref, cols_ref, start_ref, vb_ref, stage_ref, sem) = refs[:WINDOWS], refs[WINDOWS:]
     device = place_ref[0]
     small = pltpu.make_async_copy(cols_hbm, cols_ref, sem.at[CHUNKS])
     begin = pltpu.make_async_copy(start_hbm, start_ref, sem.at[CHUNKS + 1])
@@ -134,6 +133,7 @@
     hand_out(device, windows, 0, far_ref)
     hand_out(device, windows, 3, mate_ref)
     hand_out(device, windows, 4, mate_ref, mate_ref.shape[0] // 2)
+    hand_out(device, windows, 1, near_ref)
 
 
 def residual_and_update(quad, right_ref, from_ref, inv_ref, parts):
@@ -155,15 +155,15 @@
     return res, from_ref[:, lanes] + update
 
 
-def second_kernel(place_ref, cols_hbm, panel_ref, right_ref, start_ref, inv_ref, here_in, mate_in, far_in, near_in, *refs):
-    refs = refs[WINDOWS:]
+def second_kernel(place_ref, cols_hbm, panel_ref, right_ref, start_ref, inv_ref, here_in, mate_in, near_in, *refs):
     windows, (own_ref, far_ref, first_ref, cols_ref, vb_ref, stage_ref, sem) = refs[:WINDOWS], refs[WINDOWS:]
     device = place_ref[0]
     count = cols_ref.shape[1]
     small = pltpu.make_async_copy(cols_hbm, cols_ref, sem.at[CHUNKS])
     small.start()
+    clear(windows)
     for quad in range(count // 4):
-        _, first = residual_and_update(quad, right_ref, start_ref, inv_ref, (here_in, mate_in, far_in, near_in))
+        _, first = residual_and_update(quad, right_ref, start_ref, inv_ref, (here_in, mate_in, near_in))
         lanes = slice(quad * QUAD, (quad + 1) * QUAD)
         first_ref[:, lanes] = first
         vb_ref[:, lanes] = first.astype(jnp.bfloat16)
@@ -216,25 +216,42 @@
     )(place, *windows)
 
 
-def exchange(place, windows, own, far, mate, hint, again):
-    size = lax.axis_size("elem")
-    half = own.shape[0]
-    slab = jax.ShapeDtypeStruct(own.shape, jnp.float32)
+def pairs(size):
     outward = [(i, i + 2) for i in range(1, size - 2, 2)] + [(i, i - 2) for i in range(2, size, 2)]
     across = [(i, i + 1) for i in range(1, size - 1, 2)] + [(i + 1, i) for i in range(1, size - 1, 2)]
+    return outward, [(i, i ^ 1) for i in range(size)], across
+
+
+def slab_call(kernel, place, operands, outs, hint):
+    slab = jax.ShapeDtypeStruct(operands[WINDOWS].shape, jnp.float32)
+    return pl.pallas_call(
+        kernel,
+        out_shape=[slab] * outs,
+        in_specs=[SMEM] + [VMEM] * len(operands),
+        out_specs=[VMEM] * outs,
+        compiler_params=PARAMS,
+        cost_estimate=pl.CostEstimate(flops=hint, bytes_accessed=4 * 10**6, transcendentals=0),
+    )(place, *operands)
+
+
+def first_exchange(place, windows, own, far, mate, near):
+    outward, swapped, across = pairs(lax.axis_size("elem"))
+    half = own.shape[0]
     far = lax.ppermute(far, "elem", outward)
-    mate = lax.ppermute(mate, "elem", [(i, i ^ 1) for i in range(size)])
-    near, here, *windows = pl.pallas_call(
-        clearing_kernel if again else rest_kernel,
-        out_shape=[slab, slab] + [jax.ShapeDtypeStruct(w.shape, w.dtype) for w in windows if again],
-        in_specs=[SMEM] + [VMEM] * (WINDOWS + 1),
-        out_specs=[VMEM] * (2 + WINDOWS * again),
-        input_output_aliases={1 + i: 2 + i for i in range(WINDOWS * again)},
-        compiler_params=PARAMS,
-        cost_estimate=pl.CostEstimate(flops=hint, bytes_accessed=4 * 10**6, transcendentals=0),
-    )(place, *windows, own)
+    mate = lax.ppermute(mate, "elem", swapped)
     near = lax.ppermute(near + mate[half:], "elem", across)
-    return (here, mate[:half], far, near), windows
+    (here,) = slab_call(here_kernel, place, (*windows, own, far), 1, 10**8)
+    return here, mate[:half], near
+
+
+def second_exchange(place, windows, own, far):
+    outward, swapped, across = pairs(lax.axis_size("elem"))
+    half = own.shape[0]
+    far = lax.ppermute(far, "elem", outward)
+    mate = lax.ppermute(mate_slabs(place, windows, own), "elem", swapped)
+    near, here = slab_call(rest_kernel, place, (*windows, own), 2, 10**10)
+    near = lax.ppermute(near + mate[half:], "elem", across)
+    return here, mate[:half], far, near
 
 
 def body(blocks, cols, inverse, right_side, start):
@@ -243,26 +260,26 @@
     place = lax.axis_index("elem").astype(jnp.int32).reshape(1)
     out = jax.ShapeDtypeStruct(start.shape, jnp.float32)
     double = jax.ShapeDtypeStruct((count, width, 2 * DOF), jnp.float32)
+    slab = jax.ShapeDtypeStruct((count // 2, width, 2 * DOF), jnp.float32)
     cols = in_hbm(cols)
-    *windows, own, far, mate, panel = pl.pallas_call(
+    *windows, own, far, mate, near, panel = pl.pallas_call(
         first_kernel,
-        out_shape=applied(width, count) + [double, pltpu.VMEM(blocks.shape[::-1], jnp.bfloat16)],
+        out_shape=applied(width, count) + [double, slab, pltpu.VMEM(blocks.shape[::-1], jnp.bfloat16)],
         in_specs=[SMEM, HBM, HBM, HBM],
-        out_specs=[VMEM] * (WINDOWS + 4),
+        out_specs=[VMEM] * (WINDOWS + 5),
         scratch_shapes=[pltpu.SMEM(cols.shape, jnp.int32), pltpu.VMEM(start.shape, jnp.float32)] + scratch(width, count),
         compiler_params=PARAMS,
     )(place, cols, in_hbm(blocks.T), in_hbm(start))
-    parts, windows = exchange(place, windows, own, far, mate, 10**8, True)
+    parts = first_exchange(place, windows, own, far, mate, near)
     *windows, own, far, first = pl.pallas_call(
         second_kernel,
         out_shape=applied(width, count) + [out],
-        in_specs=[SMEM, HBM] + [VMEM] * (8 + WINDOWS),
-        input_output_aliases={10 + i: i for i in range(WINDOWS)},
+        in_specs=[SMEM, HBM] + [VMEM] * 7,
         out_specs=[VMEM] * (WINDOWS + 3),
         scratch_shapes=[pltpu.SMEM(cols.shape, jnp.int32)] + scratch(width, count),
         compiler_params=PARAMS,
-    )(place, cols, panel, right_side, start, inverse, *parts, *windows)
-    parts, _ = exchange(place, windows, own, far, mate_slabs(place, windows, own), 10**10, False)
+    )(place, cols, panel, right_side, start, inverse, *parts)
+    parts = second_exchange(place, windows, own, far)
     adjoint, residual = pl.pallas_call(
         last_kernel,
         out_shape=[out, out],

time: 50.7 us -> 50.6 us (level)
  the two profiles are of different devices: /device:TPU:249 before, /device:TPU:262 now
where the time goes in v8:
time: 50.6 us; the launch traced here: 50.3 us
  waiting for transfers between devices  23.2 us (46%)
  starting transfers between devices  18.5 us (37%)
  Pallas kernels  7.61 us (15%)
  between operations  0.79 us (2%)
    ppermute x1, waiting for transfers between devices, second_exchange(): near = lax.ppermute(near + mate[half:], 'elem', across)  11.3 us
    ppermute x1, waiting for transfers between devices, first_exchange(): near = lax.ppermute(near + mate[half:], 'elem', across)  10.3 us
    ppermute x1, starting transfers between devices, first_exchange(): near = lax.ppermute(near + mate[half:], 'elem', across)  6.33 us
    pallas_call x1, Pallas kernels, body(): pl.pallas_call(first_kernel, out_shape=applied(width, count) + [double, s...  3.62 us
    ppermute x1, starting transfers between devices, first_exchange(): far = lax.ppermute(far, 'elem', outward)  3.56 us
    ppermute x1, starting transfers between devices, second_exchange(): near = lax.ppermute(near + mate[half:], 'elem', across)  2.86 us
    pallas_call x1, Pallas kernels, body(): pl.pallas_call(second_kernel, out_shape=applied(width, count) + [out], in...  2.34 us
    ppermute x1, starting transfers between devices, first_exchange(): mate = lax.ppermute(mate, 'elem', swapped)  1.92 us
  transfers between devices with their start and end apart: 6, of which 3 were waited for; matrix products, arithmetic and copies ran while one was open for 0% of the time, Pallas kernels for 1%

profile of v8, /device:TPU:262, one launch (start us, length us, event | category | flops | bytes accessed | tf_op | source)
XLA Modules:
  0.0 50.3 jit_solution(16062555474184363720)
XLA Ops:
  0.6 3.6 %shard_map.68 = (f32[320,16,128]{2,1,0:T(8,128)S(1)}, f32[320,16,128]{2,1,0:T(8,128)S(1)}, f32[32,16,128]{2,1,0:T(8,128)S(1)}, f32[32,16,128]{2,1,0:T(8,128)S(1)...) custom-call(s32[1]{0:T(128)} %bitcast.place_ref, s32[6,64]{1,0:T(8,128)} %cols_hbm.3, ...), custom_call_target="tpu_custom_call" | custom-call | tf_op jit(solution)/shard_map/pallas_call | solution.py:265
  4.3 1.9 %collective-permute-start.1 = (f32[64,16,128]{2,1,0:T(8,128)S(1)}, f32[64,16,128]{2,1,0:T(8,128)S(1)}, u32[]{:S(2)}, u32[]{:S(2)}) collective-permute-start(f32[64,16,128]{2,1,0:T(8,128)S(1)} %get-tuple-element.21), channel_id=1, source_target_pairs={{0,8},{8,0},{16,24},{24,16},{32,40},{40,32},{48,56},{56,48},{64,72... | collective-permute-start | bytes 1572872 | tf_op jit(solution)/shard_map/ppermute | solution.py:241
  6.2 3.6 %collective-permute-start = (f32[32,16,128]{2,1,0:T(8,128)S(1)}, f32[32,16,128]{2,1,0:T(8,128)S(1)}, u32[]{:S(2)}, u32[]{:S(2)}) collective-permute-start(f32[32,16,128]{2,1,0:T(8,128)S(1)} %get-tuple-element.20), channel_id=1, source_target_pairs={{8,24},{24,40},{40,56},{56,72},{72,88},{88,104},{104,120},{120,136... | collective-permute-start | bytes 786440 | tf_op jit(solution)/shard_map/ppermute | solution.py:240
  9.8 0.0 collective-permute-done.1
  9.8 0.1 slice_add_fusion.1
  9.8 6.3 %collective-permute-start.2 = (f32[32,16,128]{2,1,0:T(8,128)S(1)}, f32[32,16,128]{2,1,0:T(8,128)S(1)}, u32[]{:S(2)}, u32[]{:S(2)}) collective-permute-start(f32[32,16,128]{2,1,0:T(8,128)S(1)} %get-tuple-element.32), channel_id=1, source_target_pairs={{8,16},{24,32},{40,48},{56,64},{72,80},{88,96},{104,112},{120,128}... | collective-permute-start | bytes 786440 | tf_op jit(solution)/shard_map/ppermute | solution.py:242
  16.2 0.0 collective-permute-done.refs_3_
  16.2 0.0 copy-start
  16.2 0.0 copy-start.1
  16.2 0.0 copy-start.2
  16.2 0.1 shard_map.69.here_in
  16.4 10.3 %collective-permute-done.2.near_in = f32[32,16,128]{2,1,0:T(8,128)S(1)} collective-permute-done((f32[32,16,128]{2,1,0:T(8,128)S(1)}, f32[32,16,128]{2,1,0:T(8,128)S(1)}, u32[]{:S(2)}, u32[]{:S(2)}) %collective-permute-start.2) | collective-permute-done | bytes 262176 | tf_op jit(solution)/shard_map/ppermute | solution.py:242
  26.6 0.0 copy-done
  26.7 2.3 %shard_map.70 = (f32[320,16,128]{2,1,0:T(8,128)S(1)}, f32[320,16,128]{2,1,0:T(8,128)S(1)}, f32[32,16,128]{2,1,0:T(8,128)S(1)}, f32[32,16,128]{2,1,0:T(8,128)S(1)}, f32[16,4096]{1,0:T(8,128)S(1)}) custom-call(s32[1]{0:T(128)} %bitcast.place_ref, s32[6,64]{1,0:T(8,128)} %cols_hbm.3, bf16[448,4096]{1,0:T(8,128)(2,1)S(1)} %get-tuple-element.16.panel_ref, ...), custom_call_target="tpu_custom_call" | custom-call | tf_op jit(solution)/shard_map/pallas_call | solution.py:274
  29.0 1.9 %collective-permute-start.4 = (f32[32,16,128]{2,1,0:T(8,128)S(1)}, f32[32,16,128]{2,1,0:T(8,128)S(1)}, u32[]{:S(2)}, u32[]{:S(2)}) collective-permute-start(f32[32,16,128]{2,1,0:T(8,128)S(1)} %get-tuple-element.28), channel_id=1, source_target_pairs={{8,24},{24,40},{40,56},{56,72},{72,88},{88,104},{104,120},{120,136... | collective-permute-start | bytes 786440 | tf_op jit(solution)/shard_map/ppermute | solution.py:250
  30.9 0.2 shard_map.72
  31.1 1.9 %collective-permute-start.3 = (f32[64,16,128]{2,1,0:T(8,128)S(1)}, f32[64,16,128]{2,1,0:T(8,128)S(1)}, u32[]{:S(2)}, u32[]{:S(2)}) collective-permute-start(f32[64,16,128]{2,1,0:T(8,128)S(1)} %shard_map.72), channel_id=1, source_target_pairs={{0,8},{8,0},{16,24},{24,16},{32,40},{40,32},{48,56},{56,48},{64,72... | collective-permute-start | bytes 1572872 | tf_op jit(solution)/shard_map/ppermute | solution.py:251
  33.1 0.2 shard_map.71
  33.3 1.7 %collective-permute-done.3 = f32[64,16,128]{2,1,0:T(8,128)S(1)} collective-permute-done((f32[64,16,128]{2,1,0:T(8,128)S(1)}, f32[64,16,128]{2,1,0:T(8,128)S(1)}, u32[]{:S(2)}, u32[]{:S(2)}) %collective-permute-start.3) | collective-permute-done | bytes 524320 | tf_op jit(solution)/shard_map/ppermute | solution.py:251
  35.0 0.1 slice_add_fusion
  35.0 2.9 %collective-permute-start.5 = (f32[32,16,128]{2,1,0:T(8,128)S(1)}, f32[32,16,128]{2,1,0:T(8,128)S(1)}, u32[]{:S(2)}, u32[]{:S(2)}) collective-permute-start(f32[32,16,128]{2,1,0:T(8,128)S(1)} %get-tuple-element.30), channel_id=1, source_target_pairs={{8,16},{24,32},{40,48},{56,64},{72,80},{88,96},{104,112},{120,128}... | collective-permute-start | bytes 786440 | tf_op jit(solution)/shard_map/ppermute | solution.py:253
  37.9 0.0 collective-permute-done.4.far_in
  37.9 11.3 %collective-permute-done.5.near_in = f32[32,16,128]{2,1,0:T(8,128)S(1)} collective-permute-done((f32[32,16,128]{2,1,0:T(8,128)S(1)}, f32[32,16,128]{2,1,0:T(8,128)S(1)}, u32[]{:S(2)}, u32[]{:S(2)}) %collective-permute-start.5) | collective-permute-done | bytes 262176 | tf_op jit(solution)/shard_map/ppermute | solution.py:253
  49.2 1.1 %shard_map.73 = (f32[16,4096]{1,0:T(8,128)}, f32[16,4096]{1,0:T(8,128)}) custom-call(f32[16,4096]{1,0:T(8,128)S(1)} %copy-done.2, f32[16,4096]{1,0:T(8,128)S(1)} %get-tuple-element.23.first_ref, bf16[64,4096]{1,0:T(8,128)(2,1)S(1)} %copy-done, f32[32,16,128]{2,1,0:T(8,128)S(1)} %get-tuple-element.27.here_in, f32[32,16,128]{2,1,0:T(8,128)S(1)} %get-tuple-element.31.mate_in, ...), custom_call_target="tpu_custom_call" | custom-call | tf_op jit(solution)/shard_map/pallas_call | solution.py:283
  (2 shorter events, 0.0 us)
Async XLA Ops:
  4.3 5.5 %collective-permute-start.1 = (f32[64,16,128]{2,1,0:T(8,128)S(1)}, f32[64,16,128]{2,1,0:T(8,128)S(1)}, u32[]{:S(2)}, u32[]{:S(2)}) collective-permute-start(f32[64,16,128]{2,1,0:T(8,128)S(1)} %get-tuple-element.21), channel_id=1, source_target_pairs={{0,8},{8,0},{16,24},{24,16},{32,40},{40,32},{48,56},{56,48},{64,72... | collective-permute-start | bytes 1572872 | tf_op jit(solution)/shard_map/ppermute | solution.py:241
  6.2 10.0 %collective-permute-start = (f32[32,16,128]{2,1,0:T(8,128)S(1)}, f32[32,16,128]{2,1,0:T(8,128)S(1)}, u32[]{:S(2)}, u32[]{:S(2)}) collective-permute-start(f32[32,16,128]{2,1,0:T(8,128)S(1)} %get-tuple-element.20), channel_id=1, source_target_pairs={{8,24},{24,40},{40,56},{56,72},{72,88},{88,104},{104,120},{120,136... | collective-permute-start | bytes 786440 | tf_op jit(solution)/shard_map/ppermute | solution.py:240
  9.8 16.8 %collective-permute-start.2 = (f32[32,16,128]{2,1,0:T(8,128)S(1)}, f32[32,16,128]{2,1,0:T(8,128)S(1)}, u32[]{:S(2)}, u32[]{:S(2)}) collective-permute-start(f32[32,16,128]{2,1,0:T(8,128)S(1)} %get-tuple-element.32), channel_id=1, source_target_pairs={{8,16},{24,32},{40,48},{56,64},{72,80},{88,96},{104,112},{120,128}... | collective-permute-start | bytes 786440 | tf_op jit(solution)/shard_map/ppermute | solution.py:242
  16.2 10.5 %copy-start = (bf16[64,4096]{1,0:T(8,128)(2,1)S(1)}, bf16[64,4096]{1,0:T(8,128)(2,1)}, u32[]{:S(2)}) copy-start(bf16[64,4096]{1,0:T(8,128)(2,1)} %inv_ref.3) | copy-start | bytes 1572868
  16.2 10.5 %copy-start.1 = (f32[16,4096]{1,0:T(8,128)S(1)}, f32[16,4096]{1,0:T(8,128)}, u32[]{:S(2)}) copy-start(f32[16,4096]{1,0:T(8,128)} %start_ref.1) | copy-start | bytes 786436
  16.2 10.5 %copy-start.2 = (f32[16,4096]{1,0:T(8,128)S(1)}, f32[16,4096]{1,0:T(8,128)}, u32[]{:S(2)}) copy-start(f32[16,4096]{1,0:T(8,128)} %right_ref.3) | copy-start | bytes 786436
  29.0 8.9 %collective-permute-start.4 = (f32[32,16,128]{2,1,0:T(8,128)S(1)}, f32[32,16,128]{2,1,0:T(8,128)S(1)}, u32[]{:S(2)}, u32[]{:S(2)}) collective-permute-start(f32[32,16,128]{2,1,0:T(8,128)S(1)} %get-tuple-element.28), channel_id=1, source_target_pairs={{8,24},{24,40},{40,56},{56,72},{72,88},{88,104},{104,120},{120,136... | collective-permute-start | bytes 786440 | tf_op jit(solution)/shard_map/ppermute | solution.py:250
  31.1 3.8 %collective-permute-start.3 = (f32[64,16,128]{2,1,0:T(8,128)S(1)}, f32[64,16,128]{2,1,0:T(8,128)S(1)}, u32[]{:S(2)}, u32[]{:S(2)}) collective-permute-start(f32[64,16,128]{2,1,0:T(8,128)S(1)} %shard_map.72), channel_id=1, source_target_pairs={{0,8},{8,0},{16,24},{24,16},{32,40},{40,32},{48,56},{56,48},{64,72... | collective-permute-start | bytes 1572872 | tf_op jit(solution)/shard_map/ppermute | solution.py:251
  35.0 14.2 %collective-permute-start.5 = (f32[32,16,128]{2,1,0:T(8,128)S(1)}, f32[32,16,128]{2,1,0:T(8,128)S(1)}, u32[]{:S(2)}, u32[]{:S(2)}) collective-permute-start(f32[32,16,128]{2,1,0:T(8,128)S(1)} %get-tuple-element.30), channel_id=1, source_target_pairs={{8,16},{24,32},{40,48},{56,64},{72,80},{88,96},{104,112},{120,128}... | collective-permute-start | bytes 786440 | tf_op jit(solution)/shard_map/ppermute | solution.py:253

commit v9 on v6

--- a/solution.py
+++ b/solution.py
@@ -26,7 +26,7 @@
     return against(jnp.concatenate([masked_lanes(vb, e) for e in range(4)], 0), panel)
 
 
-def scatter(vb_ref, panel_of, cols_ref, device, windows, own_ref, stage_ref):
+def scatter(vb_ref, panel_of, cols_ref, device, windows, own_ref, stage_ref, uncleared=()):
     width = vb_ref.shape[0]
     count = cols_ref.shape[1]
     low = lax.broadcasted_iota(jnp.int32, (width, 2 * DOF), 1) < DOF
@@ -57,6 +57,8 @@
 
     for quad in range(count // 4):
         multiply(quad)
+        if quad == 0:
+            clear(uncleared)
         add(quad)
 
 
@@ -125,11 +127,11 @@
     small.start()
     for cut in CUTS[1:-1]:
         copies[cut].start()
-    clear(windows)
+    clear(windows[1:])
     begin.wait()
     vb_ref[...] = start_ref[...].astype(jnp.bfloat16)
     small.wait()
-    scatter(vb_ref, panels(copies, panel_ref), cols_ref, device, windows, own_ref, stage_ref)
+    scatter(vb_ref, panels(copies, panel_ref), cols_ref, device, windows, own_ref, stage_ref, windows[:1])
     hand_out(device, windows, 0, far_ref)
 
 

time: 50.5 us -> 50.5 us (level)
  no operation moved by 1% of the time
where the time goes in v9:
time: 50.5 us; the launch traced here: 50.2 us
  waiting for transfers between devices  23 us (46%)
  starting transfers between devices  18.7 us (37%)
  Pallas kernels  7.55 us (15%)
  between operations  0.78 us (2%)
    ppermute x2, waiting for transfers between devices, exchange(): near = lax.ppermute(near + mate[half:], 'elem', across)  21.4 us
    ppermute x2, starting transfers between devices, exchange(): near = lax.ppermute(near + mate[half:], 'elem', across)  9.37 us
    ppermute x2, starting transfers between devices, exchange(): far = lax.ppermute(far, 'elem', outward)  5.49 us
    ppermute x2, starting transfers between devices, exchange(): mate = lax.ppermute(mate, 'elem', [(i, i ^ 1) for i in range(size)])  3.84 us
    pallas_call x1, Pallas kernels, body(): pl.pallas_call(first_kernel, out_shape=applied(width, count) + [pltpu.VME...  3.38 us
    pallas_call x1, Pallas kernels, body(): pl.pallas_call(second_kernel, out_shape=applied(width, count) + [out], in...  2.21 us
    ppermute x2, waiting for transfers between devices, exchange(): mate = lax.ppermute(mate, 'elem', [(i, i ^ 1) for i in range(size)])  1.66 us
    pallas_call x1, Pallas kernels, body(): pl.pallas_call(last_kernel, out_shape=[out, out], in_specs=[VMEM] * 7, ou...  1.09 us
  transfers between devices with their start and end apart: 6, of which 3 were waited for; matrix products, arithmetic and copies ran while one was open for 0% of the time, Pallas kernels for 1%

profile of v9, /device:TPU:258, one launch (start us, length us, event | category | flops | bytes accessed | tf_op | source)
XLA Modules:
  0.0 50.2 jit_solution(5568729428156504845)
XLA Ops:
  0.6 3.4 %shard_map.68 = (f32[320,16,128]{2,1,0:T(8,128)S(1)}, f32[320,16,128]{2,1,0:T(8,128)S(1)}, f32[32,16,128]{2,1,0:T(8,128)S(1)}, f32[32,16,128]{2,1,0:T(8,128)S(1)}, bf16[448,4096]{1,0:T(8,128)(2,1)S(1)}) custom-call(s32[1]{0:T(128)} %bitcast.place_ref, s32[6,64]{1,0:T(8,128)} %cols_hbm.3, bf16[448,4096]{1,0:T(8,128)(2,1)} %bitcast.2, f32[16,4096]{1,0:T(8,128)} %start_ref.1), custom_call_target="tpu_custom_call" | custom-call | tf_op jit(solution)/shard_map/pallas_call | solution.py:241
  4.0 0.2 shard_map.70
  4.2 1.9 %collective-permute-start = (f32[64,16,128]{2,1,0:T(8,128)S(1)}, f32[64,16,128]{2,1,0:T(8,128)S(1)}, u32[]{:S(2)}, u32[]{:S(2)}) collective-permute-start(f32[64,16,128]{2,1,0:T(8,128)S(1)} %shard_map.70), channel_id=1, source_target_pairs={{0,8},{8,0},{16,24},{24,16},{32,40},{40,32},{48,56},{56,48},{64,72... | collective-permute-start | bytes 1572872 | tf_op jit(solution)/shard_map/ppermute | solution.py:222
  6.2 3.6 %collective-permute-start.1 = (f32[32,16,128]{2,1,0:T(8,128)S(1)}, f32[32,16,128]{2,1,0:T(8,128)S(1)}, u32[]{:S(2)}, u32[]{:S(2)}) collective-permute-start(f32[32,16,128]{2,1,0:T(8,128)S(1)} %get-tuple-element.21), channel_id=1, source_target_pairs={{8,24},{24,40},{40,56},{56,72},{72,88},{88,104},{104,120},{120,136... | collective-permute-start | bytes 786440 | tf_op jit(solution)/shard_map/ppermute | solution.py:213
  9.7 0.0 copy-start
  9.8 0.0 copy-start.1
  9.8 0.0 copy-start.2
  9.8 0.2 shard_map.69
  10.0 0.0 collective-permute-done
  10.0 0.1 slice_add_fusion.1
  10.1 6.3 %collective-permute-start.2 = (f32[32,16,128]{2,1,0:T(8,128)S(1)}, f32[32,16,128]{2,1,0:T(8,128)S(1)}, u32[]{:S(2)}, u32[]{:S(2)}) collective-permute-start(f32[32,16,128]{2,1,0:T(8,128)S(1)} %get-tuple-element.32), channel_id=1, source_target_pairs={{8,16},{24,32},{40,48},{56,64},{72,80},{88,96},{104,112},{120,128}... | collective-permute-start | bytes 786440 | tf_op jit(solution)/shard_map/ppermute | solution.py:231
  16.4 0.0 collective-permute-done.1.far_in
  16.4 10.2 %collective-permute-done.2.near_in = f32[32,16,128]{2,1,0:T(8,128)S(1)} collective-permute-done((f32[32,16,128]{2,1,0:T(8,128)S(1)}, f32[32,16,128]{2,1,0:T(8,128)S(1)}, u32[]{:S(2)}, u32[]{:S(2)}) %collective-permute-start.2) | collective-permute-done | bytes 262176 | tf_op jit(solution)/shard_map/ppermute | solution.py:231
  26.6 2.2 %shard_map.71 = (f32[320,16,128]{2,1,0:T(8,128)S(1)}, f32[320,16,128]{2,1,0:T(8,128)S(1)}, f32[32,16,128]{2,1,0:T(8,128)S(1)}, f32[32,16,128]{2,1,0:T(8,128)S(1)}, f32[16,4096]{1,0:T(8,128)S(1)}) custom-call(s32[1]{0:T(128)} %bitcast.place_ref, s32[6,64]{1,0:T(8,128)} %cols_hbm.3, bf16[448,4096]{1,0:T(8,128)(2,1)S(1)} %get-tuple-element.16.panel_ref, ...), custom_call_target="tpu_custom_call" | custom-call | tf_op jit(solution)/shard_map/pallas_call | solution.py:250
  28.9 1.9 %collective-permute-start.4 = (f32[32,16,128]{2,1,0:T(8,128)S(1)}, f32[32,16,128]{2,1,0:T(8,128)S(1)}, u32[]{:S(2)}, u32[]{:S(2)}) collective-permute-start(f32[32,16,128]{2,1,0:T(8,128)S(1)} %get-tuple-element.28), channel_id=1, source_target_pairs={{8,24},{24,40},{40,56},{56,72},{72,88},{88,104},{104,120},{120,136... | collective-permute-start | bytes 786440 | tf_op jit(solution)/shard_map/ppermute | solution.py:213
  30.8 0.2 shard_map.73
  31.0 1.9 %collective-permute-start.3 = (f32[64,16,128]{2,1,0:T(8,128)S(1)}, f32[64,16,128]{2,1,0:T(8,128)S(1)}, u32[]{:S(2)}, u32[]{:S(2)}) collective-permute-start(f32[64,16,128]{2,1,0:T(8,128)S(1)} %shard_map.73), channel_id=1, source_target_pairs={{0,8},{8,0},{16,24},{24,16},{32,40},{40,32},{48,56},{56,48},{64,72... | collective-permute-start | bytes 1572872 | tf_op jit(solution)/shard_map/ppermute | solution.py:222
  32.9 0.2 shard_map.72
  33.2 1.7 %collective-permute-done.3 = f32[64,16,128]{2,1,0:T(8,128)S(1)} collective-permute-done((f32[64,16,128]{2,1,0:T(8,128)S(1)}, f32[64,16,128]{2,1,0:T(8,128)S(1)}, u32[]{:S(2)}, u32[]{:S(2)}) %collective-permute-start.3) | collective-permute-done | bytes 524320 | tf_op jit(solution)/shard_map/ppermute | solution.py:222
  34.8 0.1 slice_add_fusion
  34.9 3.1 %collective-permute-start.5 = (f32[32,16,128]{2,1,0:T(8,128)S(1)}, f32[32,16,128]{2,1,0:T(8,128)S(1)}, u32[]{:S(2)}, u32[]{:S(2)}) collective-permute-start(f32[32,16,128]{2,1,0:T(8,128)S(1)} %get-tuple-element.30), channel_id=1, source_target_pairs={{8,16},{24,32},{40,48},{56,64},{72,80},{88,96},{104,112},{120,128}... | collective-permute-start | bytes 786440 | tf_op jit(solution)/shard_map/ppermute | solution.py:231
  37.9 0.0 collective-permute-done.4.far_in
  37.9 11.2 %collective-permute-done.5.near_in = f32[32,16,128]{2,1,0:T(8,128)S(1)} collective-permute-done((f32[32,16,128]{2,1,0:T(8,128)S(1)}, f32[32,16,128]{2,1,0:T(8,128)S(1)}, u32[]{:S(2)}, u32[]{:S(2)}) %collective-permute-start.5) | collective-permute-done | bytes 262176 | tf_op jit(solution)/shard_map/ppermute | solution.py:231
  49.1 1.1 %shard_map.74 = (f32[16,4096]{1,0:T(8,128)}, f32[16,4096]{1,0:T(8,128)}) custom-call(f32[16,4096]{1,0:T(8,128)S(1)} %copy-done.2, f32[16,4096]{1,0:T(8,128)S(1)} %get-tuple-element.23.first_ref, bf16[64,4096]{1,0:T(8,128)(2,1)S(1)} %copy-done, f32[32,16,128]{2,1,0:T(8,128)S(1)} %get-tuple-element.27.here_in, f32[32,16,128]{2,1,0:T(8,128)S(1)} %get-tuple-element.31.mate_in, ...), custom_call_target="tpu_custom_call" | custom-call | tf_op jit(solution)/shard_map/pallas_call | solution.py:259
  (3 shorter events, 0.0 us)
Async XLA Ops:
  4.2 5.8 %collective-permute-start = (f32[64,16,128]{2,1,0:T(8,128)S(1)}, f32[64,16,128]{2,1,0:T(8,128)S(1)}, u32[]{:S(2)}, u32[]{:S(2)}) collective-permute-start(f32[64,16,128]{2,1,0:T(8,128)S(1)} %shard_map.70), channel_id=1, source_target_pairs={{0,8},{8,0},{16,24},{24,16},{32,40},{40,32},{48,56},{56,48},{64,72... | collective-permute-start | bytes 1572872 | tf_op jit(solution)/shard_map/ppermute | solution.py:222
  6.2 10.2 %collective-permute-start.1 = (f32[32,16,128]{2,1,0:T(8,128)S(1)}, f32[32,16,128]{2,1,0:T(8,128)S(1)}, u32[]{:S(2)}, u32[]{:S(2)}) collective-permute-start(f32[32,16,128]{2,1,0:T(8,128)S(1)} %get-tuple-element.21), channel_id=1, source_target_pairs={{8,24},{24,40},{40,56},{56,72},{72,88},{88,104},{104,120},{120,136... | collective-permute-start | bytes 786440 | tf_op jit(solution)/shard_map/ppermute | solution.py:213
  9.7 16.9 %copy-start = (bf16[64,4096]{1,0:T(8,128)(2,1)S(1)}, bf16[64,4096]{1,0:T(8,128)(2,1)}, u32[]{:S(2)}) copy-start(bf16[64,4096]{1,0:T(8,128)(2,1)} %inv_ref.3) | copy-start | bytes 1572868
  9.8 16.9 %copy-start.1 = (f32[16,4096]{1,0:T(8,128)S(1)}, f32[16,4096]{1,0:T(8,128)}, u32[]{:S(2)}) copy-start(f32[16,4096]{1,0:T(8,128)} %start_ref.1) | copy-start | bytes 786436
  9.8 16.9 %copy-start.2 = (f32[16,4096]{1,0:T(8,128)S(1)}, f32[16,4096]{1,0:T(8,128)}, u32[]{:S(2)}) copy-start(f32[16,4096]{1,0:T(8,128)} %right_ref.3) | copy-start | bytes 786436
  10.1 16.5 %collective-permute-start.2 = (f32[32,16,128]{2,1,0:T(8,128)S(1)}, f32[32,16,128]{2,1,0:T(8,128)S(1)}, u32[]{:S(2)}, u32[]{:S(2)}) collective-permute-start(f32[32,16,128]{2,1,0:T(8,128)S(1)} %get-tuple-element.32), channel_id=1, source_target_pairs={{8,16},{24,32},{40,48},{56,64},{72,80},{88,96},{104,112},{120,128}... | collective-permute-start | bytes 786440 | tf_op jit(solution)/shard_map/ppermute | solution.py:231
  28.9 9.1 %collective-permute-start.4 = (f32[32,16,128]{2,1,0:T(8,128)S(1)}, f32[32,16,128]{2,1,0:T(8,128)S(1)}, u32[]{:S(2)}, u32[]{:S(2)}) collective-permute-start(f32[32,16,128]{2,1,0:T(8,128)S(1)} %get-tuple-element.28), channel_id=1, source_target_pairs={{8,24},{24,40},{40,56},{56,72},{72,88},{88,104},{104,120},{120,136... | collective-permute-start | bytes 786440 | tf_op jit(solution)/shard_map/ppermute | solution.py:213
  31.0 3.8 %collective-permute-start.3 = (f32[64,16,128]{2,1,0:T(8,128)S(1)}, f32[64,16,128]{2,1,0:T(8,128)S(1)}, u32[]{:S(2)}, u32[]{:S(2)}) collective-permute-start(f32[64,16,128]{2,1,0:T(8,128)S(1)} %shard_map.73), channel_id=1, source_target_pairs={{0,8},{8,0},{16,24},{24,16},{32,40},{40,32},{48,56},{56,48},{64,72... | collective-permute-start | bytes 1572872 | tf_op jit(solution)/shard_map/ppermute | solution.py:222
  34.9 14.2 %collective-permute-start.5 = (f32[32,16,128]{2,1,0:T(8,128)S(1)}, f32[32,16,128]{2,1,0:T(8,128)S(1)}, u32[]{:S(2)}, u32[]{:S(2)}) collective-permute-start(f32[32,16,128]{2,1,0:T(8,128)S(1)} %get-tuple-element.30), channel_id=1, source_target_pairs={{8,16},{24,32},{40,48},{56,64},{72,80},{88,96},{104,112},{120,128}... | collective-permute-start | bytes 786440 | tf_op jit(solution)/shard_map/ppermute | solution.py:231
